TPU v7x, 128 devices: a whole 4x4x4 slice. The times are simulated.
128 devices in a mesh: blk: 8 (over y, x_hi), dp: 16 (over x_lo, z, core).
Axes of the slice: x: 4 (x_hi: 2, x_lo: 2; x = x_hi * 2 + x_lo), y: 4, z: 4, core: 2. Of those that a mesh axis runs over, the one named last changes fastest.
Arguments:
- proj: float32 [16384, 128], P(('blk', 'dp')), may hold values from -4 to 4
- partner: int32 [16384], replicated, may hold values from 0 to 16383, as said below
Outputs:
- loss: float32 [], replicated
- grad: float32 [16384, 128], P(('blk', 'dp'))
Inputs may be any that keep to these rules, and one draw needn't show every extreme that they name: partner is an involution without fixed points: partner[partner[i]] = i and partner[i] != i.
All inputs are finite; a program needn't handle non-finite values.
Results may differ from a plain program's by a relative error of at most 0.0042.
Values may be sent and summed in bfloat16 or wider, within the bound.
No kernel may reach another device: no remote copies, remote signals or barrier semaphores. Data moves between devices by JAX's collectives and lax.ppermute only.
A program may use at most 64 MiB of HBM per device.

v0:
```python
import math

import jax
import jax.numpy as jnp
from jax import lax
from jax.sharding import PartitionSpec as P

INV_TEMP = 10.0
EPS = 1e-06


def block_rows(count):
    return math.gcd(count, 512)


def tile_scores(rows_z, rows_p, rows_id, cols_z, cols_id, first, size):
    part_z = lax.dynamic_slice_in_dim(rows_z, first, size, 0)
    part_p = lax.dynamic_slice_in_dim(rows_p, first, size, 0)
    part_id = lax.dynamic_slice_in_dim(rows_id, first, size, 0)
    scores = (
        lax.dot_general(
            part_z, cols_z, (((1,), (1,)), ((), ())), preferred_element_type=jnp.float32
        )
        * INV_TEMP
    )
    expo = jnp.where(part_id[:, None] == cols_id[None, :], 0.0, jnp.exp(scores - INV_TEMP))
    marks = part_p[:, None] == cols_id[None, :]
    return (scores, expo, marks)


def tile_sums(rows_z, rows_p, rows_id, cols_z, cols_id):
    count = rows_z.shape[0]
    size = block_rows(count)

    def one_block(first):
        scores, expo, marks = tile_scores(rows_z, rows_p, rows_id, cols_z, cols_id, first, size)
        return (jnp.sum(expo, axis=1), jnp.sum(jnp.where(marks, scores, 0.0), axis=1))

    starts = jnp.arange(count // size) * size
    esum, pos = lax.map(one_block, starts)
    return (esum.reshape(count), pos.reshape(count))


def tile_grads(count, rows_z, rows_p, rows_id, rows_e, cols_z, cols_id, cols_e):
    size = block_rows(count)

    def one_block(offset):
        scores, expo, marks = tile_scores(rows_z, rows_p, rows_id, cols_z, cols_id, offset, size)
        own_e = lax.dynamic_slice_in_dim(rows_e, offset, size, 0)
        weight = (
            expo / own_e[:, None] + expo / cols_e[None, :] - 2.0 * marks.astype(jnp.float32)
        ).astype(jnp.bfloat16)
        return jnp.dot(weight, cols_z, preferred_element_type=jnp.float32)

    offsets = jnp.arange(count // size) * size
    blocks = lax.map(one_block, offsets)
    return blocks.reshape(count, cols_z.shape[1])


def body(proj, partner):
    views_here = proj.shape[0]
    n_dp = lax.axis_size("dp")
    n_blk = lax.axis_size("blk")
    blk_index = lax.axis_index("blk")
    dp_index = lax.axis_index("dp")
    radius = jnp.sqrt(jnp.sum(proj * proj, axis=1, keepdims=True) + EPS)
    unit = proj / radius
    unit_b = unit.astype(jnp.bfloat16)
    group_ids = blk_index * n_dp * views_here + jnp.arange(n_dp * views_here)
    shard_pos = jnp.arange(n_blk * views_here)
    shard_ids = (shard_pos // views_here * n_dp + dp_index) * views_here + shard_pos % views_here
    group_mates = jnp.take(partner, group_ids, axis=0)
    rows_z = lax.all_gather(unit_b, "dp", axis=0, tiled=True)
    cols_z = lax.all_gather(unit_b, "blk", axis=0, tiled=True)
    esum_part, pos_part = tile_sums(rows_z, group_mates, group_ids, cols_z, shard_ids)
    rows_e, rows_pos = lax.psum((esum_part, pos_part), "dp")
    own_e = lax.dynamic_slice_in_dim(rows_e, dp_index * views_here, views_here, 0)
    own_pos = lax.dynamic_slice_in_dim(rows_pos, dp_index * views_here, views_here, 0)
    cols_e = lax.all_gather(own_e, "blk", axis=0, tiled=True)
    accum = lax.psum_scatter(
        tile_grads(
            lax.axis_size("dp") * views_here,
            rows_z,
            group_mates,
            group_ids,
            rows_e,
            cols_z,
            shard_ids,
            cols_e,
        ),
        "dp",
        scatter_dimension=0,
        tiled=True,
    )
    local_loss = jnp.sum(INV_TEMP + jnp.log(own_e) - own_pos)
    loss = lax.psum(local_loss, ("blk", "dp")) / (views_here * n_dp * n_blk)
    dunit = accum * INV_TEMP
    grad = (dunit - unit * jnp.sum(unit * dunit, axis=1, keepdims=True)) / radius
    return (loss, grad)


def solution(mesh):
    return jax.shard_map(
        body,
        mesh=mesh,
        in_specs=(P(("blk", "dp"), None), P()),
        out_specs=(P(), P(("blk", "dp"), None)),
        check_vma=False,
    )
```

profile of v0, /device:TPU:0, one launch (start us, length us, event | category | flops | bytes accessed | tf_op | source)
XLA Modules:
  0.0 260.8 jit_solution(17402881528252058010)
XLA Ops:
  7.2 0.0 copy-start
  7.2 0.0 reduce-scatter.2.cloned.1.call-start
  7.2 0.9 multiply_reduce_fusion.1
  8.2 0.9 fusion.49
  9.1 22.4 %all_gather.9 = bf16[2048,128]{1,0:T(8,128)(2,1)S(1)} all-gather(bf16[128,128]{1,0:T(8,128)(2,1)S(1)} %fusion.49), channel_id=1, replica_groups=mesh['blk'=8,'dp'=16] {'dp'}, dimensions={0}, use_global_device_ids=true | all-gather | bytes 557056 | tf_op jit(solution)/shard_map/all_gather | solution.py:73
  31.5 35.0 %all_gather.10 = bf16[1024,128]{1,0:T(8,128)(2,1)S(1)} all-gather(bf16[128,128]{1,0:T(8,128)(2,1)S(1)} %fusion.49), channel_id=1, replica_groups=mesh['blk'=8,'dp'=16] {'blk'}, dimensions={0}, use_global_device_ids=true | all-gather | bytes 294912 | tf_op jit(solution)/shard_map/all_gather | solution.py:74
  66.6 0.0 copy-done
  66.6 11.8 %gather_fusion = s32[2048]{0:T(1024)S(1)} fusion(s32[16384]{0:T(1024)S(1)} %copy-done, s32[2048]{0:T(1024)S(1)} %broadcast_clamp_fusion), kind=kCustom, calls=%fused_computation | custom fusion | bytes 24576 | tf_op jit(solution)/shard_map/jit(_take)/gather | solution.py:72
  78.4 13.9 %while.28 = (s32[]{:T(128)}, f32[4,512]{1,0:T(4,128)S(1)}, f32[4,512]{1,0:T(4,128)S(1)}, s32[4]{0:T(128)S(1)}, s32[2048]{0:T(1024)S(1)}, /*index=5*/bf16[2048,12...) while((s32[]{:T(128)}, f32[4,512]{1,0:T(4,128)S(1)}, ...), condition=%wide.region_4.5_spmd.clone, body=%wide.region_1.4_spmd.clone.sunk | while | flops 138427392 | bytes 426171 | solution.py:40
  78.4 0.6 dynamic_slice.92
  80.7 0.1 dynamic_slice.93
  80.7 0.1 dynamic_slice.94
  80.8 0.9 select_reduce_fusion.3
  81.8 0.1 dynamic_update_slice.27
  81.9 0.6 dynamic_slice.92
  84.1 0.1 dynamic_slice.93
  84.2 0.1 dynamic_slice.94
  84.3 0.9 select_reduce_fusion.3
  85.3 0.1 dynamic_update_slice.27
  85.3 0.6 dynamic_slice.92
  87.6 0.1 dynamic_slice.93
  87.7 0.1 dynamic_slice.94
  87.8 0.9 select_reduce_fusion.3
  88.8 0.1 dynamic_update_slice.27
  88.8 0.6 dynamic_slice.92
  91.1 0.1 dynamic_slice.93
  91.2 0.1 dynamic_slice.94
  91.3 0.9 select_reduce_fusion.3
  92.2 0.1 dynamic_update_slice.27
  92.3 52.9 %all-reduce = (f32[2048]{0:T(1024)S(1)}, f32[2048]{0:T(1024)S(1)}) all-reduce(f32[2048]{0:T(1024)S(1)} %bitcast.40, f32[2048]{0:T(1024)S(1)} %bitcast.39), channel_id=1, replica_groups=mesh['blk'=8,'dp'=16] {'dp'}, use_global_device_ids=true, to_apply=%region_6.7 | all-reduce | flops 4096 | bytes 32768 | tf_op jit(solution)/shard_map/psum | solution.py:76
  145.2 0.7 dynamic-slice_bitcast_fusion
  145.9 23.1 %all-gather = f32[8,1,128]{2,1,0:T(1,128)S(1)} all-gather(f32[1,1,128]{2,1,0:T(1,128)S(1)} %get-tuple-element.330), channel_id=1, replica_groups=mesh['blk'=8,'dp'=16] {'blk'}, dimensions={0}, use_global_device_ids=true | all-gather | bytes 4608 | tf_op jit(solution)/shard_map/all_gather | solution.py:79
  169.1 17.3 %while.29 = (s32[]{:T(128)}, f32[4,512,128]{2,1,0:T(8,128)}, s32[4]{0:T(128)S(1)}, s32[2048]{0:T(1024)S(1)}, bf16[2048,128]{1,0:T(8,128)(2,1)S(1)}, /*index=5*/b...) while((s32[]{:T(128)}, f32[4,512,128]{2,1,0:T(8,128)}, ...), condition=%wide.region_10.11_spmd.clone, body=%wide.region_9.10_spmd.clone.sunk | while | flops 274219008 | bytes 948927 | solution.py:56
  169.1 0.6 dynamic_slice.96
  171.3 0.1 dynamic_slice.97
  171.4 0.1 dynamic_slice.98
  171.5 0.1 dynamic_slice.99
  171.6 1.8 fusion.66
  173.4 0.6 dynamic_slice.96
  175.6 0.1 dynamic_slice.97
  175.7 0.1 dynamic_slice.98
  175.8 0.1 dynamic_slice.99
  175.9 1.8 fusion.66
  177.7 0.6 dynamic_slice.96
  179.9 0.1 dynamic_slice.97
  180.0 0.1 dynamic_slice.98
  180.1 0.1 dynamic_slice.99
  180.2 1.8 fusion.66
  182.0 0.6 dynamic_slice.96
  184.3 0.1 dynamic_slice.97
  184.3 0.1 dynamic_slice.98
  184.4 0.1 dynamic_slice.99
  184.5 1.8 fusion.66
  186.3 0.0 copy-start.1
  186.3 0.0 reduce-scatter.2.cloned.1.call-update
  186.3 63.2 %psum.23 = f32[]{:T(128)} all-reduce(f32[]{:T(128)} %get-tuple-element.331), channel_id=1, replica_groups=mesh['blk'=8,'dp'=16] {'blk','dp'}, use_global_device_ids=true, to_apply=%region_8.9 | all-reduce | flops 1 | bytes 8 | tf_op jit(solution)/shard_map/psum | solution.py:96
  250.2 0.0 reduce-scatter.2.cloned.1.call-done
  250.2 0.0 copy-done.1
  250.3 1.0 multiply_reduce_fusion
  251.3 1.6 subtract_divide_fusion
  (22 shorter events, 0.3 us)
Async XLA Ops:
  7.2 59.4 %copy-start = (s32[16384]{0:T(1024)S(1)}, s32[16384]{0:T(1024)}, u32[]{:S(2)}) copy-start(s32[16384]{0:T(1024)} %param.7) | copy-start | bytes 196612
  7.2 243.1 %reduce-scatter.2.cloned.1.call-start = ((), (), s32[]{:S(2)}) async-start(), calls=%async_computation.1 | async-start | bytes 1114112 | tf_op jit(solution)/shard_map/reduce_scatter | solution.py:80
  186.3 63.9 %copy-start.1 = (f32[128,128]{1,0:T(8,128)S(1)}, f32[128,128]{1,0:T(8,128)}, u32[]{:S(2)}) copy-start(f32[128,128]{1,0:T(8,128)} %param.6) | copy-start | bytes 196612
Sparse Core Ops, SparseCore 0:
  186.5 55.0 reduce-scatter.1
where the time goes:
time: 262 us; the launch traced here: 261 us
  blocking collectives  197 us (75%)
  local copies, waits for them, and re-layouts  18.4 us (7%)
  between operations  15.9 us (6%)
  loops' own time  13.6 us (5%)
  matrix products  11 us (4%)
  other arithmetic  5.25 us (2%)
    psum x1, blocking collectives, body(): loss = lax.psum(local_loss, ('blk', 'dp')) / (views_here * n_dp * n_blk)  63.2 us
    psum x1, blocking collectives, body(): rows_e, rows_pos = lax.psum((esum_part, pos_part), 'dp')  52.9 us
    all_gather x1, blocking collectives, body(): cols_z = lax.all_gather(unit_b, 'blk', axis=0, tiled=True)  35 us
    all_gather x1, blocking collectives, body(): cols_e = lax.all_gather(own_e, 'blk', axis=0, tiled=True)  23.1 us
    all_gather x1, blocking collectives, body(): rows_z = lax.all_gather(unit_b, 'dp', axis=0, tiled=True)  22.4 us
    gather x1, local copies, waits for them, and re-layouts, body(): group_mates = jnp.take(partner, group_ids, axis=0)  11.8 us
    dot_general x4, matrix products, one_block(): return jnp.dot(weight, cols_z, preferred_element_type=jnp.float32)  7.25 us
    another operation x1, loops' own time, tile_sums(): esum, pos = lax.map(one_block, starts)  6.82 us
  transfers between devices with their start and end apart: 1, of which 0 were waited for; matrix products, arithmetic and copies ran while one was open for 0% of the time, Pallas kernels for 0%

commit v1 on v0

v1 whole, which is shorter than its diff:
```python
import functools
import math

import jax
import jax.numpy as jnp
from jax import lax
from jax.experimental import pallas as pl
from jax.experimental.pallas import tpu as pltpu
from jax.sharding import Mesh, PartitionSpec as P

EPS = 1e-06
INV_TEMP = 10.0
SCALE = INV_TEMP * math.log2(math.e)

ROWS = 128
NXY = 16
NZ = 4
NCO = 2
NDEV = NXY * NZ * NCO
VIEWS = NDEV * ROWS
XY = ("y", "xh", "xl")
ALL = ("y", "xh", "xl", "z", "co")
CHUNK = 256
F32 = jnp.float32
BF16 = jnp.bfloat16
VMEM = pl.BlockSpec(memory_space=pltpu.VMEM)
SMEM = pl.BlockSpec(memory_space=pltpu.SMEM)


def call(body, outs, scratch=(), flops=0, nbytes=0, exps=0):
    def run(*args):
        return pl.pallas_call(
            body,
            out_shape=outs,
            in_specs=[SMEM if a.dtype == jnp.int32 and a.ndim == 1 else VMEM for a in args],
            out_specs=[VMEM] * len(outs),
            scratch_shapes=list(scratch),
            compiler_params=pltpu.CompilerParams(vmem_limit_bytes=24 * 2**20),
            cost_estimate=pl.CostEstimate(flops=flops, bytes_accessed=nbytes, transcendentals=exps),
        )(*args)

    return run


def sds(shape, dtype=F32):
    return jax.ShapeDtypeStruct(shape, dtype)


def dot_nt(a, b):
    return lax.dot_general(a, b, (((1,), (1,)), ((), ())), preferred_element_type=F32)


def dot_nn(a, b):
    return lax.dot_general(a, b, (((1,), (0,)), ((), ())), preferred_element_type=F32)


def down_rows(row):
    return jnp.transpose(jnp.broadcast_to(row, (ROWS, ROWS)))


def norm_kernel(x_ref, u_ref, copies_ref):
    x = x_ref[...]
    radius = jnp.sqrt(jnp.sum(x * x, axis=1, keepdims=True) + EPS)
    unit = (x / radius).astype(BF16)
    u_ref[...] = unit
    copies_ref[...] = jnp.broadcast_to(unit[None], (NXY, ROWS, ROWS))


def expo(s):
    return jnp.exp2(s * SCALE)


def clear_self(e, col0, own_col):
    col = lax.broadcasted_iota(jnp.int32, e.shape, 1) + (col0 - own_col)
    row = lax.broadcasted_iota(jnp.int32, e.shape, 0)
    return jnp.where(col == row, 0.0, e)


def sums_kernel(own_half, *refs):
    n_in = 7 if own_half else 10
    place_ref, u0, u1, u2, u3, c_ref, mate_ref = refs[:7]
    outs = refs[n_in:-3]
    e_ref, m_ref, sum_ref = refs[-3:]
    z, co, xy = place_ref[0], place_ref[1], place_ref[2]
    cols = c_ref.shape[0]
    half = co if own_half else 1 - co
    mates = mate_ref[...]
    here = (((mates >> 8) & 3) == z) & (((mates >> 7) & 1) == half)
    local = jnp.where(here, ((mates >> 10) << 7) | (mates & 127), -1)
    lane = lax.broadcasted_iota(jnp.int32, (ROWS, CHUNK), 1)
    for r, u_ref in enumerate((u0, u1, u2, u3)):
        rows = slice(r * ROWS, (r + 1) * ROWS)
        u = u_ref[...]
        mate = down_rows(local[r : r + 1])
        mate = jnp.concatenate([mate] * (CHUNK // ROWS), axis=1)
        total = jnp.zeros((ROWS, ROWS), F32)
        for c in range(0, cols, CHUNK):
            e = expo(dot_nt(u, c_ref[c : c + CHUNK]))
            if own_half and r == 0:
                e = clear_self(e, c, xy * ROWS)
            for k in range(0, CHUNK, ROWS):
                total = total + e[:, k : k + ROWS]
            e_ref[rows, c : c + CHUNK] = e.astype(BF16)
            m_ref[rows, c : c + CHUNK] = jnp.where(mate == lane + c, 1.0, 0.0).astype(BF16)
        sum_ref[r : r + 1, :] = jnp.sum(jnp.transpose(total), axis=0, keepdims=True)
    a = dot_nn(e_ref[...], c_ref[...])
    p = dot_nn(m_ref[...], c_ref[...])
    if own_half:
        outs[0][...] = sum_ref[...]
        outs[1][...] = a
        outs[2][...] = p
        return
    sum_in, a_in, p_in = refs[7:10]
    a = a + a_in[...]
    p = p + p_in[...]
    pos = jnp.zeros((ROWS, ROWS), F32)
    for r, u_ref in enumerate((u0, u1, u2, u3)):
        rows = slice(r * ROWS, (r + 1) * ROWS)
        outs[1 + r][0:ROWS] = a[rows]
        outs[1 + r][ROWS : 2 * ROWS] = p[rows]
        pos = pos + u_ref[...].astype(F32) * p[rows]
    sums = sum_ref[...] + sum_in[...]
    pos = INV_TEMP * jnp.sum(pos, axis=0, keepdims=True)
    for k in range(NZ):
        r = lax.rem(k - z + NZ, NZ)
        row = jnp.zeros((1, ROWS), F32)
        for q in range(NZ):
            row = jnp.where(r == q, sums[q : q + 1], row)
        piece = jnp.concatenate([row, pos], axis=1)
        for xy_to in range(NXY):
            for co_to in range(NCO):
                outs[0][xy_to * 8 + k * 2 + co_to] = piece


def grads_kernel(place_ref, u0, u1, u2, u3, own_ref, other_ref, got_ref, b0, b1, b2, b3, aux_ref, inv_ref, w_ref):
    co, xy = place_ref[1], place_ref[2]
    logs = jnp.zeros((1, ROWS), F32)
    for k in range(NXY):
        for c in range(NCO):
            total = got_ref[k * 8 + c, :, 0:ROWS]
            for z in range(1, NZ):
                total = total + got_ref[k * 8 + z * 2 + c, :, 0:ROWS]
            logs = logs + jnp.log(total)
            inv_ref[c, :, k * ROWS : (k + 1) * ROWS] = 1.0 / total
    pos = got_ref[0, :, ROWS:]
    for k in range(1, NDEV):
        pos = pos + got_ref[k, :, ROWS:]
    own_col = pl.multiple_of(xy * ROWS, ROWS)
    aux_ref[0:1] = inv_ref[co, :, pl.ds(own_col, ROWS)]
    aux_ref[1:2] = pos
    aux_ref[2:8] = jnp.zeros((6, ROWS), F32)
    for r, (u_ref, b_ref) in enumerate(zip((u0, u1, u2, u3), (b0, b1, b2, b3))):
        rows = slice(r * ROWS, (r + 1) * ROWS)
        u = u_ref[...]
        for h, c_ref in enumerate((own_ref, other_ref)):
            cols = c_ref.shape[0]
            for c in range(0, cols, CHUNK):
                e = expo(dot_nt(u, c_ref[c : c + CHUNK]))
                if h == 0 and r == 0:
                    e = clear_self(e, c, xy * ROWS)
                half = co if h == 0 else 1 - co
                w_ref[h, rows, c : c + CHUNK] = (e * inv_ref[half, :, c : c + CHUNK]).astype(BF16)
    b = dot_nn(w_ref[0], own_ref[...]) + dot_nn(w_ref[1], other_ref[...])
    for r, b_ref in enumerate((b0, b1, b2, b3)):
        b_ref[0:ROWS] = b[r * ROWS : (r + 1) * ROWS]
        b_ref[ROWS : ROWS + 1] = logs
        b_ref[ROWS + 1 :] = jnp.zeros((7, ROWS), F32)


def final_kernel(place_ref, x_ref, aux_ref, a0, a1, a2, a3, b0, b1, b2, b3, loss_ref, grad_ref, log_ref):
    z = place_ref[0]
    x = x_ref[...]
    radius = jnp.sqrt(jnp.sum(x * x, axis=1, keepdims=True) + EPS)
    unit = x / radius
    ap = a0[...] + a1[...] + a2[...] + a3[...]
    b = b0[0:ROWS] + b1[0:ROWS] + b2[0:ROWS] + b3[0:ROWS]
    inv = down_rows(aux_ref[0:1])
    d = INV_TEMP * (ap[0:ROWS] * inv + b - 2.0 * ap[ROWS:])
    grad_ref[...] = (d - unit * jnp.sum(unit * d, axis=1, keepdims=True)) / radius
    for r, b_ref in enumerate((b0, b1, b2, b3)):
        log_ref[lax.rem(z - r + NZ, NZ)] = b_ref[ROWS : ROWS + 8]
    logs = log_ref[0, 0:1]
    for k in range(1, NZ):
        logs = logs + log_ref[k, 0:1]
    loss_ref[...] = jnp.sum(logs - aux_ref[1:2], axis=1, keepdims=True) / VIEWS


def shift(x, by):
    return lax.ppermute(x, "z", [((k + by) % NZ, k) for k in range(NZ)])


def body(proj, partner):
    y, xh, xl = (lax.axis_index(a) for a in XY)
    z, co = lax.axis_index("z"), lax.axis_index("co")
    xy = (y * 2 + xh) * 2 + xl
    place = jnp.stack([z, co, xy]).astype(jnp.int32)
    unit, copies = call(norm_kernel, [sds((ROWS, ROWS), BF16), sds((NXY, ROWS, ROWS), BF16)])(proj)
    plane = lax.all_to_all(copies, XY, 0, 0, tiled=True)
    rows = [unit] + [shift(unit, r) for r in range(1, NZ)]
    mates = partner.reshape(NXY, NZ, NCO, ROWS)
    mates = lax.dynamic_slice(mates, (xy, 0, co, 0), (1, NZ, 1, ROWS)).reshape(NZ, ROWS)
    mates = jnp.concatenate([mates, mates])
    mates = lax.dynamic_slice_in_dim(mates, z, NZ, 0)
    plane, mates, *rows = lax.optimization_barrier((plane, mates, *rows))
    other = lax.ppermute(plane, "co", [(0, 1), (1, 0)])
    cols = NXY * ROWS
    plane = plane.reshape(cols, ROWS)
    other = other.reshape(cols, ROWS)
    n = NZ * ROWS
    work = dict(flops=6 * n * cols * ROWS, nbytes=2**20, exps=n * cols)
    scratch = (pltpu.VMEM((n, cols), BF16), pltpu.VMEM((n, cols), BF16), pltpu.VMEM((NZ, ROWS), F32))
    first = call(
        functools.partial(sums_kernel, True),
        [sds((NZ, ROWS)), sds((n, ROWS)), sds((n, ROWS))],
        scratch,
        **work,
    )(place, *rows, plane, mates)
    send, *ap = call(
        functools.partial(sums_kernel, False),
        [sds((NDEV, 1, 2 * ROWS))] + [sds((2 * ROWS, ROWS))] * NZ,
        scratch,
        **work,
    )(place, *rows, other, mates, *first)
    got = lax.all_to_all(send, ALL, 0, 0, tiled=True)
    ap = [ap[0]] + [shift(ap[r], -r) for r in range(1, NZ)]
    got, *ap = lax.optimization_barrier((got, *ap))
    *b, aux = call(
        grads_kernel,
        [sds((ROWS + 8, ROWS))] * NZ + [sds((8, ROWS))],
        (pltpu.VMEM((NCO, 1, cols), F32), pltpu.VMEM((NCO, n, cols), BF16)),
        flops=8 * n * cols * ROWS,
        nbytes=2**20,
        exps=2 * n * cols,
    )(place, *rows, plane, other, got)
    b = [b[0]] + [shift(b[r], -r) for r in range(1, NZ)]
    loss, grad = call(
        final_kernel,
        [sds((1, 1)), sds((ROWS, ROWS))],
        (pltpu.VMEM((NZ, 8, ROWS), F32),),
    )(place, proj, aux, *ap, *b)
    return loss.reshape(()), grad


def solution(mesh):
    fine = Mesh(mesh.devices.reshape(4, 2, 2, 4, 2), ALL)
    return jax.shard_map(
        body,
        mesh=fine,
        in_specs=(P(ALL, None), P()),
        out_specs=(P(), P(ALL, None)),
        check_vma=False,
    )
```

time: 262 us -> 59 us (0.23)
  blocking collectives: 197 us -> 14.4 us
  starting transfers between devices: 0.04 us -> 23.9 us
  local copies, waits for them, and re-layouts: 18.4 us -> 0.9 us
  between operations: 15.9 us -> 0.73 us
  loops' own time: 13.6 us -> 0 us
  matrix products: 11 us -> 0 us
  Pallas kernels: 0 us -> 10.2 us
  waiting for transfers between devices: 0.04 us -> 8.45 us
  other arithmetic: 5.25 us -> 0.08 us
    psum x2 -> x0, blocking collectives: 116 us -> none  [the longest x1 63.2 us: body(): loss = lax.psum(local_loss, ('blk', 'dp')) / (views_here * n_dp * n_blk)]
    all_gather x3 -> x0, blocking collectives: 80.5 us -> none  [the longest x1 35 us: body(): cols_z = lax.all_gather(unit_b, 'blk', axis=0, tiled=True)]
    ppermute x0 -> x10, starting transfers between devices: none -> 16.8 us  [the longest x9 16.8 us: shift(): return lax.ppermute(x, 'z', [((k + by) % NZ, k) for k in range(NZ)])]
    all_to_all x0 -> x1, blocking collectives: none -> 14.4 us  [body(): got = lax.all_to_all(send, ALL, 0, 0, tiled=True)]
    another operation x2 -> x0, loops' own time: 13.6 us -> none  [the longest x1 6.82 us: tile_sums(): esum, pos = lax.map(one_block, starts)]
    gather x1 -> x0, local copies, waits for them, and re-layouts: 11.8 us -> none  [body(): group_mates = jnp.take(partner, group_ids, axis=0)]
    dot_general x8 -> x0, matrix products: 11 us -> none  [the longest x4 7.25 us: one_block(): return jnp.dot(weight, cols_z, preferred_element_type=jnp.float32)]
    pallas_call x0 -> x5, Pallas kernels: none -> 10.2 us  [run(): pl.pallas_call(body, out_shape=outs, in_specs=[SMEM if a.dtype == jnp.int...]
  transfers between devices with their start and end apart: 1 -> 11, of which waited for: 0 -> 5; matrix products, arithmetic and copies ran while one was open for 0% -> 0% of each run, Pallas kernels for 0% -> 4%
where the time goes in v1:
time: 59 us; the launch traced here: 58.8 us
  starting transfers between devices  23.9 us (41%)
  blocking collectives  14.4 us (24%)
  Pallas kernels  10.2 us (17%)
  waiting for transfers between devices  8.45 us (14%)
  local copies, waits for them, and re-layouts  0.9 us (2%)
  between operations  0.73 us (1%)
    ppermute x9, starting transfers between devices, shift(): return lax.ppermute(x, 'z', [((k + by) % NZ, k) for k in range(NZ)])  16.8 us
    all_to_all x1, blocking collectives, body(): got = lax.all_to_all(send, ALL, 0, 0, tiled=True)  14.4 us
    pallas_call x5, Pallas kernels, run(): pl.pallas_call(body, out_shape=outs, in_specs=[SMEM if a.dtype == jnp.int...  10.2 us
    all_to_all x1, starting transfers between devices, body(): plane = lax.all_to_all(copies, XY, 0, 0, tiled=True)  7.12 us
    ppermute x9, waiting for transfers between devices, shift(): return lax.ppermute(x, 'z', [((k + by) % NZ, k) for k in range(NZ)])  6.4 us
    all_to_all x1, waiting for transfers between devices, body(): plane = lax.all_to_all(copies, XY, 0, 0, tiled=True)  2.05 us
  transfers between devices with their start and end apart: 11, of which 5 were waited for; matrix products, arithmetic and copies ran while one was open for 0% of the time, Pallas kernels for 4%

profile of v1, /device:TPU:0, one launch (start us, length us, event | category | flops | bytes accessed | tf_op | source)
XLA Modules:
  0.0 58.8 jit_solution(1383295548316247507)
XLA Ops:
  0.6 0.0 copy-start
  0.6 0.0 copy-start.1
  0.7 0.9 %copy-done.1 = f32[128,128]{1,0:T(8,128)S(1)} copy-done((f32[128,128]{1,0:T(8,128)S(1)}, f32[128,128]{1,0:T(8,128)}, u32[]{:S(2)}) %copy-start.1) | copy-done | bytes 65560
  1.5 0.9 %shard_map.41 = (bf16[128,128]{1,0:T(8,128)(2,1)S(1)}, bf16[16,128,128]{2,1,0:T(8,128)(2,1)}) custom-call(f32[128,128]{1,0:T(8,128)S(1)} %copy-done.1), custom_call_target="tpu_custom_call" | custom-call | tf_op jit(solution)/shard_map/pallas_call | solution.py:32
  2.5 7.1 %all-to-all-start = ((bf16[16,128,128]{2,1,0:T(8,128)(2,1)}), bf16[16,128,128]{2,1,0:T(8,128)(2,1)S(1)}, u32[]{:S(2)}, u32[]{:S(2)}) async-start(bf16[16,128,128]{2,1,0:T(8,128)(2,1)} %get-tuple-element.30), calls=%async_computation | async-start | bytes 1048576 | tf_op jit(solution)/shard_map/all_to_all | solution.py:198
  9.6 2.0 %collective-permute-start.2 = (bf16[128,128]{1,0:T(8,128)(2,1)S(1)}, bf16[128,128]{1,0:T(8,128)(2,1)S(1)}, u32[]{:S(2)}, u32[]{:S(2)}) collective-permute-start(bf16[128,128]{1,0:T(8,128)(2,1)S(1)} %get-tuple-element.32.refs_1_.u0), channel_id=1, source_target_pairs={{6,0},{0,2},{2,4},{4,6},{7,1},{1,3},{3,5},{5,7},{14,8},{8,10},{10,... | collective-permute-start | bytes 98312 | tf_op jit(solution)/shard_map/ppermute | solution.py:189
  11.6 3.6 %collective-permute-start.1 = (bf16[128,128]{1,0:T(8,128)(2,1)S(1)}, bf16[128,128]{1,0:T(8,128)(2,1)S(1)}, u32[]{:S(2)}, u32[]{:S(2)}) collective-permute-start(bf16[128,128]{1,0:T(8,128)(2,1)S(1)} %get-tuple-element.32.refs_1_.u0), channel_id=1, source_target_pairs={{4,0},{6,2},{0,4},{2,6},{5,1},{7,3},{1,5},{3,7},{12,8},{14,10},{8,... | collective-permute-start | bytes 98312 | tf_op jit(solution)/shard_map/ppermute | solution.py:189
  15.2 1.0 %collective-permute-start = (bf16[128,128]{1,0:T(8,128)(2,1)S(1)}, bf16[128,128]{1,0:T(8,128)(2,1)S(1)}, u32[]{:S(2)}, u32[]{:S(2)}) collective-permute-start(bf16[128,128]{1,0:T(8,128)(2,1)S(1)} %get-tuple-element.32.refs_1_.u0), channel_id=1, source_target_pairs={{2,0},{4,2},{6,4},{0,6},{3,1},{5,3},{7,5},{1,7},{10,8},{12,10},{14... | collective-permute-start | bytes 98312 | tf_op jit(solution)/shard_map/ppermute | solution.py:189
  16.2 0.0 copy-done
  16.2 0.0 collective-permute-done.2.refs_4_.u3
  16.2 1.2 %collective-permute-done.1.refs_3_.u2 = bf16[128,128]{1,0:T(8,128)(2,1)S(1)} collective-permute-done((bf16[128,128]{1,0:T(8,128)(2,1)S(1)}, bf16[128,128]{1,0:T(8,128)(2,1)S(1)}, u32[]{:S(2)}, u32[]{:S(2)}) %collective-permute-start.1) | collective-permute-done | bytes 32800 | tf_op jit(solution)/shard_map/ppermute | solution.py:189
  17.4 1.7 %collective-permute-done.refs_2_.u1 = bf16[128,128]{1,0:T(8,128)(2,1)S(1)} collective-permute-done((bf16[128,128]{1,0:T(8,128)(2,1)S(1)}, bf16[128,128]{1,0:T(8,128)(2,1)S(1)}, u32[]{:S(2)}, u32[]{:S(2)}) %collective-permute-start) | collective-permute-done | bytes 32800 | tf_op jit(solution)/shard_map/ppermute | solution.py:189
  19.1 2.0 %all-to-all-done = bf16[16,128,128]{2,1,0:T(8,128)(2,1)S(1)} async-done(((bf16[16,128,128]{2,1,0:T(8,128)(2,1)}), bf16[16,128,128]{2,1,0:T(8,128)(2,1)S(1)}, u32[]{:S(2)}, u32[]{:S(2)}) %all-to-all-start) | async-done | bytes 524320 | tf_op jit(solution)/shard_map/all_to_all | solution.py:198
  21.1 0.0 collective-permute-start.3
  21.1 0.1 pad_add_fusion.1.refs_0_.place_ref
  21.2 2.5 %shard_map.42 = (f32[4,128]{1,0:T(4,128)S(1)}, f32[512,128]{1,0:T(8,128)S(1)}, f32[512,128]{1,0:T(8,128)S(1)}) custom-call(s32[3]{0:T(128)S(1)} %pad_add_fusion.1.refs_0_.place_ref, bf16[128,128]{1,0:T(8,128)(2,1)S(1)} %get-tuple-element.32.refs_1_.u0, bf16[128,128]{1,0:T(8,128)(2,1)S(1)} %collective-permute-done.refs_2_.u1, ...), custom_call_target="tpu_custom_call" | custom-call | flops 805306368 | bytes 1048576 | tf_op jit(solution)/shard_map/pallas_call | solution.py:32
  23.7 0.0 collective-permute-done.3
  23.7 2.4 %shard_map.43 = (f32[128,1,256]{2,1,0:T(1,128)S(1)}, f32[256,128]{1,0:T(8,128)S(1)}, f32[256,128]{1,0:T(8,128)S(1)}, f32[256,128]{1,0:T(8,128)S(1)}, f32[256,128]{1,0:T(8,128)S(1)}) custom-call(s32[3]{0:T(128)S(1)} %pad_add_fusion.1.refs_0_.place_ref, bf16[128,128]{1,0:T(8,128)(2,1)S(1)} %get-tuple-element.32.refs_1_.u0, ...), custom_call_target="tpu_custom_call" | custom-call | flops 805306368 | bytes 1048576 | tf_op jit(solution)/shard_map/pallas_call | solution.py:32
  26.1 2.0 %collective-permute-start.4 = (f32[256,128]{1,0:T(8,128)S(1)}, f32[256,128]{1,0:T(8,128)S(1)}, u32[]{:S(2)}, u32[]{:S(2)}) collective-permute-start(f32[256,128]{1,0:T(8,128)S(1)} %get-tuple-element.43), channel_id=1, source_target_pairs={{6,0},{0,2},{2,4},{4,6},{7,1},{1,3},{3,5},{5,7},{14,8},{8,10},{10,... | collective-permute-start | bytes 393224 | tf_op jit(solution)/shard_map/ppermute | solution.py:189
  28.1 3.6 %collective-permute-start.5 = (f32[256,128]{1,0:T(8,128)S(1)}, f32[256,128]{1,0:T(8,128)S(1)}, u32[]{:S(2)}, u32[]{:S(2)}) collective-permute-start(f32[256,128]{1,0:T(8,128)S(1)} %get-tuple-element.44), channel_id=1, source_target_pairs={{4,0},{6,2},{0,4},{2,6},{5,1},{7,3},{1,5},{3,7},{12,8},{14,10},{8,... | collective-permute-start | bytes 393224 | tf_op jit(solution)/shard_map/ppermute | solution.py:189
  31.7 1.0 %collective-permute-start.6 = (f32[256,128]{1,0:T(8,128)S(1)}, f32[256,128]{1,0:T(8,128)S(1)}, u32[]{:S(2)}, u32[]{:S(2)}) collective-permute-start(f32[256,128]{1,0:T(8,128)S(1)} %get-tuple-element.45), channel_id=1, source_target_pairs={{2,0},{4,2},{6,4},{0,6},{3,1},{5,3},{7,5},{1,7},{10,8},{12,10},{14... | collective-permute-start | bytes 393224 | tf_op jit(solution)/shard_map/ppermute | solution.py:189
  32.7 14.4 %all_to_all.10.got_ref = f32[128,1,256]{2,1,0:T(1,128)S(1)} all-to-all(f32[128,1,256]{2,1,0:T(1,128)S(1)} %get-tuple-element.41), channel_id=1, replica_groups=mesh['y'=4,'xh'=2,'xl'=2,'z'=4,'co'=2] {'y','xh','xl','z','co'}, dimensions={0} | all-to-all | bytes 262144 | tf_op jit(solution)/shard_map/all_to_all | solution.py:224
  47.1 0.0 collective-permute-done.4.a1
  47.1 0.0 collective-permute-done.5.a2
  47.1 0.0 collective-permute-done.6.a3
  47.1 0.0 copy-start.2
  47.1 3.0 %shard_map.44 = (f32[136,128]{1,0:T(8,128)S(1)}, f32[136,128]{1,0:T(8,128)S(1)}, f32[136,128]{1,0:T(8,128)S(1)}, f32[136,128]{1,0:T(8,128)S(1)}, f32[8,128]{1,0:T(8,128)S(1)}) custom-call(s32[3]{0:T(128)S(1)} %pad_add_fusion.1.refs_0_.place_ref, bf16[128,128]{1,0:T(8,128)(2,1)S(1)} %get-tuple-element.32.refs_1_.u0, ...), custom_call_target="tpu_custom_call" | custom-call | flops 1073741824 | bytes 1048576 | tf_op jit(solution)/shard_map/pallas_call | solution.py:32
  50.1 0.4 collective-permute-start.7
  50.6 1.7 %collective-permute-start.8 = (f32[136,128]{1,0:T(8,128)S(1)}, f32[136,128]{1,0:T(8,128)S(1)}, u32[]{:S(2)}, u32[]{:S(2)}) collective-permute-start(f32[136,128]{1,0:T(8,128)S(1)} %get-tuple-element.54), channel_id=1, source_target_pairs={{4,0},{6,2},{0,4},{2,6},{5,1},{7,3},{1,5},{3,7},{12,8},{14,10},{8,... | collective-permute-start | bytes 208904 | tf_op jit(solution)/shard_map/ppermute | solution.py:189
  52.3 1.5 %collective-permute-start.9 = (f32[136,128]{1,0:T(8,128)S(1)}, f32[136,128]{1,0:T(8,128)S(1)}, u32[]{:S(2)}, u32[]{:S(2)}) collective-permute-start(f32[136,128]{1,0:T(8,128)S(1)} %get-tuple-element.55), channel_id=1, source_target_pairs={{2,0},{4,2},{6,4},{0,6},{3,1},{5,3},{7,5},{1,7},{10,8},{12,10},{14... | collective-permute-start | bytes 208904 | tf_op jit(solution)/shard_map/ppermute | solution.py:189
  53.8 3.0 %collective-permute-done.7.b1 = f32[136,128]{1,0:T(8,128)S(1)} collective-permute-done((f32[136,128]{1,0:T(8,128)S(1)}, f32[136,128]{1,0:T(8,128)S(1)}, u32[]{:S(2)}, u32[]{:S(2)}) %collective-permute-start.7) | collective-permute-done | bytes 69664 | tf_op jit(solution)/shard_map/ppermute | solution.py:189
  56.8 0.0 collective-permute-done.8.b2
  56.8 0.5 collective-permute-done.9.b3
  57.3 0.0 copy-done.2
  57.3 1.4 %shard_map.45 = (f32[1,1]{1,0:T(1,128)}, f32[128,128]{1,0:T(8,128)}) custom-call(s32[3]{0:T(128)S(1)} %pad_add_fusion.1.refs_0_.place_ref, f32[128,128]{1,0:T(8,128)S(1)} %copy-done.2, f32[8,128]{1,0:T(8,128)S(1)} %get-tuple-element.47.aux_ref, f32[256,128]{1,0:T(8,128)S(1)} %get-tuple-element.48.a0, f32[256,128]{1,0:T(8,128)S(1)} %collective-permute-done.4.a1, ...), custom_call_target="tpu_custom_call" | custom-call | tf_op jit(solution)/shard_map/pallas_call | solution.py:32
  (3 shorter events, 0.0 us)
Async XLA Ops:
  0.6 15.5 %copy-start = (s32[16384]{0:T(1024)S(1)}, s32[16384]{0:T(1024)}, u32[]{:S(2)}) copy-start(s32[16384]{0:T(1024)} %param.3) | copy-start | bytes 196612
  0.6 0.9 %copy-start.1 = (f32[128,128]{1,0:T(8,128)S(1)}, f32[128,128]{1,0:T(8,128)}, u32[]{:S(2)}) copy-start(f32[128,128]{1,0:T(8,128)} %x_ref.3) | copy-start | bytes 196612
  2.5 18.7 %all-to-all-start = ((bf16[16,128,128]{2,1,0:T(8,128)(2,1)}), bf16[16,128,128]{2,1,0:T(8,128)(2,1)S(1)}, u32[]{:S(2)}, u32[]{:S(2)}) async-start(bf16[16,128,128]{2,1,0:T(8,128)(2,1)} %get-tuple-element.30), calls=%async_computation | async-start | bytes 1048576 | tf_op jit(solution)/shard_map/all_to_all | solution.py:198
  9.6 6.6 %collective-permute-start.2 = (bf16[128,128]{1,0:T(8,128)(2,1)S(1)}, bf16[128,128]{1,0:T(8,128)(2,1)S(1)}, u32[]{:S(2)}, u32[]{:S(2)}) collective-permute-start(bf16[128,128]{1,0:T(8,128)(2,1)S(1)} %get-tuple-element.32.refs_1_.u0), channel_id=1, source_target_pairs={{6,0},{0,2},{2,4},{4,6},{7,1},{1,3},{3,5},{5,7},{14,8},{8,10},{10,... | collective-permute-start | bytes 98312 | tf_op jit(solution)/shard_map/ppermute | solution.py:189
  11.6 5.8 %collective-permute-start.1 = (bf16[128,128]{1,0:T(8,128)(2,1)S(1)}, bf16[128,128]{1,0:T(8,128)(2,1)S(1)}, u32[]{:S(2)}, u32[]{:S(2)}) collective-permute-start(bf16[128,128]{1,0:T(8,128)(2,1)S(1)} %get-tuple-element.32.refs_1_.u0), channel_id=1, source_target_pairs={{4,0},{6,2},{0,4},{2,6},{5,1},{7,3},{1,5},{3,7},{12,8},{14,10},{8,... | collective-permute-start | bytes 98312 | tf_op jit(solution)/shard_map/ppermute | solution.py:189
  15.2 3.9 %collective-permute-start = (bf16[128,128]{1,0:T(8,128)(2,1)S(1)}, bf16[128,128]{1,0:T(8,128)(2,1)S(1)}, u32[]{:S(2)}, u32[]{:S(2)}) collective-permute-start(bf16[128,128]{1,0:T(8,128)(2,1)S(1)} %get-tuple-element.32.refs_1_.u0), channel_id=1, source_target_pairs={{2,0},{4,2},{6,4},{0,6},{3,1},{5,3},{7,5},{1,7},{10,8},{12,10},{14... | collective-permute-start | bytes 98312 | tf_op jit(solution)/shard_map/ppermute | solution.py:189
  21.1 2.6 %collective-permute-start.3 = (bf16[16,128,128]{2,1,0:T(8,128)(2,1)S(1)}, bf16[16,128,128]{2,1,0:T(8,128)(2,1)S(1)}, u32[]{:S(2)}, u32[]{:S(2)}) collective-permute-start(bf16[16,128,128]{2,1,0:T(8,128)(2,1)S(1)} %all-to-all-done), channel_id=1, source_target_pairs={{0,1},{1,0},{2,3},{3,2},{4,5},{5,4},{6,7},{7,6},{8,9},{9,8},{10,11... | collective-permute-start | bytes 1572872 | tf_op jit(solution)/shard_map/ppermute | solution.py:205
  26.1 21.0 %collective-permute-start.4 = (f32[256,128]{1,0:T(8,128)S(1)}, f32[256,128]{1,0:T(8,128)S(1)}, u32[]{:S(2)}, u32[]{:S(2)}) collective-permute-start(f32[256,128]{1,0:T(8,128)S(1)} %get-tuple-element.43), channel_id=1, source_target_pairs={{6,0},{0,2},{2,4},{4,6},{7,1},{1,3},{3,5},{5,7},{14,8},{8,10},{10,... | collective-permute-start | bytes 393224 | tf_op jit(solution)/shard_map/ppermute | solution.py:189
  28.1 19.0 %collective-permute-start.5 = (f32[256,128]{1,0:T(8,128)S(1)}, f32[256,128]{1,0:T(8,128)S(1)}, u32[]{:S(2)}, u32[]{:S(2)}) collective-permute-start(f32[256,128]{1,0:T(8,128)S(1)} %get-tuple-element.44), channel_id=1, source_target_pairs={{4,0},{6,2},{0,4},{2,6},{5,1},{7,3},{1,5},{3,7},{12,8},{14,10},{8,... | collective-permute-start | bytes 393224 | tf_op jit(solution)/shard_map/ppermute | solution.py:189
  31.7 15.4 %collective-permute-start.6 = (f32[256,128]{1,0:T(8,128)S(1)}, f32[256,128]{1,0:T(8,128)S(1)}, u32[]{:S(2)}, u32[]{:S(2)}) collective-permute-start(f32[256,128]{1,0:T(8,128)S(1)} %get-tuple-element.45), channel_id=1, source_target_pairs={{2,0},{4,2},{6,4},{0,6},{3,1},{5,3},{7,5},{1,7},{10,8},{12,10},{14... | collective-permute-start | bytes 393224 | tf_op jit(solution)/shard_map/ppermute | solution.py:189
  47.1 10.2 %copy-start.2 = (f32[128,128]{1,0:T(8,128)S(1)}, f32[128,128]{1,0:T(8,128)}, u32[]{:S(2)}) copy-start(f32[128,128]{1,0:T(8,128)} %x_ref.3) | copy-start | bytes 196612
  50.1 6.7 %collective-permute-start.7 = (f32[136,128]{1,0:T(8,128)S(1)}, f32[136,128]{1,0:T(8,128)S(1)}, u32[]{:S(2)}, u32[]{:S(2)}) collective-permute-start(f32[136,128]{1,0:T(8,128)S(1)} %get-tuple-element.53), channel_id=1, source_target_pairs={{6,0},{0,2},{2,4},{4,6},{7,1},{1,3},{3,5},{5,7},{14,8},{8,10},{10,... | collective-permute-start | bytes 208904 | tf_op jit(solution)/shard_map/ppermute | solution.py:189
  50.6 6.2 %collective-permute-start.8 = (f32[136,128]{1,0:T(8,128)S(1)}, f32[136,128]{1,0:T(8,128)S(1)}, u32[]{:S(2)}, u32[]{:S(2)}) collective-permute-start(f32[136,128]{1,0:T(8,128)S(1)} %get-tuple-element.54), channel_id=1, source_target_pairs={{4,0},{6,2},{0,4},{2,6},{5,1},{7,3},{1,5},{3,7},{12,8},{14,10},{8,... | collective-permute-start | bytes 208904 | tf_op jit(solution)/shard_map/ppermute | solution.py:189
  52.3 5.0 %collective-permute-start.9 = (f32[136,128]{1,0:T(8,128)S(1)}, f32[136,128]{1,0:T(8,128)S(1)}, u32[]{:S(2)}, u32[]{:S(2)}) collective-permute-start(f32[136,128]{1,0:T(8,128)S(1)} %get-tuple-element.55), channel_id=1, source_target_pairs={{2,0},{4,2},{6,4},{0,6},{3,1},{5,3},{7,5},{1,7},{10,8},{12,10},{14... | collective-permute-start | bytes 208904 | tf_op jit(solution)/shard_map/ppermute | solution.py:189

commit v2 on v1

v2 whole, which is shorter than its diff:
```python
import functools
import math

import jax
import jax.numpy as jnp
from jax import lax
from jax.experimental import pallas as pl
from jax.experimental.pallas import tpu as pltpu
from jax.sharding import Mesh, PartitionSpec as P

EPS = 1e-06
INV_TEMP = 10.0
SCALE = INV_TEMP * math.log2(math.e)

ROWS = 128
NXY = 16
NZ = 4
NCO = 2
NDEV = NXY * NZ * NCO
VIEWS = NDEV * ROWS
XY = ("y", "xh", "xl")
ALL = ("y", "xh", "xl", "z", "co")
CHUNK = 256
F32 = jnp.float32
BF16 = jnp.bfloat16
VMEM = pl.BlockSpec(memory_space=pltpu.VMEM)
SMEM = pl.BlockSpec(memory_space=pltpu.SMEM)


def call(body, outs, scratch=(), flops=0, nbytes=0, exps=0):
    def run(*args):
        return pl.pallas_call(
            body,
            out_shape=outs,
            in_specs=[SMEM if a.dtype == jnp.int32 and a.ndim == 1 else VMEM for a in args],
            out_specs=[VMEM] * len(outs),
            scratch_shapes=list(scratch),
            compiler_params=pltpu.CompilerParams(vmem_limit_bytes=24 * 2**20),
            cost_estimate=pl.CostEstimate(flops=flops, bytes_accessed=nbytes, transcendentals=exps),
        )(*args)

    return run


def sds(shape, dtype=F32):
    return jax.ShapeDtypeStruct(shape, dtype)


def dot_nt(a, b):
    return lax.dot_general(a, b, (((1,), (1,)), ((), ())), preferred_element_type=F32)


def dot_nn(a, b):
    return lax.dot_general(a, b, (((1,), (0,)), ((), ())), preferred_element_type=F32)


def down_rows(row):
    return jnp.transpose(jnp.broadcast_to(row, (ROWS, ROWS)))


def norm_kernel(x_ref, u_ref, copies_ref):
    x = x_ref[...]
    radius = jnp.sqrt(jnp.sum(x * x, axis=1, keepdims=True) + EPS)
    unit = (x / radius).astype(BF16)
    u_ref[...] = unit
    copies_ref[...] = jnp.broadcast_to(unit[None], (NXY, ROWS, ROWS))


def expo(s):
    return jnp.exp2(s * SCALE)


def local_mates(mates, z, half):
    here = (((mates >> 8) & 3) == z) & (((mates >> 7) & 1) == half)
    return jnp.where(here, ((mates >> 10) << 7) | (mates & 127), -1)


def sums_kernel(own_half, *refs):
    place_ref, u0, u1, u2, u3, c_ref, mate_ref = refs[:7]
    z, co, xy = place_ref[0], place_ref[1], place_ref[2]
    half = co if own_half else 1 - co
    mates = mate_ref[...]
    local = local_mates(mates, z, half)
    width = NZ * ROWS
    mate = jnp.concatenate([local[r : r + 1] for r in range(NZ)], axis=1)
    mate = jnp.broadcast_to(mate, (8, width))
    u = jnp.concatenate([u0[...], u1[...], u2[...], u3[...]], axis=0)
    down = lax.broadcasted_iota(jnp.int32, (8, width), 0)
    sums = jnp.zeros((8, width), F32)
    pos = jnp.zeros((8, width), F32)
    for c in range(0, c_ref.shape[0], CHUNK):
        s = dot_nt(c_ref[c : c + CHUNK], u)
        e = expo(s)
        if own_half:
            col = lax.broadcasted_iota(jnp.int32, (CHUNK, ROWS), 0) + (c - xy * ROWS)
            row = lax.broadcasted_iota(jnp.int32, (CHUNK, ROWS), 1)
            e = jnp.concatenate([jnp.where(col == row, 0.0, e[:, :ROWS]), e[:, ROWS:]], axis=1)
        for k in range(0, CHUNK, 8):
            sums = sums + e[k : k + 8]
            pos = pos + jnp.where(mate == down + (c + k), s[k : k + 8], 0.0)
    sums = jnp.sum(sums, axis=0, keepdims=True)
    pos = jnp.sum(pos, axis=0, keepdims=True) * INV_TEMP
    rows = [sums[:, r * ROWS : (r + 1) * ROWS] for r in range(NZ)]
    rows.append(sum(pos[:, r * ROWS : (r + 1) * ROWS] for r in range(NZ)))
    if own_half:
        out_ref = refs[7]
        for q, row in enumerate(rows):
            out_ref[q : q + 1] = row
        out_ref[5:8] = jnp.zeros((3, ROWS), F32)
        return
    in_ref, send_ref, out_ref = refs[7:]
    rows = [row + in_ref[q : q + 1] for q, row in enumerate(rows)]
    for q in range(NZ):
        out_ref[q : q + 1] = rows[q]
    out_ref[4:8] = jnp.zeros((4, ROWS), F32)
    for k in range(NZ):
        r = lax.rem(k - z + NZ, NZ)
        row = rows[0]
        for q in range(1, NZ):
            row = jnp.where(r == q, rows[q], row)
        piece = jnp.concatenate([row, rows[NZ]], axis=1)
        for xy_to in range(NXY):
            for co_to in range(NCO):
                send_ref[xy_to * 8 + k * 2 + co_to] = piece


def grads_kernel(
    place_ref, u0, u1, u2, u3, own_ref, other_ref, mate_ref, got_ref, s0, s1, s2, s3, b0, b1, b2, b3, aux_ref, inv_ref
):
    z, co, xy = place_ref[0], place_ref[1], place_ref[2]
    logs = jnp.zeros((1, ROWS), F32)
    for k in range(NXY):
        for c in range(NCO):
            total = got_ref[k * 8 + c, :, 0:ROWS]
            for q in range(1, NZ):
                total = total + got_ref[k * 8 + q * 2 + c, :, 0:ROWS]
            logs = logs + jnp.log(total)
            inv_ref[c, :, k * ROWS : (k + 1) * ROWS] = 1.0 / total
    pos = got_ref[0, :, ROWS:]
    for k in range(1, NDEV):
        pos = pos + got_ref[k, :, ROWS:]
    aux_ref[0:1] = pos
    aux_ref[1:8] = jnp.zeros((7, ROWS), F32)
    parts = (s0, s1, s2, s3)
    inv_row = []
    for r in range(NZ):
        total = s0[r : r + 1]
        for q in range(1, NZ):
            k = (r - q) % NZ
            total = total + parts[q][k : k + 1]
        inv_row.append(down_rows(1.0 / total))
    inv_row = jnp.concatenate(inv_row, axis=0)
    mates = mate_ref[...]
    u = jnp.concatenate([u0[...], u1[...], u2[...], u3[...]], axis=0)
    lane = lax.broadcasted_iota(jnp.int32, (NZ * ROWS, ROWS), 1)
    total = jnp.zeros((NZ * ROWS, ROWS), F32)
    for h, c_ref in enumerate((own_ref, other_ref)):
        half = co if h == 0 else 1 - co
        local = local_mates(mates, z, half)
        mate = jnp.concatenate([down_rows(local[r : r + 1]) for r in range(NZ)], axis=0)
        for c in range(0, c_ref.shape[0], CHUNK):
            e = expo(dot_nt(u, c_ref[c : c + CHUNK]))
            if h == 0:
                col = lax.broadcasted_iota(jnp.int32, (ROWS, CHUNK), 1) + (c - xy * ROWS)
                row = lax.broadcasted_iota(jnp.int32, (ROWS, CHUNK), 0)
                e = jnp.concatenate([jnp.where(col == row, 0.0, e[:ROWS]), e[ROWS:]], axis=0)
            weight = []
            for k in range(0, CHUNK, ROWS):
                w = e[:, k : k + ROWS] * (inv_row + inv_ref[half, :, c + k : c + k + ROWS])
                w = w - jnp.where(mate == lane + (c + k), 2.0, 0.0)
                weight.append(w.astype(BF16))
            total = total + dot_nn(jnp.concatenate(weight, axis=1), c_ref[c : c + CHUNK])
    for r, b_ref in enumerate((b0, b1, b2, b3)):
        b_ref[0:ROWS] = total[r * ROWS : (r + 1) * ROWS]
        b_ref[ROWS : ROWS + 1] = logs
        b_ref[ROWS + 1 :] = jnp.zeros((7, ROWS), F32)


def final_kernel(place_ref, x_ref, aux_ref, b0, b1, b2, b3, loss_ref, grad_ref, log_ref):
    z = place_ref[0]
    x = x_ref[...]
    radius = jnp.sqrt(jnp.sum(x * x, axis=1, keepdims=True) + EPS)
    unit = x / radius
    d = INV_TEMP * (b0[0:ROWS] + b1[0:ROWS] + b2[0:ROWS] + b3[0:ROWS])
    grad_ref[...] = (d - unit * jnp.sum(unit * d, axis=1, keepdims=True)) / radius
    for r, b_ref in enumerate((b0, b1, b2, b3)):
        log_ref[lax.rem(z - r + NZ, NZ)] = b_ref[ROWS : ROWS + 8]
    logs = log_ref[0, 0:1]
    for k in range(1, NZ):
        logs = logs + log_ref[k, 0:1]
    loss_ref[...] = jnp.sum(logs - aux_ref[0:1], axis=1, keepdims=True) / VIEWS


def shift(x, by):
    return lax.ppermute(x, "z", [((k + by) % NZ, k) for k in range(NZ)])


def body(proj, partner):
    y, xh, xl = (lax.axis_index(a) for a in XY)
    z, co = lax.axis_index("z"), lax.axis_index("co")
    xy = (y * 2 + xh) * 2 + xl
    place = jnp.stack([z, co, xy]).astype(jnp.int32)
    unit, copies = call(norm_kernel, [sds((ROWS, ROWS), BF16), sds((NXY, ROWS, ROWS), BF16)])(proj)
    plane = lax.all_to_all(copies, XY, 0, 0, tiled=True)
    rows = [unit] + [shift(unit, r) for r in range(1, NZ)]
    mates = partner.reshape(NXY, NZ, NCO, ROWS)
    mates = lax.dynamic_slice(mates, (xy, 0, co, 0), (1, NZ, 1, ROWS)).reshape(NZ, ROWS)
    mates = jnp.concatenate([mates, mates])
    mates = lax.dynamic_slice_in_dim(mates, z, NZ, 0)
    plane, mates, *rows = lax.optimization_barrier((plane, mates, *rows))
    other = lax.ppermute(plane, "co", [(0, 1), (1, 0)])
    cols = NXY * ROWS
    plane = plane.reshape(cols, ROWS)
    other = other.reshape(cols, ROWS)
    n = NZ * ROWS
    work = dict(flops=2 * n * cols * ROWS, nbytes=2**20, exps=n * cols)
    first = call(
        functools.partial(sums_kernel, True), [sds((8, ROWS))], **work
    )(place, *rows, plane, mates)
    send, sums = call(
        functools.partial(sums_kernel, False),
        [sds((NDEV, 1, 2 * ROWS)), sds((8, ROWS))],
        **work,
    )(place, *rows, other, mates, *first)
    got = lax.all_to_all(send, ALL, 0, 0, tiled=True)
    sums = [sums] + [shift(sums, r) for r in range(1, NZ)]
    got, *sums = lax.optimization_barrier((got, *sums))
    *b, aux = call(
        grads_kernel,
        [sds((ROWS + 8, ROWS))] * NZ + [sds((8, ROWS))],
        (pltpu.VMEM((NCO, 1, cols), F32),),
        flops=8 * n * cols * ROWS,
        nbytes=2**20,
        exps=2 * n * cols,
    )(place, *rows, plane, other, mates, got, *sums)
    b = [b[0]] + [shift(b[r], -r) for r in range(1, NZ)]
    loss, grad = call(
        final_kernel,
        [sds((1, 1)), sds((ROWS, ROWS))],
        (pltpu.VMEM((NZ, 8, ROWS), F32),),
    )(place, proj, aux, *b)
    return loss.reshape(()), grad


def solution(mesh):
    fine = Mesh(mesh.devices.reshape(4, 2, 2, 4, 2), ALL)
    return jax.shard_map(
        body,
        mesh=fine,
        in_specs=(P(ALL, None), P()),
        out_specs=(P(), P(ALL, None)),
        check_vma=False,
    )
```

time: 59 us -> 54.5 us (0.924)
  blocking collectives: 14.4 us -> 0 us
  starting transfers between devices: 23.9 us -> 30.4 us
  waiting for transfers between devices: 8.45 us -> 12.5 us
    all_to_all x1 -> x0, blocking collectives: 14.4 us -> none  [body(): got = lax.all_to_all(send, ALL, 0, 0, tiled=True)]
    all_to_all x0 -> x1, starting transfers between devices: none -> 7.34 us  [body(): got = lax.all_to_all(send, ALL, 0, 0, tiled=True)]
    ppermute x9, waiting for transfers between devices: 6.4 us -> 8.68 us  [shift(): return lax.ppermute(x, 'z', [((k + by) % NZ, k) for k in range(NZ)])]
    all_to_all x0 -> x1, waiting for transfers between devices: none -> 1.65 us  [body(): got = lax.all_to_all(send, ALL, 0, 0, tiled=True)]
    ppermute x9, starting transfers between devices: 16.8 us -> 15.9 us  [shift(): return lax.ppermute(x, 'z', [((k + by) % NZ, k) for k in range(NZ)])]
  transfers between devices with their start and end apart: 11 -> 12, of which waited for: 5 -> 9; matrix products, arithmetic and copies ran while one was open for 0% -> 0% of each run, Pallas kernels for 4% -> 3%
where the time goes in v2:
time: 54.5 us; the launch traced here: 54.3 us
  starting transfers between devices  30.4 us (56%)
  waiting for transfers between devices  12.5 us (23%)
  Pallas kernels  9.68 us (18%)
  local copies, waits for them, and re-layouts  0.9 us (2%)
  between operations  0.72 us (1%)
    ppermute x9, starting transfers between devices, shift(): return lax.ppermute(x, 'z', [((k + by) % NZ, k) for k in range(NZ)])  15.9 us
    pallas_call x5, Pallas kernels, run(): pl.pallas_call(body, out_shape=outs, in_specs=[SMEM if a.dtype == jnp.int...  9.68 us
    ppermute x9, waiting for transfers between devices, shift(): return lax.ppermute(x, 'z', [((k + by) % NZ, k) for k in range(NZ)])  8.68 us
    all_to_all x1, starting transfers between devices, body(): got = lax.all_to_all(send, ALL, 0, 0, tiled=True)  7.34 us
    all_to_all x1, starting transfers between devices, body(): plane = lax.all_to_all(copies, XY, 0, 0, tiled=True)  7.12 us
    all_to_all x1, waiting for transfers between devices, body(): plane = lax.all_to_all(copies, XY, 0, 0, tiled=True)  2.05 us
    all_to_all x1, waiting for transfers between devices, body(): got = lax.all_to_all(send, ALL, 0, 0, tiled=True)  1.65 us
  transfers between devices with their start and end apart: 12, of which 9 were waited for; matrix products, arithmetic and copies ran while one was open for 0% of the time, Pallas kernels for 3%

profile of v2, /device:TPU:0, one launch (start us, length us, event | category | flops | bytes accessed | tf_op | source)
XLA Modules:
  0.0 54.3 jit_solution(2118422829065578116)
XLA Ops:
  0.6 0.0 copy-start
  0.6 0.0 copy-start.1
  0.7 0.9 %copy-done.1 = f32[128,128]{1,0:T(8,128)S(1)} copy-done((f32[128,128]{1,0:T(8,128)S(1)}, f32[128,128]{1,0:T(8,128)}, u32[]{:S(2)}) %copy-start.1) | copy-done | bytes 65560
  1.5 0.9 %shard_map.41 = (bf16[128,128]{1,0:T(8,128)(2,1)S(1)}, bf16[16,128,128]{2,1,0:T(8,128)(2,1)}) custom-call(f32[128,128]{1,0:T(8,128)S(1)} %copy-done.1), custom_call_target="tpu_custom_call" | custom-call | tf_op jit(solution)/shard_map/pallas_call | solution.py:32
  2.5 7.1 %all-to-all-start = ((bf16[16,128,128]{2,1,0:T(8,128)(2,1)}), bf16[16,128,128]{2,1,0:T(8,128)(2,1)S(1)}, u32[]{:S(2)}, u32[]{:S(2)}) async-start(bf16[16,128,128]{2,1,0:T(8,128)(2,1)} %get-tuple-element.24), calls=%async_computation | async-start | bytes 1048576 | tf_op jit(solution)/shard_map/all_to_all | solution.py:204
  9.6 2.0 %collective-permute-start.2 = (bf16[128,128]{1,0:T(8,128)(2,1)S(1)}, bf16[128,128]{1,0:T(8,128)(2,1)S(1)}, u32[]{:S(2)}, u32[]{:S(2)}) collective-permute-start(bf16[128,128]{1,0:T(8,128)(2,1)S(1)} %get-tuple-element.26.refs_1_.u0), channel_id=1, source_target_pairs={{6,0},{0,2},{2,4},{4,6},{7,1},{1,3},{3,5},{5,7},{14,8},{8,10},{10,... | collective-permute-start | bytes 98312 | tf_op jit(solution)/shard_map/ppermute | solution.py:195
  11.6 3.6 %collective-permute-start.1 = (bf16[128,128]{1,0:T(8,128)(2,1)S(1)}, bf16[128,128]{1,0:T(8,128)(2,1)S(1)}, u32[]{:S(2)}, u32[]{:S(2)}) collective-permute-start(bf16[128,128]{1,0:T(8,128)(2,1)S(1)} %get-tuple-element.26.refs_1_.u0), channel_id=1, source_target_pairs={{4,0},{6,2},{0,4},{2,6},{5,1},{7,3},{1,5},{3,7},{12,8},{14,10},{8,... | collective-permute-start | bytes 98312 | tf_op jit(solution)/shard_map/ppermute | solution.py:195
  15.2 1.0 %collective-permute-start = (bf16[128,128]{1,0:T(8,128)(2,1)S(1)}, bf16[128,128]{1,0:T(8,128)(2,1)S(1)}, u32[]{:S(2)}, u32[]{:S(2)}) collective-permute-start(bf16[128,128]{1,0:T(8,128)(2,1)S(1)} %get-tuple-element.26.refs_1_.u0), channel_id=1, source_target_pairs={{2,0},{4,2},{6,4},{0,6},{3,1},{5,3},{7,5},{1,7},{10,8},{12,10},{14... | collective-permute-start | bytes 98312 | tf_op jit(solution)/shard_map/ppermute | solution.py:195
  16.2 0.0 copy-done
  16.2 0.0 collective-permute-done.2.refs_4_.u3
  16.2 1.2 %collective-permute-done.1.refs_3_.u2 = bf16[128,128]{1,0:T(8,128)(2,1)S(1)} collective-permute-done((bf16[128,128]{1,0:T(8,128)(2,1)S(1)}, bf16[128,128]{1,0:T(8,128)(2,1)S(1)}, u32[]{:S(2)}, u32[]{:S(2)}) %collective-permute-start.1) | collective-permute-done | bytes 32800 | tf_op jit(solution)/shard_map/ppermute | solution.py:195
  17.4 1.7 %collective-permute-done.refs_2_.u1 = bf16[128,128]{1,0:T(8,128)(2,1)S(1)} collective-permute-done((bf16[128,128]{1,0:T(8,128)(2,1)S(1)}, bf16[128,128]{1,0:T(8,128)(2,1)S(1)}, u32[]{:S(2)}, u32[]{:S(2)}) %collective-permute-start) | collective-permute-done | bytes 32800 | tf_op jit(solution)/shard_map/ppermute | solution.py:195
  19.1 2.0 %all-to-all-done = bf16[16,128,128]{2,1,0:T(8,128)(2,1)S(1)} async-done(((bf16[16,128,128]{2,1,0:T(8,128)(2,1)}), bf16[16,128,128]{2,1,0:T(8,128)(2,1)S(1)}, u32[]{:S(2)}, u32[]{:S(2)}) %all-to-all-start) | async-done | bytes 524320 | tf_op jit(solution)/shard_map/all_to_all | solution.py:204
  21.1 0.0 collective-permute-start.3
  21.1 0.1 pad_add_fusion.1.refs_0_.place_ref
  21.2 1.7 %shard_map.42.refs_7_ = f32[8,128]{1,0:T(8,128)S(1)} custom-call(s32[3]{0:T(128)S(1)} %pad_add_fusion.1.refs_0_.place_ref, bf16[128,128]{1,0:T(8,128)(2,1)S(1)} %get-tuple-element.26.refs_1_.u0, bf16[128,128]{1,0:T(8,128)(2,1)S(1)} %collective-permute-done.refs_2_.u1, bf16[128,128]{1,0:T(8,128)(2,1)S(1)} %collective-permute-done.1.refs_3_.u2, ...), custom_call_target="tpu_custom_call" | custom-call | flops 268435456 | bytes 1048576 | tf_op jit(solution)/shard_map/pallas_call | solution.py:32
  22.9 0.1 collective-permute-done.3
  23.0 2.2 %shard_map.43 = (f32[128,1,256]{2,1,0:T(1,128)}, f32[8,128]{1,0:T(8,128)S(1)}) custom-call(s32[3]{0:T(128)S(1)} %pad_add_fusion.1.refs_0_.place_ref, bf16[128,128]{1,0:T(8,128)(2,1)S(1)} %get-tuple-element.26.refs_1_.u0, bf16[128,128]{1,0:T(8,128)(2,1)S(1)} %collective-permute-done.refs_2_.u1, bf16[128,128]{1,0:T(8,128)(2,1)S(1)} %collective-permute-done.1.refs_3_.u2, ...), custom_call_target="tpu_custom_call" | custom-call | flops 268435456 | bytes 1048576 | tf_op jit(solution)/shard_map/pallas_call | solution.py:32
  25.3 7.3 %all-to-all-start.1 = ((f32[128,1,256]{2,1,0:T(1,128)}), f32[128,1,256]{2,1,0:T(1,128)S(1)}, u32[]{:S(2)}, u32[]{:S(2)}) async-start(f32[128,1,256]{2,1,0:T(1,128)} %get-tuple-element.32), calls=%async_computation.1 | async-start | bytes 262144 | tf_op jit(solution)/shard_map/all_to_all | solution.py:225
  32.6 0.0 copy-start.2
  32.6 1.1 %collective-permute-start.6 = (f32[8,128]{1,0:T(8,128)S(1)}, f32[8,128]{1,0:T(8,128)S(1)}, u32[]{:S(2)}, u32[]{:S(2)}) collective-permute-start(f32[8,128]{1,0:T(8,128)S(1)} %get-tuple-element.35.s0), channel_id=1, source_target_pairs={{6,0},{0,2},{2,4},{4,6},{7,1},{1,3},{3,5},{5,7},{14,8},{8,10},{10,... | collective-permute-start | bytes 12296 | tf_op jit(solution)/shard_map/ppermute | solution.py:195
  33.8 3.2 %collective-permute-start.5 = (f32[8,128]{1,0:T(8,128)S(1)}, f32[8,128]{1,0:T(8,128)S(1)}, u32[]{:S(2)}, u32[]{:S(2)}) collective-permute-start(f32[8,128]{1,0:T(8,128)S(1)} %get-tuple-element.35.s0), channel_id=1, source_target_pairs={{4,0},{6,2},{0,4},{2,6},{5,1},{7,3},{1,5},{3,7},{12,8},{14,10},{8,... | collective-permute-start | bytes 12296 | tf_op jit(solution)/shard_map/ppermute | solution.py:195
  37.0 1.2 %collective-permute-start.4 = (f32[8,128]{1,0:T(8,128)S(1)}, f32[8,128]{1,0:T(8,128)S(1)}, u32[]{:S(2)}, u32[]{:S(2)}) collective-permute-start(f32[8,128]{1,0:T(8,128)S(1)} %get-tuple-element.35.s0), channel_id=1, source_target_pairs={{2,0},{4,2},{6,4},{0,6},{3,1},{5,3},{7,5},{1,7},{10,8},{12,10},{14... | collective-permute-start | bytes 12296 | tf_op jit(solution)/shard_map/ppermute | solution.py:195
  38.2 0.0 collective-permute-done.6.s3
  38.2 0.7 %collective-permute-done.5.s2 = f32[8,128]{1,0:T(8,128)S(1)} collective-permute-done((f32[8,128]{1,0:T(8,128)S(1)}, f32[8,128]{1,0:T(8,128)S(1)}, u32[]{:S(2)}, u32[]{:S(2)}) %collective-permute-start.5) | collective-permute-done | bytes 4128 | tf_op jit(solution)/shard_map/ppermute | solution.py:195
  38.9 1.7 %collective-permute-done.4.s1 = f32[8,128]{1,0:T(8,128)S(1)} collective-permute-done((f32[8,128]{1,0:T(8,128)S(1)}, f32[8,128]{1,0:T(8,128)S(1)}, u32[]{:S(2)}, u32[]{:S(2)}) %collective-permute-start.4) | collective-permute-done | bytes 4128 | tf_op jit(solution)/shard_map/ppermute | solution.py:195
  40.6 1.7 %all-to-all-done.1.got_ref = f32[128,1,256]{2,1,0:T(1,128)S(1)} async-done(((f32[128,1,256]{2,1,0:T(1,128)}), f32[128,1,256]{2,1,0:T(1,128)S(1)}, u32[]{:S(2)}, u32[]{:S(2)}) %all-to-all-start.1) | async-done | bytes 131104 | tf_op jit(solution)/shard_map/all_to_all | solution.py:225
  42.3 3.4 %shard_map.44 = (f32[136,128]{1,0:T(8,128)S(1)}, f32[136,128]{1,0:T(8,128)S(1)}, f32[136,128]{1,0:T(8,128)S(1)}, f32[136,128]{1,0:T(8,128)S(1)}, f32[8,128]{1,0:T(8,128)S(1)}) custom-call(s32[3]{0:T(128)S(1)} %pad_add_fusion.1.refs_0_.place_ref, bf16[128,128]{1,0:T(8,128)(2,1)S(1)} %get-tuple-element.26.refs_1_.u0, ...), custom_call_target="tpu_custom_call" | custom-call | flops 1073741824 | bytes 1048576 | tf_op jit(solution)/shard_map/pallas_call | solution.py:32
  45.7 0.5 collective-permute-start.7
  46.1 1.8 %collective-permute-start.8 = (f32[136,128]{1,0:T(8,128)S(1)}, f32[136,128]{1,0:T(8,128)S(1)}, u32[]{:S(2)}, u32[]{:S(2)}) collective-permute-start(f32[136,128]{1,0:T(8,128)S(1)} %get-tuple-element.42), channel_id=1, source_target_pairs={{4,0},{6,2},{0,4},{2,6},{5,1},{7,3},{1,5},{3,7},{12,8},{14,10},{8,... | collective-permute-start | bytes 208904 | tf_op jit(solution)/shard_map/ppermute | solution.py:195
  48.0 1.5 %collective-permute-start.9 = (f32[136,128]{1,0:T(8,128)S(1)}, f32[136,128]{1,0:T(8,128)S(1)}, u32[]{:S(2)}, u32[]{:S(2)}) collective-permute-start(f32[136,128]{1,0:T(8,128)S(1)} %get-tuple-element.43), channel_id=1, source_target_pairs={{2,0},{4,2},{6,4},{0,6},{3,1},{5,3},{7,5},{1,7},{10,8},{12,10},{14... | collective-permute-start | bytes 208904 | tf_op jit(solution)/shard_map/ppermute | solution.py:195
  49.5 3.0 %collective-permute-done.7.b1 = f32[136,128]{1,0:T(8,128)S(1)} collective-permute-done((f32[136,128]{1,0:T(8,128)S(1)}, f32[136,128]{1,0:T(8,128)S(1)}, u32[]{:S(2)}, u32[]{:S(2)}) %collective-permute-start.7) | collective-permute-done | bytes 69664 | tf_op jit(solution)/shard_map/ppermute | solution.py:195
  52.5 0.0 collective-permute-done.8.b2
  52.5 0.4 collective-permute-done.9.b3
  52.9 0.0 copy-done.2
  52.9 1.4 %shard_map.45 = (f32[1,1]{1,0:T(1,128)}, f32[128,128]{1,0:T(8,128)}) custom-call(s32[3]{0:T(128)S(1)} %pad_add_fusion.1.refs_0_.place_ref, f32[128,128]{1,0:T(8,128)S(1)} %copy-done.2, f32[8,128]{1,0:T(8,128)S(1)} %get-tuple-element.39.aux_ref, f32[136,128]{1,0:T(8,128)S(1)} %get-tuple-element.40.b0, f32[136,128]{1,0:T(8,128)S(1)} %collective-permute-done.7.b1, ...), custom_call_target="tpu_custom_call" | custom-call | tf_op jit(solution)/shard_map/pallas_call | solution.py:32
  (3 shorter events, 0.0 us)
Async XLA Ops:
  0.6 15.5 %copy-start = (s32[16384]{0:T(1024)S(1)}, s32[16384]{0:T(1024)}, u32[]{:S(2)}) copy-start(s32[16384]{0:T(1024)} %param.3) | copy-start | bytes 196612
  0.6 0.9 %copy-start.1 = (f32[128,128]{1,0:T(8,128)S(1)}, f32[128,128]{1,0:T(8,128)}, u32[]{:S(2)}) copy-start(f32[128,128]{1,0:T(8,128)} %x_ref.3) | copy-start | bytes 196612
  2.5 18.7 %all-to-all-start = ((bf16[16,128,128]{2,1,0:T(8,128)(2,1)}), bf16[16,128,128]{2,1,0:T(8,128)(2,1)S(1)}, u32[]{:S(2)}, u32[]{:S(2)}) async-start(bf16[16,128,128]{2,1,0:T(8,128)(2,1)} %get-tuple-element.24), calls=%async_computation | async-start | bytes 1048576 | tf_op jit(solution)/shard_map/all_to_all | solution.py:204
  9.6 6.6 %collective-permute-start.2 = (bf16[128,128]{1,0:T(8,128)(2,1)S(1)}, bf16[128,128]{1,0:T(8,128)(2,1)S(1)}, u32[]{:S(2)}, u32[]{:S(2)}) collective-permute-start(bf16[128,128]{1,0:T(8,128)(2,1)S(1)} %get-tuple-element.26.refs_1_.u0), channel_id=1, source_target_pairs={{6,0},{0,2},{2,4},{4,6},{7,1},{1,3},{3,5},{5,7},{14,8},{8,10},{10,... | collective-permute-start | bytes 98312 | tf_op jit(solution)/shard_map/ppermute | solution.py:195
  11.6 5.8 %collective-permute-start.1 = (bf16[128,128]{1,0:T(8,128)(2,1)S(1)}, bf16[128,128]{1,0:T(8,128)(2,1)S(1)}, u32[]{:S(2)}, u32[]{:S(2)}) collective-permute-start(bf16[128,128]{1,0:T(8,128)(2,1)S(1)} %get-tuple-element.26.refs_1_.u0), channel_id=1, source_target_pairs={{4,0},{6,2},{0,4},{2,6},{5,1},{7,3},{1,5},{3,7},{12,8},{14,10},{8,... | collective-permute-start | bytes 98312 | tf_op jit(solution)/shard_map/ppermute | solution.py:195
  15.2 3.9 %collective-permute-start = (bf16[128,128]{1,0:T(8,128)(2,1)S(1)}, bf16[128,128]{1,0:T(8,128)(2,1)S(1)}, u32[]{:S(2)}, u32[]{:S(2)}) collective-permute-start(bf16[128,128]{1,0:T(8,128)(2,1)S(1)} %get-tuple-element.26.refs_1_.u0), channel_id=1, source_target_pairs={{2,0},{4,2},{6,4},{0,6},{3,1},{5,3},{7,5},{1,7},{10,8},{12,10},{14... | collective-permute-start | bytes 98312 | tf_op jit(solution)/shard_map/ppermute | solution.py:195
  21.1 1.9 %collective-permute-start.3 = (bf16[16,128,128]{2,1,0:T(8,128)(2,1)S(1)}, bf16[16,128,128]{2,1,0:T(8,128)(2,1)S(1)}, u32[]{:S(2)}, u32[]{:S(2)}) collective-permute-start(bf16[16,128,128]{2,1,0:T(8,128)(2,1)S(1)} %all-to-all-done), channel_id=1, source_target_pairs={{0,1},{1,0},{2,3},{3,2},{4,5},{5,4},{6,7},{7,6},{8,9},{9,8},{10,11... | collective-permute-start | bytes 1572872 | tf_op jit(solution)/shard_map/ppermute | solution.py:211
  25.3 17.0 %all-to-all-start.1 = ((f32[128,1,256]{2,1,0:T(1,128)}), f32[128,1,256]{2,1,0:T(1,128)S(1)}, u32[]{:S(2)}, u32[]{:S(2)}) async-start(f32[128,1,256]{2,1,0:T(1,128)} %get-tuple-element.32), calls=%async_computation.1 | async-start | bytes 262144 | tf_op jit(solution)/shard_map/all_to_all | solution.py:225
  32.6 20.2 %copy-start.2 = (f32[128,128]{1,0:T(8,128)S(1)}, f32[128,128]{1,0:T(8,128)}, u32[]{:S(2)}) copy-start(f32[128,128]{1,0:T(8,128)} %x_ref.3) | copy-start | bytes 196612
  32.6 5.6 %collective-permute-start.6 = (f32[8,128]{1,0:T(8,128)S(1)}, f32[8,128]{1,0:T(8,128)S(1)}, u32[]{:S(2)}, u32[]{:S(2)}) collective-permute-start(f32[8,128]{1,0:T(8,128)S(1)} %get-tuple-element.35.s0), channel_id=1, source_target_pairs={{6,0},{0,2},{2,4},{4,6},{7,1},{1,3},{3,5},{5,7},{14,8},{8,10},{10,... | collective-permute-start | bytes 12296 | tf_op jit(solution)/shard_map/ppermute | solution.py:195
  33.8 5.1 %collective-permute-start.5 = (f32[8,128]{1,0:T(8,128)S(1)}, f32[8,128]{1,0:T(8,128)S(1)}, u32[]{:S(2)}, u32[]{:S(2)}) collective-permute-start(f32[8,128]{1,0:T(8,128)S(1)} %get-tuple-element.35.s0), channel_id=1, source_target_pairs={{4,0},{6,2},{0,4},{2,6},{5,1},{7,3},{1,5},{3,7},{12,8},{14,10},{8,... | collective-permute-start | bytes 12296 | tf_op jit(solution)/shard_map/ppermute | solution.py:195
  37.0 3.6 %collective-permute-start.4 = (f32[8,128]{1,0:T(8,128)S(1)}, f32[8,128]{1,0:T(8,128)S(1)}, u32[]{:S(2)}, u32[]{:S(2)}) collective-permute-start(f32[8,128]{1,0:T(8,128)S(1)} %get-tuple-element.35.s0), channel_id=1, source_target_pairs={{2,0},{4,2},{6,4},{0,6},{3,1},{5,3},{7,5},{1,7},{10,8},{12,10},{14... | collective-permute-start | bytes 12296 | tf_op jit(solution)/shard_map/ppermute | solution.py:195
  45.7 6.8 %collective-permute-start.7 = (f32[136,128]{1,0:T(8,128)S(1)}, f32[136,128]{1,0:T(8,128)S(1)}, u32[]{:S(2)}, u32[]{:S(2)}) collective-permute-start(f32[136,128]{1,0:T(8,128)S(1)} %get-tuple-element.41), channel_id=1, source_target_pairs={{6,0},{0,2},{2,4},{4,6},{7,1},{1,3},{3,5},{5,7},{14,8},{8,10},{10,... | collective-permute-start | bytes 208904 | tf_op jit(solution)/shard_map/ppermute | solution.py:195
  46.1 6.4 %collective-permute-start.8 = (f32[136,128]{1,0:T(8,128)S(1)}, f32[136,128]{1,0:T(8,128)S(1)}, u32[]{:S(2)}, u32[]{:S(2)}) collective-permute-start(f32[136,128]{1,0:T(8,128)S(1)} %get-tuple-element.42), channel_id=1, source_target_pairs={{4,0},{6,2},{0,4},{2,6},{5,1},{7,3},{1,5},{3,7},{12,8},{14,10},{8,... | collective-permute-start | bytes 208904 | tf_op jit(solution)/shard_map/ppermute | solution.py:195
  48.0 4.9 %collective-permute-start.9 = (f32[136,128]{1,0:T(8,128)S(1)}, f32[136,128]{1,0:T(8,128)S(1)}, u32[]{:S(2)}, u32[]{:S(2)}) collective-permute-start(f32[136,128]{1,0:T(8,128)S(1)} %get-tuple-element.43), channel_id=1, source_target_pairs={{2,0},{4,2},{6,4},{0,6},{3,1},{5,3},{7,5},{1,7},{10,8},{12,10},{14... | collective-permute-start | bytes 208904 | tf_op jit(solution)/shard_map/ppermute | solution.py:195

commit v3 on v2

v3 whole, which is shorter than its diff:
```python
import functools
import math

import jax
import jax.numpy as jnp
from jax import lax
from jax.experimental import pallas as pl
from jax.experimental.pallas import tpu as pltpu
from jax.sharding import Mesh, PartitionSpec as P

EPS = 1e-06
INV_TEMP = 10.0
SCALE = INV_TEMP * math.log2(math.e)

ROWS = 128
NXY = 16
NZ = 4
NCO = 2
NDEV = NXY * NZ * NCO
VIEWS = NDEV * ROWS
XY = ("y", "xh", "xl")
ALL = ("y", "xh", "xl", "z", "co")
CHUNK = 256
F32 = jnp.float32
BF16 = jnp.bfloat16
VMEM = pl.BlockSpec(memory_space=pltpu.VMEM)
SMEM = pl.BlockSpec(memory_space=pltpu.SMEM)


def call(body, outs, scratch=(), flops=0, nbytes=0, exps=0):
    def run(*args):
        return pl.pallas_call(
            body,
            out_shape=outs,
            in_specs=[SMEM if a.dtype == jnp.int32 and a.ndim == 1 else VMEM for a in args],
            out_specs=[VMEM] * len(outs),
            scratch_shapes=list(scratch),
            compiler_params=pltpu.CompilerParams(vmem_limit_bytes=16 * 2**20),
            cost_estimate=pl.CostEstimate(flops=flops, bytes_accessed=nbytes, transcendentals=exps),
        )(*args)

    return run


def sds(shape, dtype=F32):
    return jax.ShapeDtypeStruct(shape, dtype)


def dot_nt(a, b):
    return lax.dot_general(a, b, (((1,), (1,)), ((), ())), preferred_element_type=F32)


def dot_nn(a, b):
    return lax.dot_general(a, b, (((1,), (0,)), ((), ())), preferred_element_type=F32)


def down_rows(row):
    return jnp.transpose(jnp.broadcast_to(row, (ROWS, ROWS)))


def norm_kernel(x_ref, u_ref, copies_ref):
    x = x_ref[...]
    radius = jnp.sqrt(jnp.sum(x * x, axis=1, keepdims=True) + EPS)
    unit = (x / radius).astype(BF16)
    u_ref[...] = unit
    copies_ref[...] = jnp.broadcast_to(unit[None], (NXY, ROWS, ROWS))


def expo(s):
    return jnp.exp2(s * SCALE)


def local_mates(mates, z, half):
    here = (((mates >> 8) & 3) == z) & (((mates >> 7) & 1) == half)
    return jnp.where(here, ((mates >> 10) << 7) | (mates & 127), -1)


def sums_kernel(own_half, *refs):
    place_ref, u0, u1, u2, u3, c_ref, mate_ref = refs[:7]
    z, co, xy = place_ref[0], place_ref[1], place_ref[2]
    half = co if own_half else 1 - co
    mates = mate_ref[...]
    here = local_mates(mates, z, half)
    width = 2 * ROWS
    down = lax.broadcasted_iota(jnp.int32, (8, width), 0)
    sums, pos = [], jnp.zeros((8, width), F32)
    for g in range(0, NZ, 2):
        u = jnp.concatenate([ref[...] for ref in (u0, u1, u2, u3)[g : g + 2]], axis=0)
        mate = jnp.broadcast_to(jnp.concatenate([here[g : g + 1], here[g + 1 : g + 2]], axis=1), (8, width))
        block = mate >> 7
        total = jnp.zeros((8, width), F32)
        kept = [jnp.zeros((8, width), F32)] * (ROWS // 8)
        for c in range(0, c_ref.shape[0], CHUNK):
            s = dot_nt(c_ref[c : c + CHUNK], u)
            for k in range(0, CHUNK, 8):
                q = k % ROWS // 8
                kept[q] = jnp.where(block == (c + k) // ROWS, s[k : k + 8], kept[q])
            e = expo(s)
            if own_half and g == 0:
                col = lax.broadcasted_iota(jnp.int32, (CHUNK, ROWS), 0) + (c - xy * ROWS)
                row = lax.broadcasted_iota(jnp.int32, (CHUNK, ROWS), 1)
                e = jnp.concatenate([jnp.where(col == row, 0.0, e[:, :ROWS]), e[:, ROWS:]], axis=1)
            for k in range(0, CHUNK, 8):
                total = total + e[k : k + 8]
        for q, s in enumerate(kept):
            pos = pos + jnp.where((mate & 127) == down + 8 * q, s, 0.0)
        sums.append(jnp.sum(total, axis=0, keepdims=True))
    sums = jnp.concatenate(sums, axis=1)
    pos = jnp.sum(pos, axis=0, keepdims=True) * INV_TEMP
    rows = [sums[:, r * ROWS : (r + 1) * ROWS] for r in range(NZ)]
    rows.append(pos[:, :ROWS] + pos[:, ROWS:])
    if own_half:
        out_ref = refs[7]
        for q, row in enumerate(rows):
            out_ref[q : q + 1] = row
        out_ref[5:8] = jnp.zeros((3, ROWS), F32)
        return
    in_ref, send_ref = refs[7:]
    rows = [row + in_ref[q : q + 1] for q, row in enumerate(rows)]
    planes = []
    for k in range(NZ):
        r = lax.rem(k - z + NZ, NZ)
        row = rows[0]
        for q in range(1, NZ):
            row = jnp.where(r == q, rows[q], row)
        planes.append(row)
    pos = rows[NZ]
    high = pos.astype(BF16).astype(F32)
    for k in range(NZ):
        q = [planes[(k + r) % NZ] for r in range(NZ)]
        top = jnp.concatenate([q[0], q[1], high], axis=1)
        low = jnp.concatenate([q[2], q[3], pos - high], axis=1)
        piece = jnp.concatenate([top, low], axis=0).astype(BF16)
        for xy_to in range(NXY):
            for co_to in range(NCO):
                send_ref[xy_to * 8 + k * 2 + co_to] = piece


def grads_kernel(blocks, *refs):
    n = len(blocks)
    first = 0 not in blocks
    place_ref, own_ref, other_ref, mate_ref = refs[:4]
    u_refs = refs[4 : 4 + n]
    z, co, xy = place_ref[0], place_ref[1], place_ref[2]
    got_ref = refs[4 + n]
    if first:
        out_refs = refs[5 + n : 5 + 2 * n]
        inv_ref, aux_ref = refs[5 + 2 * n :]
        for k in range(NXY):
            for c in range(NCO):
                got = [got_ref[k * 8 + q * 2 + c, :, 0:ROWS].astype(F32) for q in range(NZ)]
                total = got[0] + got[1] + (got[2] + got[3])
                inv_ref[c, :, k * ROWS : (k + 1) * ROWS] = 1.0 / total[0:1]
        got = [got_ref[xy * 8 + q * 2 + co, :, 0 : 2 * ROWS].astype(F32) for q in range(NZ)]
        total = got[0] + got[1] + (got[2] + got[3])
        for r in range(NZ):
            part = total[r // 2 : r // 2 + 1, r % 2 * ROWS : (r % 2 + 1) * ROWS]
            aux_ref[r : r + 1] = 1.0 / part
        aux_ref[NZ:] = jnp.zeros((8 - NZ, ROWS), F32)
    else:
        inv_ref, aux_ref, *out_refs, loss_ref = refs[5 + n :]
        logs = jnp.zeros((2, 2 * ROWS), F32)
        pos = jnp.zeros((2, ROWS), F32)
        for k in range(NXY):
            for c in range(NCO):
                got = [got_ref[k * 8 + q * 2 + c].astype(F32) for q in range(NZ)]
                got = got[0] + got[1] + (got[2] + got[3])
                pos = pos + got[:, 2 * ROWS :]
                logs = logs + jnp.log(got[:, : 2 * ROWS])
        pos = jnp.sum(pos, axis=0, keepdims=True)
        parts = [logs[r // 2 : r // 2 + 1, r % 2 * ROWS : (r % 2 + 1) * ROWS] for r in range(NZ)]
        loss = -pos
        for k in range(NZ):
            r = lax.rem(k - z + NZ, NZ)
            row = parts[0]
            for q in range(1, NZ):
                row = jnp.where(r == q, parts[q], row)
            loss = loss + row
        loss_ref[...] = jnp.sum(loss, axis=1, keepdims=True) / VIEWS
    inv_row = jnp.concatenate([down_rows(aux_ref[r : r + 1]) for r in blocks], axis=0)
    mates = mate_ref[...]
    u = jnp.concatenate([ref[...] for ref in u_refs], axis=0)
    lane = lax.broadcasted_iota(jnp.int32, (n * ROWS, ROWS), 1)
    total = jnp.zeros((n * ROWS, ROWS), F32)
    for h, c_ref in enumerate((own_ref, other_ref)):
        half = co if h == 0 else 1 - co
        local = local_mates(mates, z, half)
        mate = jnp.concatenate([down_rows(local[r : r + 1]) for r in blocks], axis=0)
        for c in range(0, c_ref.shape[0], CHUNK):
            e = expo(dot_nt(u, c_ref[c : c + CHUNK]))
            if h == 0 and not first:
                col = lax.broadcasted_iota(jnp.int32, e.shape, 1) + (c - xy * ROWS)
                row = lax.broadcasted_iota(jnp.int32, e.shape, 0)
                e = jnp.where(col == row, 0.0, e)
            weight = []
            for k in range(0, CHUNK, ROWS):
                w = e[:, k : k + ROWS] * (inv_row + inv_ref[half, :, c + k : c + k + ROWS])
                w = w - jnp.where(mate == lane + (c + k), 2.0, 0.0)
                weight.append(w.astype(BF16))
            total = total + dot_nn(jnp.concatenate(weight, axis=1), c_ref[c : c + CHUNK])
    for q, out_ref in enumerate(out_refs):
        out_ref[...] = total[q * ROWS : (q + 1) * ROWS]


def final_kernel(x_ref, b0, b1, b2, b3, grad_ref):
    x = x_ref[...]
    radius = jnp.sqrt(jnp.sum(x * x, axis=1, keepdims=True) + EPS)
    unit = x / radius
    d = INV_TEMP * (b0[...] + b1[...] + b2[...] + b3[...])
    grad_ref[...] = (d - unit * jnp.sum(unit * d, axis=1, keepdims=True)) / radius


def shift(x, by):
    return lax.ppermute(x, "z", [((k + by) % NZ, k) for k in range(NZ)])


def body(proj, partner):
    y, xh, xl = (lax.axis_index(a) for a in XY)
    z, co = lax.axis_index("z"), lax.axis_index("co")
    xy = (y * 2 + xh) * 2 + xl
    place = jnp.stack([z, co, xy]).astype(jnp.int32)
    unit, copies = call(norm_kernel, [sds((ROWS, ROWS), BF16), sds((NXY, ROWS, ROWS), BF16)])(proj)
    plane = lax.all_to_all(copies, XY, 0, 0, tiled=True)
    rows = [unit] + [shift(unit, r) for r in range(1, NZ)]
    mates = partner.reshape(NXY, NZ, NCO, ROWS)
    mates = lax.dynamic_slice(mates, (xy, 0, co, 0), (1, NZ, 1, ROWS)).reshape(NZ, ROWS)
    mates = jnp.concatenate([mates, mates])
    mates = lax.dynamic_slice_in_dim(mates, z, NZ, 0)
    plane, mates, *rows = lax.optimization_barrier((plane, mates, *rows))
    other = lax.ppermute(plane, "co", [(0, 1), (1, 0)])
    cols = NXY * ROWS
    plane = plane.reshape(cols, ROWS)
    other = other.reshape(cols, ROWS)
    n = NZ * ROWS
    work = dict(flops=2 * n * cols * ROWS, nbytes=2**20, exps=n * cols)
    first = call(
        functools.partial(sums_kernel, True), [sds((8, ROWS))], **work
    )(place, *rows, plane, mates)
    (send,) = call(
        functools.partial(sums_kernel, False), [sds((NDEV, 2, 3 * ROWS), BF16)], **work
    )(place, *rows, other, mates, *first)
    got = lax.all_to_all(send, ALL, 0, 0, tiled=True)
    work = dict(flops=6 * n * cols * ROWS, nbytes=2**20, exps=2 * n * cols)
    block = sds((ROWS, ROWS))
    held = (place, plane, other, mates)
    b1, b2, b3, *inv = call(
        functools.partial(grads_kernel, (1, 2, 3)),
        [block] * 3 + [sds((NCO, 1, cols)), sds((8, ROWS))],
        **work,
    )(*held, *rows[1:], got)
    b0, loss = call(functools.partial(grads_kernel, (0,)), [block, sds((1, 1))], **work)(*held, rows[0], got, *inv)
    b = [b0, shift(b1, -1), shift(b2, -2), shift(b3, -3)]
    (grad,) = call(final_kernel, [sds((ROWS, ROWS))])(proj, *b)
    return loss.reshape(()), grad


def solution(mesh):
    fine = Mesh(mesh.devices.reshape(4, 2, 2, 4, 2), ALL)
    return jax.shard_map(
        body,
        mesh=fine,
        in_specs=(P(ALL, None), P()),
        out_specs=(P(), P(ALL, None)),
        check_vma=False,
    )
```

time: 54.5 us -> 52.8 us (0.969)
  blocking collectives: 0 us -> 17.4 us
  starting transfers between devices: 30.4 us -> 17.4 us
  waiting for transfers between devices: 12.5 us -> 6.46 us
    all_to_all x0 -> x1, blocking collectives: none -> 17.4 us  [body(): got = lax.all_to_all(send, ALL, 0, 0, tiled=True)]
    all_to_all x1 -> x0, starting transfers between devices: 7.34 us -> none  [body(): got = lax.all_to_all(send, ALL, 0, 0, tiled=True)]
    ppermute x9 -> x6, starting transfers between devices: 15.9 us -> 10.3 us  [shift(): return lax.ppermute(x, 'z', [((k + by) % NZ, k) for k in range(NZ)])]
    ppermute x9 -> x6, waiting for transfers between devices: 8.68 us -> 4.1 us  [shift(): return lax.ppermute(x, 'z', [((k + by) % NZ, k) for k in range(NZ)])]
    all_to_all x1 -> x0, waiting for transfers between devices: 1.65 us -> none  [body(): got = lax.all_to_all(send, ALL, 0, 0, tiled=True)]
    pallas_call x5 -> x6, Pallas kernels: 9.68 us -> 9.59 us  [run(): pl.pallas_call(body, out_shape=outs, in_specs=[SMEM if a.dtype == jnp.int...]
  transfers between devices with their start and end apart: 12 -> 8, of which waited for: 9 -> 6; matrix products, arithmetic and copies ran while one was open for 0% -> 0% of each run, Pallas kernels for 3% -> 7%
where the time goes in v3:
time: 52.8 us; the launch traced here: 52.5 us
  starting transfers between devices  17.4 us (33%)
  blocking collectives  17.4 us (33%)
  Pallas kernels  9.59 us (18%)
  waiting for transfers between devices  6.46 us (12%)
  local copies, waits for them, and re-layouts  0.9 us (2%)
  between operations  0.71 us (1%)
    all_to_all x1, blocking collectives, body(): got = lax.all_to_all(send, ALL, 0, 0, tiled=True)  17.4 us
    ppermute x6, starting transfers between devices, shift(): return lax.ppermute(x, 'z', [((k + by) % NZ, k) for k in range(NZ)])  10.3 us
    pallas_call x6, Pallas kernels, run(): pl.pallas_call(body, out_shape=outs, in_specs=[SMEM if a.dtype == jnp.int...  9.59 us
    all_to_all x1, starting transfers between devices, body(): plane = lax.all_to_all(copies, XY, 0, 0, tiled=True)  7.12 us
    ppermute x6, waiting for transfers between devices, shift(): return lax.ppermute(x, 'z', [((k + by) % NZ, k) for k in range(NZ)])  4.1 us
    all_to_all x1, waiting for transfers between devices, body(): plane = lax.all_to_all(copies, XY, 0, 0, tiled=True)  2.05 us
  transfers between devices with their start and end apart: 8, of which 6 were waited for; matrix products, arithmetic and copies ran while one was open for 0% of the time, Pallas kernels for 7%

profile of v3, /device:TPU:0, one launch (start us, length us, event | category | flops | bytes accessed | tf_op | source)
XLA Modules:
  0.0 52.5 jit_solution(13824004194753888697)
XLA Ops:
  0.6 0.0 copy-start
  0.6 0.0 copy-start.1
  0.7 0.9 %copy-done.1 = f32[128,128]{1,0:T(8,128)S(1)} copy-done((f32[128,128]{1,0:T(8,128)S(1)}, f32[128,128]{1,0:T(8,128)}, u32[]{:S(2)}) %copy-start.1) | copy-done | bytes 65560
  1.5 0.9 %shard_map.41 = (bf16[128,128]{1,0:T(8,128)(2,1)S(1)}, bf16[16,128,128]{2,1,0:T(8,128)(2,1)}) custom-call(f32[128,128]{1,0:T(8,128)S(1)} %copy-done.1), custom_call_target="tpu_custom_call" | custom-call | tf_op jit(solution)/shard_map/pallas_call | solution.py:32
  2.5 7.1 %all-to-all-start = ((bf16[16,128,128]{2,1,0:T(8,128)(2,1)}), bf16[16,128,128]{2,1,0:T(8,128)(2,1)S(1)}, u32[]{:S(2)}, u32[]{:S(2)}) async-start(bf16[16,128,128]{2,1,0:T(8,128)(2,1)} %get-tuple-element.17), calls=%async_computation | async-start | bytes 1048576 | tf_op jit(solution)/shard_map/all_to_all | solution.py:223
  9.6 2.0 %collective-permute-start.2 = (bf16[128,128]{1,0:T(8,128)(2,1)S(1)}, bf16[128,128]{1,0:T(8,128)(2,1)S(1)}, u32[]{:S(2)}, u32[]{:S(2)}) collective-permute-start(bf16[128,128]{1,0:T(8,128)(2,1)S(1)} %get-tuple-element.21.refs_1_.refs_4_), channel_id=1, source_target_pairs={{6,0},{0,2},{2,4},{4,6},{7,1},{1,3},{3,5},{5,7},{14,8},{8,10},{10,... | collective-permute-start | bytes 98312 | tf_op jit(solution)/shard_map/ppermute | solution.py:214
  11.6 3.6 %collective-permute-start.1 = (bf16[128,128]{1,0:T(8,128)(2,1)S(1)}, bf16[128,128]{1,0:T(8,128)(2,1)S(1)}, u32[]{:S(2)}, u32[]{:S(2)}) collective-permute-start(bf16[128,128]{1,0:T(8,128)(2,1)S(1)} %get-tuple-element.21.refs_1_.refs_4_), channel_id=1, source_target_pairs={{4,0},{6,2},{0,4},{2,6},{5,1},{7,3},{1,5},{3,7},{12,8},{14,10},{8,... | collective-permute-start | bytes 98312 | tf_op jit(solution)/shard_map/ppermute | solution.py:214
  15.2 1.0 %collective-permute-start = (bf16[128,128]{1,0:T(8,128)(2,1)S(1)}, bf16[128,128]{1,0:T(8,128)(2,1)S(1)}, u32[]{:S(2)}, u32[]{:S(2)}) collective-permute-start(bf16[128,128]{1,0:T(8,128)(2,1)S(1)} %get-tuple-element.21.refs_1_.refs_4_), channel_id=1, source_target_pairs={{2,0},{4,2},{6,4},{0,6},{3,1},{5,3},{7,5},{1,7},{10,8},{12,10},{14... | collective-permute-start | bytes 98312 | tf_op jit(solution)/shard_map/ppermute | solution.py:214
  16.2 0.0 copy-done
  16.2 0.0 collective-permute-done.2.refs_4_.refs_6_
  16.2 1.2 %collective-permute-done.1.refs_3_.refs_5_ = bf16[128,128]{1,0:T(8,128)(2,1)S(1)} collective-permute-done((bf16[128,128]{1,0:T(8,128)(2,1)S(1)}, bf16[128,128]{1,0:T(8,128)(2,1)S(1)}, u32[]{:S(2)}, u32[]{:S(2)}) %collective-permute-start.1) | collective-permute-done | bytes 32800 | tf_op jit(solution)/shard_map/ppermute | solution.py:214
  17.4 1.7 %collective-permute-done.refs_2_.refs_4_ = bf16[128,128]{1,0:T(8,128)(2,1)S(1)} collective-permute-done((bf16[128,128]{1,0:T(8,128)(2,1)S(1)}, bf16[128,128]{1,0:T(8,128)(2,1)S(1)}, u32[]{:S(2)}, u32[]{:S(2)}) %collective-permute-start) | collective-permute-done | bytes 32800 | tf_op jit(solution)/shard_map/ppermute | solution.py:214
  19.1 2.0 %all-to-all-done = bf16[16,128,128]{2,1,0:T(8,128)(2,1)S(1)} async-done(((bf16[16,128,128]{2,1,0:T(8,128)(2,1)}), bf16[16,128,128]{2,1,0:T(8,128)(2,1)S(1)}, u32[]{:S(2)}, u32[]{:S(2)}) %all-to-all-start) | async-done | bytes 524320 | tf_op jit(solution)/shard_map/all_to_all | solution.py:223
  21.1 0.0 collective-permute-start.3
  21.1 0.1 pad_add_fusion.1.refs_0_
  21.2 1.5 %shard_map.42.refs_7_ = f32[8,128]{1,0:T(8,128)S(1)} custom-call(s32[3]{0:T(128)S(1)} %pad_add_fusion.1.refs_0_, bf16[128,128]{1,0:T(8,128)(2,1)S(1)} %get-tuple-element.21.refs_1_.refs_4_, bf16[128,128]{1,0:T(8,128)(2,1)S(1)} %collective-permute-done.refs_2_.refs_4_, bf16[128,128]{1,0:T(8,128)(2,1)S(1)} %collective-permute-done.1.refs_3_.refs_5_, ...), custom_call_target="tpu_custom_call" | custom-call | flops 268435456 | bytes 1048576 | tf_op jit(solution)/shard_map/pallas_call | solution.py:32
  22.7 0.3 collective-permute-done.3
  23.0 1.5 %shard_map.43 = bf16[128,2,384]{2,1,0:T(2,128)(2,1)S(1)} custom-call(s32[3]{0:T(128)S(1)} %pad_add_fusion.1.refs_0_, bf16[128,128]{1,0:T(8,128)(2,1)S(1)} %get-tuple-element.21.refs_1_.refs_4_, bf16[128,128]{1,0:T(8,128)(2,1)S(1)} %collective-permute-done.refs_2_.refs_4_, bf16[128,128]{1,0:T(8,128)(2,1)S(1)} %collective-permute-done.1.refs_3_.refs_5_, ...), custom_call_target="tpu_custom_call" | custom-call | flops 268435456 | bytes 1048576 | tf_op jit(solution)/shard_map/pallas_call | solution.py:32
  24.5 17.4 %all_to_all.10.refs_7_.refs_5_ = bf16[128,2,384]{2,1,0:T(2,128)(2,1)S(1)} all-to-all(bf16[128,2,384]{2,1,0:T(2,128)(2,1)S(1)} %shard_map.43), channel_id=1, replica_groups=mesh['y'=4,'xh'=2,'xl'=2,'z'=4,'co'=2] {'y','xh','xl','z','co'}, dimensions={0} | all-to-all | bytes 393216 | tf_op jit(solution)/shard_map/all_to_all | solution.py:242
  41.9 2.7 %shard_map.44 = (f32[128,128]{1,0:T(8,128)S(1)}, f32[128,128]{1,0:T(8,128)S(1)}, f32[128,128]{1,0:T(8,128)S(1)}, f32[2,1,2048]{2,1,0:T(1,128)S(1)}, f32[8,128]{1,0:T(8,128)S(1)}) custom-call(s32[3]{0:T(128)S(1)} %pad_add_fusion.1.refs_0_, bf16[2048,128]{1,0:T(8,128)(2,1)S(1)} %bitcast.10, bf16[2048,128]{1,0:T(8,128)(2,1)S(1)} %bitcast.13, ...), custom_call_target="tpu_custom_call" | custom-call | flops 805306368 | bytes 1048576 | tf_op jit(solution)/shard_map/pallas_call | solution.py:32
  44.6 0.5 collective-permute-start.4
  45.1 1.7 %collective-permute-start.5 = (f32[128,128]{1,0:T(8,128)S(1)}, f32[128,128]{1,0:T(8,128)S(1)}, u32[]{:S(2)}, u32[]{:S(2)}) collective-permute-start(f32[128,128]{1,0:T(8,128)S(1)} %get-tuple-element.30), channel_id=1, source_target_pairs={{4,0},{6,2},{0,4},{2,6},{5,1},{7,3},{1,5},{3,7},{12,8},{14,10},{8,... | collective-permute-start | bytes 196616 | tf_op jit(solution)/shard_map/ppermute | solution.py:214
  46.8 1.5 %collective-permute-start.6 = (f32[128,128]{1,0:T(8,128)S(1)}, f32[128,128]{1,0:T(8,128)S(1)}, u32[]{:S(2)}, u32[]{:S(2)}) collective-permute-start(f32[128,128]{1,0:T(8,128)S(1)} %get-tuple-element.31), channel_id=1, source_target_pairs={{2,0},{4,2},{6,4},{0,6},{3,1},{5,3},{7,5},{1,7},{10,8},{12,10},{14... | collective-permute-start | bytes 196616 | tf_op jit(solution)/shard_map/ppermute | solution.py:214
  48.3 0.0 copy-start.2
  48.3 2.1 %shard_map.45 = (f32[128,128]{1,0:T(8,128)S(1)}, f32[1,1]{1,0:T(1,128)}) custom-call(s32[3]{0:T(128)S(1)} %pad_add_fusion.1.refs_0_, bf16[2048,128]{1,0:T(8,128)(2,1)S(1)} %bitcast.11, bf16[2048,128]{1,0:T(8,128)(2,1)S(1)} %bitcast.14, s32[4,128]{1,0:T(4,128)S(1)} %constant_dynamic-slice_fusion.refs_6_.refs_3_, ...), custom_call_target="tpu_custom_call" | custom-call | flops 805306368 | bytes 1048576 | tf_op jit(solution)/shard_map/pallas_call | solution.py:32
  50.4 0.7 %collective-permute-done.4.b1 = f32[128,128]{1,0:T(8,128)S(1)} collective-permute-done((f32[128,128]{1,0:T(8,128)S(1)}, f32[128,128]{1,0:T(8,128)S(1)}, u32[]{:S(2)}, u32[]{:S(2)}) %collective-permute-start.4) | collective-permute-done | bytes 65568 | tf_op jit(solution)/shard_map/ppermute | solution.py:214
  51.1 0.0 collective-permute-done.5.b2
  51.1 0.5 %collective-permute-done.6.b3 = f32[128,128]{1,0:T(8,128)S(1)} collective-permute-done((f32[128,128]{1,0:T(8,128)S(1)}, f32[128,128]{1,0:T(8,128)S(1)}, u32[]{:S(2)}, u32[]{:S(2)}) %collective-permute-start.6) | collective-permute-done | bytes 65568 | tf_op jit(solution)/shard_map/ppermute | solution.py:214
  51.7 0.0 copy-done.2
  51.7 0.8 %shard_map.46 = f32[128,128]{1,0:T(8,128)} custom-call(f32[128,128]{1,0:T(8,128)S(1)} %copy-done.2, f32[128,128]{1,0:T(8,128)S(1)} %get-tuple-element.28.b0, f32[128,128]{1,0:T(8,128)S(1)} %collective-permute-done.4.b1, f32[128,128]{1,0:T(8,128)S(1)} %collective-permute-done.5.b2, f32[128,128]{1,0:T(8,128)S(1)} %collective-permute-done.6.b3), custom_call_target="tpu_custom_call" | custom-call | tf_op jit(solution)/shard_map/pallas_call | solution.py:32
  (3 shorter events, 0.0 us)
Async XLA Ops:
  0.6 15.5 %copy-start = (s32[16384]{0:T(1024)S(1)}, s32[16384]{0:T(1024)}, u32[]{:S(2)}) copy-start(s32[16384]{0:T(1024)} %param.3) | copy-start | bytes 196612
  0.6 0.9 %copy-start.1 = (f32[128,128]{1,0:T(8,128)S(1)}, f32[128,128]{1,0:T(8,128)}, u32[]{:S(2)}) copy-start(f32[128,128]{1,0:T(8,128)} %x_ref.3) | copy-start | bytes 196612
  2.5 18.7 %all-to-all-start = ((bf16[16,128,128]{2,1,0:T(8,128)(2,1)}), bf16[16,128,128]{2,1,0:T(8,128)(2,1)S(1)}, u32[]{:S(2)}, u32[]{:S(2)}) async-start(bf16[16,128,128]{2,1,0:T(8,128)(2,1)} %get-tuple-element.17), calls=%async_computation | async-start | bytes 1048576 | tf_op jit(solution)/shard_map/all_to_all | solution.py:223
  9.6 6.6 %collective-permute-start.2 = (bf16[128,128]{1,0:T(8,128)(2,1)S(1)}, bf16[128,128]{1,0:T(8,128)(2,1)S(1)}, u32[]{:S(2)}, u32[]{:S(2)}) collective-permute-start(bf16[128,128]{1,0:T(8,128)(2,1)S(1)} %get-tuple-element.21.refs_1_.refs_4_), channel_id=1, source_target_pairs={{6,0},{0,2},{2,4},{4,6},{7,1},{1,3},{3,5},{5,7},{14,8},{8,10},{10,... | collective-permute-start | bytes 98312 | tf_op jit(solution)/shard_map/ppermute | solution.py:214
  11.6 5.8 %collective-permute-start.1 = (bf16[128,128]{1,0:T(8,128)(2,1)S(1)}, bf16[128,128]{1,0:T(8,128)(2,1)S(1)}, u32[]{:S(2)}, u32[]{:S(2)}) collective-permute-start(bf16[128,128]{1,0:T(8,128)(2,1)S(1)} %get-tuple-element.21.refs_1_.refs_4_), channel_id=1, source_target_pairs={{4,0},{6,2},{0,4},{2,6},{5,1},{7,3},{1,5},{3,7},{12,8},{14,10},{8,... | collective-permute-start | bytes 98312 | tf_op jit(solution)/shard_map/ppermute | solution.py:214
  15.2 3.9 %collective-permute-start = (bf16[128,128]{1,0:T(8,128)(2,1)S(1)}, bf16[128,128]{1,0:T(8,128)(2,1)S(1)}, u32[]{:S(2)}, u32[]{:S(2)}) collective-permute-start(bf16[128,128]{1,0:T(8,128)(2,1)S(1)} %get-tuple-element.21.refs_1_.refs_4_), channel_id=1, source_target_pairs={{2,0},{4,2},{6,4},{0,6},{3,1},{5,3},{7,5},{1,7},{10,8},{12,10},{14... | collective-permute-start | bytes 98312 | tf_op jit(solution)/shard_map/ppermute | solution.py:214
  21.1 1.9 %collective-permute-start.3 = (bf16[16,128,128]{2,1,0:T(8,128)(2,1)S(1)}, bf16[16,128,128]{2,1,0:T(8,128)(2,1)S(1)}, u32[]{:S(2)}, u32[]{:S(2)}) collective-permute-start(bf16[16,128,128]{2,1,0:T(8,128)(2,1)S(1)} %all-to-all-done), channel_id=1, source_target_pairs={{0,1},{1,0},{2,3},{3,2},{4,5},{5,4},{6,7},{7,6},{8,9},{9,8},{10,11... | collective-permute-start | bytes 1572872 | tf_op jit(solution)/shard_map/ppermute | solution.py:230
  44.6 6.6 %collective-permute-start.4 = (f32[128,128]{1,0:T(8,128)S(1)}, f32[128,128]{1,0:T(8,128)S(1)}, u32[]{:S(2)}, u32[]{:S(2)}) collective-permute-start(f32[128,128]{1,0:T(8,128)S(1)} %get-tuple-element.29), channel_id=1, source_target_pairs={{6,0},{0,2},{2,4},{4,6},{7,1},{1,3},{3,5},{5,7},{14,8},{8,10},{10,... | collective-permute-start | bytes 196616 | tf_op jit(solution)/shard_map/ppermute | solution.py:214
  45.1 6.1 %collective-permute-start.5 = (f32[128,128]{1,0:T(8,128)S(1)}, f32[128,128]{1,0:T(8,128)S(1)}, u32[]{:S(2)}, u32[]{:S(2)}) collective-permute-start(f32[128,128]{1,0:T(8,128)S(1)} %get-tuple-element.30), channel_id=1, source_target_pairs={{4,0},{6,2},{0,4},{2,6},{5,1},{7,3},{1,5},{3,7},{12,8},{14,10},{8,... | collective-permute-start | bytes 196616 | tf_op jit(solution)/shard_map/ppermute | solution.py:214
  46.8 4.9 %collective-permute-start.6 = (f32[128,128]{1,0:T(8,128)S(1)}, f32[128,128]{1,0:T(8,128)S(1)}, u32[]{:S(2)}, u32[]{:S(2)}) collective-permute-start(f32[128,128]{1,0:T(8,128)S(1)} %get-tuple-element.31), channel_id=1, source_target_pairs={{2,0},{4,2},{6,4},{0,6},{3,1},{5,3},{7,5},{1,7},{10,8},{12,10},{14... | collective-permute-start | bytes 196616 | tf_op jit(solution)/shard_map/ppermute | solution.py:214
  48.3 3.4 %copy-start.2 = (f32[128,128]{1,0:T(8,128)S(1)}, f32[128,128]{1,0:T(8,128)}, u32[]{:S(2)}) copy-start(f32[128,128]{1,0:T(8,128)} %x_ref.3) | copy-start | bytes 196612

commit v4 on v3

--- a/solution.py
+++ b/solution.py
@@ -20,6 +20,10 @@
 VIEWS = NDEV * ROWS
 XY = ("y", "xh", "xl")
 ALL = ("y", "xh", "xl", "z", "co")
+FIRST = (10, 5)
+PLANES = [
+    [(FIRST[c] + k) % NXY * 8 + z * 2 + c for k in range(NXY)] for z in range(NZ) for c in range(NCO)
+]
 CHUNK = 256
 F32 = jnp.float32
 BF16 = jnp.bfloat16
@@ -70,9 +74,13 @@
     return jnp.exp2(s * SCALE)
 
 
+def slot(xy, half):
+    return (xy - FIRST[0] + (FIRST[0] - FIRST[1]) * half) & (NXY - 1)
+
+
 def local_mates(mates, z, half):
     here = (((mates >> 8) & 3) == z) & (((mates >> 7) & 1) == half)
-    return jnp.where(here, ((mates >> 10) << 7) | (mates & 127), -1)
+    return jnp.where(here, (slot(mates >> 10, half) << 7) | (mates & 127), -1)
 
 
 def sums_kernel(own_half, *refs):
@@ -81,6 +89,7 @@
     half = co if own_half else 1 - co
     mates = mate_ref[...]
     here = local_mates(mates, z, half)
+    own = slot(xy, co)
     width = 2 * ROWS
     down = lax.broadcasted_iota(jnp.int32, (8, width), 0)
     sums, pos = [], jnp.zeros((8, width), F32)
@@ -97,7 +106,7 @@
                 kept[q] = jnp.where(block == (c + k) // ROWS, s[k : k + 8], kept[q])
             e = expo(s)
             if own_half and g == 0:
-                col = lax.broadcasted_iota(jnp.int32, (CHUNK, ROWS), 0) + (c - xy * ROWS)
+                col = lax.broadcasted_iota(jnp.int32, (CHUNK, ROWS), 0) + (c - own * ROWS)
                 row = lax.broadcasted_iota(jnp.int32, (CHUNK, ROWS), 1)
                 e = jnp.concatenate([jnp.where(col == row, 0.0, e[:, :ROWS]), e[:, ROWS:]], axis=1)
             for k in range(0, CHUNK, 8):
@@ -150,7 +159,8 @@
             for c in range(NCO):
                 got = [got_ref[k * 8 + q * 2 + c, :, 0:ROWS].astype(F32) for q in range(NZ)]
                 total = got[0] + got[1] + (got[2] + got[3])
-                inv_ref[c, :, k * ROWS : (k + 1) * ROWS] = 1.0 / total[0:1]
+                at = slot(k, c) * ROWS
+                inv_ref[c, :, at : at + ROWS] = 1.0 / total[0:1]
         got = [got_ref[xy * 8 + q * 2 + co, :, 0 : 2 * ROWS].astype(F32) for q in range(NZ)]
         total = got[0] + got[1] + (got[2] + got[3])
         for r in range(NZ):
@@ -177,6 +187,7 @@
                 row = jnp.where(r == q, parts[q], row)
             loss = loss + row
         loss_ref[...] = jnp.sum(loss, axis=1, keepdims=True) / VIEWS
+    own = slot(xy, co)
     inv_row = jnp.concatenate([down_rows(aux_ref[r : r + 1]) for r in blocks], axis=0)
     mates = mate_ref[...]
     u = jnp.concatenate([ref[...] for ref in u_refs], axis=0)
@@ -189,7 +200,7 @@
         for c in range(0, c_ref.shape[0], CHUNK):
             e = expo(dot_nt(u, c_ref[c : c + CHUNK]))
             if h == 0 and not first:
-                col = lax.broadcasted_iota(jnp.int32, e.shape, 1) + (c - xy * ROWS)
+                col = lax.broadcasted_iota(jnp.int32, e.shape, 1) + (c - own * ROWS)
                 row = lax.broadcasted_iota(jnp.int32, e.shape, 0)
                 e = jnp.where(col == row, 0.0, e)
             weight = []
@@ -220,7 +231,7 @@
     xy = (y * 2 + xh) * 2 + xl
     place = jnp.stack([z, co, xy]).astype(jnp.int32)
     unit, copies = call(norm_kernel, [sds((ROWS, ROWS), BF16), sds((NXY, ROWS, ROWS), BF16)])(proj)
-    plane = lax.all_to_all(copies, XY, 0, 0, tiled=True)
+    plane = lax.all_to_all(copies, ALL, 0, 0, axis_index_groups=PLANES, tiled=True)
     rows = [unit] + [shift(unit, r) for r in range(1, NZ)]
     mates = partner.reshape(NXY, NZ, NCO, ROWS)
     mates = lax.dynamic_slice(mates, (xy, 0, co, 0), (1, NZ, 1, ROWS)).reshape(NZ, ROWS)

time: 52.8 us -> 51.8 us (0.981)
  waiting for transfers between devices: 6.46 us -> 4.43 us
  starting transfers between devices: 17.4 us -> 19.3 us
  blocking collectives: 17.4 us -> 16.5 us
    all_to_all x1, waiting for transfers between devices: 2.05 us -> 0.01 us  [body(): lax.all_to_all(copies, ALL, 0, 0, axis_index_groups=PLANES, tiled=True)]
    all_to_all x1, starting transfers between devices: 7.12 us -> 9.13 us  [body(): lax.all_to_all(copies, ALL, 0, 0, axis_index_groups=PLANES, tiled=True)]
    all_to_all x1, blocking collectives: 17.4 us -> 16.5 us  [body(): got = lax.all_to_all(send, ALL, 0, 0, tiled=True)]
  transfers between devices with their start and end apart: 8 -> 8, of which waited for: 6 -> 5; matrix products, arithmetic and copies ran while one was open for 0% -> 0% of each run, Pallas kernels for 7% -> 7%
where the time goes in v4:
time: 51.8 us; the launch traced here: 51.5 us
  starting transfers between devices  19.3 us (37%)
  blocking collectives  16.5 us (32%)
  Pallas kernels  9.59 us (19%)
  waiting for transfers between devices  4.43 us (9%)
  local copies, waits for them, and re-layouts  0.9 us (2%)
  between operations  0.7 us (1%)
    all_to_all x1, blocking collectives, body(): got = lax.all_to_all(send, ALL, 0, 0, tiled=True)  16.5 us
    ppermute x6, starting transfers between devices, shift(): return lax.ppermute(x, 'z', [((k + by) % NZ, k) for k in range(NZ)])  10.2 us
    pallas_call x6, Pallas kernels, run(): pl.pallas_call(body, out_shape=outs, in_specs=[SMEM if a.dtype == jnp.int...  9.59 us
    all_to_all x1, starting transfers between devices, body(): lax.all_to_all(copies, ALL, 0, 0, axis_index_groups=PLANES, tiled=True)  9.13 us
    ppermute x6, waiting for transfers between devices, shift(): return lax.ppermute(x, 'z', [((k + by) % NZ, k) for k in range(NZ)])  4.1 us
  transfers between devices with their start and end apart: 8, of which 5 were waited for; matrix products, arithmetic and copies ran while one was open for 0% of the time, Pallas kernels for 7%

profile of v4, /device:TPU:0, one launch (start us, length us, event | category | flops | bytes accessed | tf_op | source)
XLA Modules:
  0.0 51.5 jit_solution(13819796626533785549)
XLA Ops:
  0.6 0.0 copy-start
  0.6 0.0 copy-start.1
  0.7 0.9 %copy-done.1 = f32[128,128]{1,0:T(8,128)S(1)} copy-done((f32[128,128]{1,0:T(8,128)S(1)}, f32[128,128]{1,0:T(8,128)}, u32[]{:S(2)}) %copy-start.1) | copy-done | bytes 65560
  1.5 0.9 %shard_map.41 = (bf16[128,128]{1,0:T(8,128)(2,1)S(1)}, bf16[16,128,128]{2,1,0:T(8,128)(2,1)}) custom-call(f32[128,128]{1,0:T(8,128)S(1)} %copy-done.1), custom_call_target="tpu_custom_call" | custom-call | tf_op jit(solution)/shard_map/pallas_call | solution.py:36
  2.5 9.1 %all-to-all-start = ((bf16[16,128,128]{2,1,0:T(8,128)(2,1)}), bf16[16,128,128]{2,1,0:T(8,128)(2,1)S(1)}, u32[]{:S(2)}, u32[]{:S(2)}) async-start(bf16[16,128,128]{2,1,0:T(8,128)(2,1)} %get-tuple-element.17), calls=%async_computation | async-start | bytes 1048576 | tf_op jit(solution)/shard_map/all_to_all | solution.py:234
  11.6 1.9 %collective-permute-start.2 = (bf16[128,128]{1,0:T(8,128)(2,1)S(1)}, bf16[128,128]{1,0:T(8,128)(2,1)S(1)}, u32[]{:S(2)}, u32[]{:S(2)}) collective-permute-start(bf16[128,128]{1,0:T(8,128)(2,1)S(1)} %get-tuple-element.21.refs_1_.refs_4_), channel_id=1, source_target_pairs={{6,0},{0,2},{2,4},{4,6},{7,1},{1,3},{3,5},{5,7},{14,8},{8,10},{10,... | collective-permute-start | bytes 98312 | tf_op jit(solution)/shard_map/ppermute | solution.py:225
  13.5 3.6 %collective-permute-start.1 = (bf16[128,128]{1,0:T(8,128)(2,1)S(1)}, bf16[128,128]{1,0:T(8,128)(2,1)S(1)}, u32[]{:S(2)}, u32[]{:S(2)}) collective-permute-start(bf16[128,128]{1,0:T(8,128)(2,1)S(1)} %get-tuple-element.21.refs_1_.refs_4_), channel_id=1, source_target_pairs={{4,0},{6,2},{0,4},{2,6},{5,1},{7,3},{1,5},{3,7},{12,8},{14,10},{8,... | collective-permute-start | bytes 98312 | tf_op jit(solution)/shard_map/ppermute | solution.py:225
  17.1 1.0 %collective-permute-start = (bf16[128,128]{1,0:T(8,128)(2,1)S(1)}, bf16[128,128]{1,0:T(8,128)(2,1)S(1)}, u32[]{:S(2)}, u32[]{:S(2)}) collective-permute-start(bf16[128,128]{1,0:T(8,128)(2,1)S(1)} %get-tuple-element.21.refs_1_.refs_4_), channel_id=1, source_target_pairs={{2,0},{4,2},{6,4},{0,6},{3,1},{5,3},{7,5},{1,7},{10,8},{12,10},{14... | collective-permute-start | bytes 98312 | tf_op jit(solution)/shard_map/ppermute | solution.py:225
  18.1 0.0 copy-done
  18.1 0.0 collective-permute-done.2.refs_4_.refs_6_
  18.2 1.2 %collective-permute-done.1.refs_3_.refs_5_ = bf16[128,128]{1,0:T(8,128)(2,1)S(1)} collective-permute-done((bf16[128,128]{1,0:T(8,128)(2,1)S(1)}, bf16[128,128]{1,0:T(8,128)(2,1)S(1)}, u32[]{:S(2)}, u32[]{:S(2)}) %collective-permute-start.1) | collective-permute-done | bytes 32800 | tf_op jit(solution)/shard_map/ppermute | solution.py:225
  19.3 1.7 %collective-permute-done.refs_2_.refs_4_ = bf16[128,128]{1,0:T(8,128)(2,1)S(1)} collective-permute-done((bf16[128,128]{1,0:T(8,128)(2,1)S(1)}, bf16[128,128]{1,0:T(8,128)(2,1)S(1)}, u32[]{:S(2)}, u32[]{:S(2)}) %collective-permute-start) | collective-permute-done | bytes 32800 | tf_op jit(solution)/shard_map/ppermute | solution.py:225
  21.0 0.0 all-to-all-done
  21.0 0.0 collective-permute-start.3
  21.0 0.1 pad_add_fusion.1.refs_0_
  21.1 1.5 %shard_map.42.refs_7_ = f32[8,128]{1,0:T(8,128)S(1)} custom-call(s32[3]{0:T(128)S(1)} %pad_add_fusion.1.refs_0_, bf16[128,128]{1,0:T(8,128)(2,1)S(1)} %get-tuple-element.21.refs_1_.refs_4_, bf16[128,128]{1,0:T(8,128)(2,1)S(1)} %collective-permute-done.refs_2_.refs_4_, bf16[128,128]{1,0:T(8,128)(2,1)S(1)} %collective-permute-done.1.refs_3_.refs_5_, ...), custom_call_target="tpu_custom_call" | custom-call | flops 268435456 | bytes 1048576 | tf_op jit(solution)/shard_map/pallas_call | solution.py:36
  22.6 0.3 collective-permute-done.3
  22.9 1.5 %shard_map.43 = bf16[128,2,384]{2,1,0:T(2,128)(2,1)S(1)} custom-call(s32[3]{0:T(128)S(1)} %pad_add_fusion.1.refs_0_, bf16[128,128]{1,0:T(8,128)(2,1)S(1)} %get-tuple-element.21.refs_1_.refs_4_, bf16[128,128]{1,0:T(8,128)(2,1)S(1)} %collective-permute-done.refs_2_.refs_4_, bf16[128,128]{1,0:T(8,128)(2,1)S(1)} %collective-permute-done.1.refs_3_.refs_5_, ...), custom_call_target="tpu_custom_call" | custom-call | flops 268435456 | bytes 1048576 | tf_op jit(solution)/shard_map/pallas_call | solution.py:36
  24.4 16.5 %all_to_all.10.refs_7_.refs_5_ = bf16[128,2,384]{2,1,0:T(2,128)(2,1)S(1)} all-to-all(bf16[128,2,384]{2,1,0:T(2,128)(2,1)S(1)} %shard_map.43), channel_id=1, replica_groups=mesh['y'=4,'xh'=2,'xl'=2,'z'=4,'co'=2] {'y','xh','xl','z','co'}, dimensions={0} | all-to-all | bytes 393216 | tf_op jit(solution)/shard_map/all_to_all | solution.py:253
  40.9 2.7 %shard_map.44 = (f32[128,128]{1,0:T(8,128)S(1)}, f32[128,128]{1,0:T(8,128)S(1)}, f32[128,128]{1,0:T(8,128)S(1)}, f32[2,1,2048]{2,1,0:T(1,128)S(1)}, f32[8,128]{1,0:T(8,128)S(1)}) custom-call(s32[3]{0:T(128)S(1)} %pad_add_fusion.1.refs_0_, bf16[2048,128]{1,0:T(8,128)(2,1)S(1)} %bitcast.10, bf16[2048,128]{1,0:T(8,128)(2,1)S(1)} %bitcast.13, ...), custom_call_target="tpu_custom_call" | custom-call | flops 805306368 | bytes 1048576 | tf_op jit(solution)/shard_map/pallas_call | solution.py:36
  43.6 0.5 collective-permute-start.4
  44.1 1.7 %collective-permute-start.5 = (f32[128,128]{1,0:T(8,128)S(1)}, f32[128,128]{1,0:T(8,128)S(1)}, u32[]{:S(2)}, u32[]{:S(2)}) collective-permute-start(f32[128,128]{1,0:T(8,128)S(1)} %get-tuple-element.30), channel_id=1, source_target_pairs={{4,0},{6,2},{0,4},{2,6},{5,1},{7,3},{1,5},{3,7},{12,8},{14,10},{8,... | collective-permute-start | bytes 196616 | tf_op jit(solution)/shard_map/ppermute | solution.py:225
  45.8 1.5 %collective-permute-start.6 = (f32[128,128]{1,0:T(8,128)S(1)}, f32[128,128]{1,0:T(8,128)S(1)}, u32[]{:S(2)}, u32[]{:S(2)}) collective-permute-start(f32[128,128]{1,0:T(8,128)S(1)} %get-tuple-element.31), channel_id=1, source_target_pairs={{2,0},{4,2},{6,4},{0,6},{3,1},{5,3},{7,5},{1,7},{10,8},{12,10},{14... | collective-permute-start | bytes 196616 | tf_op jit(solution)/shard_map/ppermute | solution.py:225
  47.3 0.0 copy-start.2
  47.3 2.1 %shard_map.45 = (f32[128,128]{1,0:T(8,128)S(1)}, f32[1,1]{1,0:T(1,128)}) custom-call(s32[3]{0:T(128)S(1)} %pad_add_fusion.1.refs_0_, bf16[2048,128]{1,0:T(8,128)(2,1)S(1)} %bitcast.11, bf16[2048,128]{1,0:T(8,128)(2,1)S(1)} %bitcast.14, s32[4,128]{1,0:T(4,128)S(1)} %constant_dynamic-slice_fusion.refs_6_.refs_3_, ...), custom_call_target="tpu_custom_call" | custom-call | flops 805306368 | bytes 1048576 | tf_op jit(solution)/shard_map/pallas_call | solution.py:36
  49.4 0.7 %collective-permute-done.4.b1 = f32[128,128]{1,0:T(8,128)S(1)} collective-permute-done((f32[128,128]{1,0:T(8,128)S(1)}, f32[128,128]{1,0:T(8,128)S(1)}, u32[]{:S(2)}, u32[]{:S(2)}) %collective-permute-start.4) | collective-permute-done | bytes 65568 | tf_op jit(solution)/shard_map/ppermute | solution.py:225
  50.1 0.0 collective-permute-done.5.b2
  50.1 0.5 %collective-permute-done.6.b3 = f32[128,128]{1,0:T(8,128)S(1)} collective-permute-done((f32[128,128]{1,0:T(8,128)S(1)}, f32[128,128]{1,0:T(8,128)S(1)}, u32[]{:S(2)}, u32[]{:S(2)}) %collective-permute-start.6) | collective-permute-done | bytes 65568 | tf_op jit(solution)/shard_map/ppermute | solution.py:225
  50.7 0.0 copy-done.2
  50.7 0.8 %shard_map.46 = f32[128,128]{1,0:T(8,128)} custom-call(f32[128,128]{1,0:T(8,128)S(1)} %copy-done.2, f32[128,128]{1,0:T(8,128)S(1)} %get-tuple-element.28.b0, f32[128,128]{1,0:T(8,128)S(1)} %collective-permute-done.4.b1, f32[128,128]{1,0:T(8,128)S(1)} %collective-permute-done.5.b2, f32[128,128]{1,0:T(8,128)S(1)} %collective-permute-done.6.b3), custom_call_target="tpu_custom_call" | custom-call | tf_op jit(solution)/shard_map/pallas_call | solution.py:36
  (3 shorter events, 0.0 us)
Async XLA Ops:
  0.6 17.5 %copy-start = (s32[16384]{0:T(1024)S(1)}, s32[16384]{0:T(1024)}, u32[]{:S(2)}) copy-start(s32[16384]{0:T(1024)} %param.3) | copy-start | bytes 196612
  0.6 0.9 %copy-start.1 = (f32[128,128]{1,0:T(8,128)S(1)}, f32[128,128]{1,0:T(8,128)}, u32[]{:S(2)}) copy-start(f32[128,128]{1,0:T(8,128)} %x_ref.3) | copy-start | bytes 196612
  2.5 18.6 %all-to-all-start = ((bf16[16,128,128]{2,1,0:T(8,128)(2,1)}), bf16[16,128,128]{2,1,0:T(8,128)(2,1)S(1)}, u32[]{:S(2)}, u32[]{:S(2)}) async-start(bf16[16,128,128]{2,1,0:T(8,128)(2,1)} %get-tuple-element.17), calls=%async_computation | async-start | bytes 1048576 | tf_op jit(solution)/shard_map/all_to_all | solution.py:234
  11.6 6.6 %collective-permute-start.2 = (bf16[128,128]{1,0:T(8,128)(2,1)S(1)}, bf16[128,128]{1,0:T(8,128)(2,1)S(1)}, u32[]{:S(2)}, u32[]{:S(2)}) collective-permute-start(bf16[128,128]{1,0:T(8,128)(2,1)S(1)} %get-tuple-element.21.refs_1_.refs_4_), channel_id=1, source_target_pairs={{6,0},{0,2},{2,4},{4,6},{7,1},{1,3},{3,5},{5,7},{14,8},{8,10},{10,... | collective-permute-start | bytes 98312 | tf_op jit(solution)/shard_map/ppermute | solution.py:225
  13.5 5.8 %collective-permute-start.1 = (bf16[128,128]{1,0:T(8,128)(2,1)S(1)}, bf16[128,128]{1,0:T(8,128)(2,1)S(1)}, u32[]{:S(2)}, u32[]{:S(2)}) collective-permute-start(bf16[128,128]{1,0:T(8,128)(2,1)S(1)} %get-tuple-element.21.refs_1_.refs_4_), channel_id=1, source_target_pairs={{4,0},{6,2},{0,4},{2,6},{5,1},{7,3},{1,5},{3,7},{12,8},{14,10},{8,... | collective-permute-start | bytes 98312 | tf_op jit(solution)/shard_map/ppermute | solution.py:225
  17.1 3.9 %collective-permute-start = (bf16[128,128]{1,0:T(8,128)(2,1)S(1)}, bf16[128,128]{1,0:T(8,128)(2,1)S(1)}, u32[]{:S(2)}, u32[]{:S(2)}) collective-permute-start(bf16[128,128]{1,0:T(8,128)(2,1)S(1)} %get-tuple-element.21.refs_1_.refs_4_), channel_id=1, source_target_pairs={{2,0},{4,2},{6,4},{0,6},{3,1},{5,3},{7,5},{1,7},{10,8},{12,10},{14... | collective-permute-start | bytes 98312 | tf_op jit(solution)/shard_map/ppermute | solution.py:225
  21.0 1.9 %collective-permute-start.3 = (bf16[16,128,128]{2,1,0:T(8,128)(2,1)S(1)}, bf16[16,128,128]{2,1,0:T(8,128)(2,1)S(1)}, u32[]{:S(2)}, u32[]{:S(2)}) collective-permute-start(bf16[16,128,128]{2,1,0:T(8,128)(2,1)S(1)} %all-to-all-done), channel_id=1, source_target_pairs={{0,1},{1,0},{2,3},{3,2},{4,5},{5,4},{6,7},{7,6},{8,9},{9,8},{10,11... | collective-permute-start | bytes 1572872 | tf_op jit(solution)/shard_map/ppermute | solution.py:241
  43.6 6.6 %collective-permute-start.4 = (f32[128,128]{1,0:T(8,128)S(1)}, f32[128,128]{1,0:T(8,128)S(1)}, u32[]{:S(2)}, u32[]{:S(2)}) collective-permute-start(f32[128,128]{1,0:T(8,128)S(1)} %get-tuple-element.29), channel_id=1, source_target_pairs={{6,0},{0,2},{2,4},{4,6},{7,1},{1,3},{3,5},{5,7},{14,8},{8,10},{10,... | collective-permute-start | bytes 196616 | tf_op jit(solution)/shard_map/ppermute | solution.py:225
  44.1 6.1 %collective-permute-start.5 = (f32[128,128]{1,0:T(8,128)S(1)}, f32[128,128]{1,0:T(8,128)S(1)}, u32[]{:S(2)}, u32[]{:S(2)}) collective-permute-start(f32[128,128]{1,0:T(8,128)S(1)} %get-tuple-element.30), channel_id=1, source_target_pairs={{4,0},{6,2},{0,4},{2,6},{5,1},{7,3},{1,5},{3,7},{12,8},{14,10},{8,... | collective-permute-start | bytes 196616 | tf_op jit(solution)/shard_map/ppermute | solution.py:225
  45.8 4.9 %collective-permute-start.6 = (f32[128,128]{1,0:T(8,128)S(1)}, f32[128,128]{1,0:T(8,128)S(1)}, u32[]{:S(2)}, u32[]{:S(2)}) collective-permute-start(f32[128,128]{1,0:T(8,128)S(1)} %get-tuple-element.31), channel_id=1, source_target_pairs={{2,0},{4,2},{6,4},{0,6},{3,1},{5,3},{7,5},{1,7},{10,8},{12,10},{14... | collective-permute-start | bytes 196616 | tf_op jit(solution)/shard_map/ppermute | solution.py:225
  47.3 3.4 %copy-start.2 = (f32[128,128]{1,0:T(8,128)S(1)}, f32[128,128]{1,0:T(8,128)}, u32[]{:S(2)}) copy-start(f32[128,128]{1,0:T(8,128)} %x_ref.3) | copy-start | bytes 196612

commit v5 on v4

--- a/solution.py
+++ b/solution.py
@@ -20,11 +20,12 @@
 VIEWS = NDEV * ROWS
 XY = ("y", "xh", "xl")
 ALL = ("y", "xh", "xl", "z", "co")
-FIRST = (10, 5)
+FIRST = (13, 5)
 PLANES = [
     [(FIRST[c] + k) % NXY * 8 + z * 2 + c for k in range(NXY)] for z in range(NZ) for c in range(NCO)
 ]
 CHUNK = 256
+STRIP = 128
 F32 = jnp.float32
 BF16 = jnp.bfloat16
 VMEM = pl.BlockSpec(memory_space=pltpu.VMEM)
@@ -99,17 +100,17 @@
         block = mate >> 7
         total = jnp.zeros((8, width), F32)
         kept = [jnp.zeros((8, width), F32)] * (ROWS // 8)
-        for c in range(0, c_ref.shape[0], CHUNK):
-            s = dot_nt(c_ref[c : c + CHUNK], u)
-            for k in range(0, CHUNK, 8):
+        for c in range(0, c_ref.shape[0], STRIP):
+            s = dot_nt(c_ref[c : c + STRIP], u)
+            for k in range(0, STRIP, 8):
                 q = k % ROWS // 8
                 kept[q] = jnp.where(block == (c + k) // ROWS, s[k : k + 8], kept[q])
             e = expo(s)
             if own_half and g == 0:
-                col = lax.broadcasted_iota(jnp.int32, (CHUNK, ROWS), 0) + (c - own * ROWS)
-                row = lax.broadcasted_iota(jnp.int32, (CHUNK, ROWS), 1)
+                col = lax.broadcasted_iota(jnp.int32, (STRIP, ROWS), 0) + (c - own * ROWS)
+                row = lax.broadcasted_iota(jnp.int32, (STRIP, ROWS), 1)
                 e = jnp.concatenate([jnp.where(col == row, 0.0, e[:, :ROWS]), e[:, ROWS:]], axis=1)
-            for k in range(0, CHUNK, 8):
+            for k in range(0, STRIP, 8):
                 total = total + e[k : k + 8]
         for q, s in enumerate(kept):
             pos = pos + jnp.where((mate & 127) == down + 8 * q, s, 0.0)
@@ -254,13 +255,14 @@
     work = dict(flops=6 * n * cols * ROWS, nbytes=2**20, exps=2 * n * cols)
     block = sds((ROWS, ROWS))
     held = (place, plane, other, mates)
-    b1, b2, b3, *inv = call(
-        functools.partial(grads_kernel, (1, 2, 3)),
+    b2, b1, b3, *inv = call(
+        functools.partial(grads_kernel, (2, 1, 3)),
         [block] * 3 + [sds((NCO, 1, cols)), sds((8, ROWS))],
         **work,
-    )(*held, *rows[1:], got)
+    )(*held, rows[2], rows[1], rows[3], got)
     b0, loss = call(functools.partial(grads_kernel, (0,)), [block, sds((1, 1))], **work)(*held, rows[0], got, *inv)
-    b = [b0, shift(b1, -1), shift(b2, -2), shift(b3, -3)]
+    b = {1: b1, 2: b2, 3: b3}
+    b = [shift(b[r], -r) for r in (2, 1, 3)] + [b0]
     (grad,) = call(final_kernel, [sds((ROWS, ROWS))])(proj, *b)
     return loss.reshape(()), grad
 

time: 51.8 us -> 51.5 us (level)
  blocking collectives: 16.5 us -> 17.5 us
  waiting for transfers between devices: 4.43 us -> 3.65 us
    all_to_all x1, starting transfers between devices: 9.13 us -> 8.11 us  [body(): lax.all_to_all(copies, ALL, 0, 0, axis_index_groups=PLANES, tiled=True)]
    all_to_all x1, blocking collectives: 16.5 us -> 17.5 us  [body(): got = lax.all_to_all(send, ALL, 0, 0, tiled=True)]
    ppermute x6, waiting for transfers between devices: 4.1 us -> 3.3 us  [shift(): return lax.ppermute(x, 'z', [((k + by) % NZ, k) for k in range(NZ)])]
    ppermute x6, starting transfers between devices: 10.2 us -> 10.8 us  [shift(): return lax.ppermute(x, 'z', [((k + by) % NZ, k) for k in range(NZ)])]
  transfers between devices with their start and end apart: 8 -> 8, of which waited for: 5 -> 4; matrix products, arithmetic and copies ran while one was open for 0% -> 0% of each run, Pallas kernels for 7% -> 7%
where the time goes in v5:
time: 51.5 us; the launch traced here: 51.2 us
  starting transfers between devices  18.9 us (37%)
  blocking collectives  17.5 us (34%)
  Pallas kernels  9.51 us (18%)
  waiting for transfers between devices  3.65 us (7%)
  local copies, waits for them, and re-layouts  0.9 us (2%)
  between operations  0.7 us (1%)
    all_to_all x1, blocking collectives, body(): got = lax.all_to_all(send, ALL, 0, 0, tiled=True)  17.5 us
    ppermute x6, starting transfers between devices, shift(): return lax.ppermute(x, 'z', [((k + by) % NZ, k) for k in range(NZ)])  10.8 us
    pallas_call x6, Pallas kernels, run(): pl.pallas_call(body, out_shape=outs, in_specs=[SMEM if a.dtype == jnp.int...  9.51 us
    all_to_all x1, starting transfers between devices, body(): lax.all_to_all(copies, ALL, 0, 0, axis_index_groups=PLANES, tiled=True)  8.11 us
    ppermute x6, waiting for transfers between devices, shift(): return lax.ppermute(x, 'z', [((k + by) % NZ, k) for k in range(NZ)])  3.3 us
  transfers between devices with their start and end apart: 8, of which 4 were waited for; matrix products, arithmetic and copies ran while one was open for 0% of the time, Pallas kernels for 7%

profile of v5, /device:TPU:0, one launch (start us, length us, event | category | flops | bytes accessed | tf_op | source)
XLA Modules:
  0.0 51.2 jit_solution(17444683292133607077)
XLA Ops:
  0.6 0.0 copy-start
  0.6 0.0 copy-start.1
  0.7 0.9 %copy-done.1 = f32[128,128]{1,0:T(8,128)S(1)} copy-done((f32[128,128]{1,0:T(8,128)S(1)}, f32[128,128]{1,0:T(8,128)}, u32[]{:S(2)}) %copy-start.1) | copy-done | bytes 65560
  1.5 0.9 %shard_map.41 = (bf16[128,128]{1,0:T(8,128)(2,1)S(1)}, bf16[16,128,128]{2,1,0:T(8,128)(2,1)}) custom-call(f32[128,128]{1,0:T(8,128)S(1)} %copy-done.1), custom_call_target="tpu_custom_call" | custom-call | tf_op jit(solution)/shard_map/pallas_call | solution.py:37
  2.5 8.1 %all-to-all-start = ((bf16[16,128,128]{2,1,0:T(8,128)(2,1)}), bf16[16,128,128]{2,1,0:T(8,128)(2,1)S(1)}, u32[]{:S(2)}, u32[]{:S(2)}) async-start(bf16[16,128,128]{2,1,0:T(8,128)(2,1)} %get-tuple-element.17), calls=%async_computation | async-start | bytes 1048576 | tf_op jit(solution)/shard_map/all_to_all | solution.py:235
  10.6 1.9 %collective-permute-start.2 = (bf16[128,128]{1,0:T(8,128)(2,1)S(1)}, bf16[128,128]{1,0:T(8,128)(2,1)S(1)}, u32[]{:S(2)}, u32[]{:S(2)}) collective-permute-start(bf16[128,128]{1,0:T(8,128)(2,1)S(1)} %get-tuple-element.21.refs_1_.refs_4_), channel_id=1, source_target_pairs={{6,0},{0,2},{2,4},{4,6},{7,1},{1,3},{3,5},{5,7},{14,8},{8,10},{10,... | collective-permute-start | bytes 98312 | tf_op jit(solution)/shard_map/ppermute | solution.py:226
  12.5 3.6 %collective-permute-start.1 = (bf16[128,128]{1,0:T(8,128)(2,1)S(1)}, bf16[128,128]{1,0:T(8,128)(2,1)S(1)}, u32[]{:S(2)}, u32[]{:S(2)}) collective-permute-start(bf16[128,128]{1,0:T(8,128)(2,1)S(1)} %get-tuple-element.21.refs_1_.refs_4_), channel_id=1, source_target_pairs={{4,0},{6,2},{0,4},{2,6},{5,1},{7,3},{1,5},{3,7},{12,8},{14,10},{8,... | collective-permute-start | bytes 98312 | tf_op jit(solution)/shard_map/ppermute | solution.py:226
  16.1 1.0 %collective-permute-start = (bf16[128,128]{1,0:T(8,128)(2,1)S(1)}, bf16[128,128]{1,0:T(8,128)(2,1)S(1)}, u32[]{:S(2)}, u32[]{:S(2)}) collective-permute-start(bf16[128,128]{1,0:T(8,128)(2,1)S(1)} %get-tuple-element.21.refs_1_.refs_4_), channel_id=1, source_target_pairs={{2,0},{4,2},{6,4},{0,6},{3,1},{5,3},{7,5},{1,7},{10,8},{12,10},{14... | collective-permute-start | bytes 98312 | tf_op jit(solution)/shard_map/ppermute | solution.py:226
  17.1 0.0 copy-done
  17.1 0.0 collective-permute-done.2.refs_4_.refs_6_
  17.1 1.2 %collective-permute-done.1.refs_3_.refs_4_ = bf16[128,128]{1,0:T(8,128)(2,1)S(1)} collective-permute-done((bf16[128,128]{1,0:T(8,128)(2,1)S(1)}, bf16[128,128]{1,0:T(8,128)(2,1)S(1)}, u32[]{:S(2)}, u32[]{:S(2)}) %collective-permute-start.1) | collective-permute-done | bytes 32800 | tf_op jit(solution)/shard_map/ppermute | solution.py:226
  18.3 1.7 %collective-permute-done.refs_2_.refs_5_ = bf16[128,128]{1,0:T(8,128)(2,1)S(1)} collective-permute-done((bf16[128,128]{1,0:T(8,128)(2,1)S(1)}, bf16[128,128]{1,0:T(8,128)(2,1)S(1)}, u32[]{:S(2)}, u32[]{:S(2)}) %collective-permute-start) | collective-permute-done | bytes 32800 | tf_op jit(solution)/shard_map/ppermute | solution.py:226
  20.0 0.0 all-to-all-done
  20.0 0.0 collective-permute-start.3
  20.0 0.1 pad_add_fusion.1.refs_0_
  20.1 1.5 %shard_map.42.refs_7_ = f32[8,128]{1,0:T(8,128)S(1)} custom-call(s32[3]{0:T(128)S(1)} %pad_add_fusion.1.refs_0_, bf16[128,128]{1,0:T(8,128)(2,1)S(1)} %get-tuple-element.21.refs_1_.refs_4_, bf16[128,128]{1,0:T(8,128)(2,1)S(1)} %collective-permute-done.refs_2_.refs_5_, bf16[128,128]{1,0:T(8,128)(2,1)S(1)} %collective-permute-done.1.refs_3_.refs_4_, ...), custom_call_target="tpu_custom_call" | custom-call | flops 268435456 | bytes 1048576 | tf_op jit(solution)/shard_map/pallas_call | solution.py:37
  21.6 0.3 collective-permute-done.3
  21.9 1.4 %shard_map.43 = bf16[128,2,384]{2,1,0:T(2,128)(2,1)S(1)} custom-call(s32[3]{0:T(128)S(1)} %pad_add_fusion.1.refs_0_, bf16[128,128]{1,0:T(8,128)(2,1)S(1)} %get-tuple-element.21.refs_1_.refs_4_, bf16[128,128]{1,0:T(8,128)(2,1)S(1)} %collective-permute-done.refs_2_.refs_5_, bf16[128,128]{1,0:T(8,128)(2,1)S(1)} %collective-permute-done.1.refs_3_.refs_4_, ...), custom_call_target="tpu_custom_call" | custom-call | flops 268435456 | bytes 1048576 | tf_op jit(solution)/shard_map/pallas_call | solution.py:37
  23.3 17.5 %all_to_all.10.refs_7_.refs_5_ = bf16[128,2,384]{2,1,0:T(2,128)(2,1)S(1)} all-to-all(bf16[128,2,384]{2,1,0:T(2,128)(2,1)S(1)} %shard_map.43), channel_id=1, replica_groups=mesh['y'=4,'xh'=2,'xl'=2,'z'=4,'co'=2] {'y','xh','xl','z','co'}, dimensions={0} | all-to-all | bytes 393216 | tf_op jit(solution)/shard_map/all_to_all | solution.py:254
  40.8 2.7 %shard_map.44 = (f32[128,128]{1,0:T(8,128)S(1)}, f32[128,128]{1,0:T(8,128)S(1)}, f32[128,128]{1,0:T(8,128)S(1)}, f32[2,1,2048]{2,1,0:T(1,128)S(1)}, f32[8,128]{1,0:T(8,128)S(1)}) custom-call(s32[3]{0:T(128)S(1)} %pad_add_fusion.1.refs_0_, bf16[2048,128]{1,0:T(8,128)(2,1)S(1)} %bitcast.10, bf16[2048,128]{1,0:T(8,128)(2,1)S(1)} %bitcast.13, ...), custom_call_target="tpu_custom_call" | custom-call | flops 805306368 | bytes 1048576 | tf_op jit(solution)/shard_map/pallas_call | solution.py:37
  43.5 1.1 %collective-permute-start.4 = (f32[128,128]{1,0:T(8,128)S(1)}, f32[128,128]{1,0:T(8,128)S(1)}, u32[]{:S(2)}, u32[]{:S(2)}) collective-permute-start(f32[128,128]{1,0:T(8,128)S(1)} %get-tuple-element.28), channel_id=1, source_target_pairs={{4,0},{6,2},{0,4},{2,6},{5,1},{7,3},{1,5},{3,7},{12,8},{14,10},{8,... | collective-permute-start | bytes 196616 | tf_op jit(solution)/shard_map/ppermute | solution.py:226
  44.6 0.5 %collective-permute-start.5 = (f32[128,128]{1,0:T(8,128)S(1)}, f32[128,128]{1,0:T(8,128)S(1)}, u32[]{:S(2)}, u32[]{:S(2)}) collective-permute-start(f32[128,128]{1,0:T(8,128)S(1)} %get-tuple-element.29), channel_id=1, source_target_pairs={{6,0},{0,2},{2,4},{4,6},{7,1},{1,3},{3,5},{5,7},{14,8},{8,10},{10,... | collective-permute-start | bytes 196616 | tf_op jit(solution)/shard_map/ppermute | solution.py:226
  45.1 2.7 %collective-permute-start.6 = (f32[128,128]{1,0:T(8,128)S(1)}, f32[128,128]{1,0:T(8,128)S(1)}, u32[]{:S(2)}, u32[]{:S(2)}) collective-permute-start(f32[128,128]{1,0:T(8,128)S(1)} %get-tuple-element.30), channel_id=1, source_target_pairs={{2,0},{4,2},{6,4},{0,6},{3,1},{5,3},{7,5},{1,7},{10,8},{12,10},{14... | collective-permute-start | bytes 196616 | tf_op jit(solution)/shard_map/ppermute | solution.py:226
  47.8 0.0 copy-start.2
  47.8 2.1 %shard_map.45 = (f32[128,128]{1,0:T(8,128)S(1)}, f32[1,1]{1,0:T(1,128)}) custom-call(s32[3]{0:T(128)S(1)} %pad_add_fusion.1.refs_0_, bf16[2048,128]{1,0:T(8,128)(2,1)S(1)} %bitcast.11, bf16[2048,128]{1,0:T(8,128)(2,1)S(1)} %bitcast.14, s32[4,128]{1,0:T(4,128)S(1)} %constant_dynamic-slice_fusion.refs_6_.refs_3_, ...), custom_call_target="tpu_custom_call" | custom-call | flops 805306368 | bytes 1048576 | tf_op jit(solution)/shard_map/pallas_call | solution.py:37
  50.0 0.0 collective-permute-done.4.b0
  50.0 0.4 collective-permute-done.5.b1
  50.4 0.0 collective-permute-done.6.b2
  50.4 0.0 copy-done.2
  50.4 0.8 %shard_map.46 = f32[128,128]{1,0:T(8,128)} custom-call(f32[128,128]{1,0:T(8,128)S(1)} %copy-done.2, f32[128,128]{1,0:T(8,128)S(1)} %collective-permute-done.4.b0, f32[128,128]{1,0:T(8,128)S(1)} %collective-permute-done.5.b1, f32[128,128]{1,0:T(8,128)S(1)} %collective-permute-done.6.b2, f32[128,128]{1,0:T(8,128)S(1)} %get-tuple-element.31.b3), custom_call_target="tpu_custom_call" | custom-call | tf_op jit(solution)/shard_map/pallas_call | solution.py:37
  (3 shorter events, 0.0 us)
Async XLA Ops:
  0.6 16.5 %copy-start = (s32[16384]{0:T(1024)S(1)}, s32[16384]{0:T(1024)}, u32[]{:S(2)}) copy-start(s32[16384]{0:T(1024)} %param.3) | copy-start | bytes 196612
  0.6 0.9 %copy-start.1 = (f32[128,128]{1,0:T(8,128)S(1)}, f32[128,128]{1,0:T(8,128)}, u32[]{:S(2)}) copy-start(f32[128,128]{1,0:T(8,128)} %x_ref.3) | copy-start | bytes 196612
  2.5 17.5 %all-to-all-start = ((bf16[16,128,128]{2,1,0:T(8,128)(2,1)}), bf16[16,128,128]{2,1,0:T(8,128)(2,1)S(1)}, u32[]{:S(2)}, u32[]{:S(2)}) async-start(bf16[16,128,128]{2,1,0:T(8,128)(2,1)} %get-tuple-element.17), calls=%async_computation | async-start | bytes 1048576 | tf_op jit(solution)/shard_map/all_to_all | solution.py:235
  10.6 6.6 %collective-permute-start.2 = (bf16[128,128]{1,0:T(8,128)(2,1)S(1)}, bf16[128,128]{1,0:T(8,128)(2,1)S(1)}, u32[]{:S(2)}, u32[]{:S(2)}) collective-permute-start(bf16[128,128]{1,0:T(8,128)(2,1)S(1)} %get-tuple-element.21.refs_1_.refs_4_), channel_id=1, source_target_pairs={{6,0},{0,2},{2,4},{4,6},{7,1},{1,3},{3,5},{5,7},{14,8},{8,10},{10,... | collective-permute-start | bytes 98312 | tf_op jit(solution)/shard_map/ppermute | solution.py:226
  12.5 5.8 %collective-permute-start.1 = (bf16[128,128]{1,0:T(8,128)(2,1)S(1)}, bf16[128,128]{1,0:T(8,128)(2,1)S(1)}, u32[]{:S(2)}, u32[]{:S(2)}) collective-permute-start(bf16[128,128]{1,0:T(8,128)(2,1)S(1)} %get-tuple-element.21.refs_1_.refs_4_), channel_id=1, source_target_pairs={{4,0},{6,2},{0,4},{2,6},{5,1},{7,3},{1,5},{3,7},{12,8},{14,10},{8,... | collective-permute-start | bytes 98312 | tf_op jit(solution)/shard_map/ppermute | solution.py:226
  16.1 3.9 %collective-permute-start = (bf16[128,128]{1,0:T(8,128)(2,1)S(1)}, bf16[128,128]{1,0:T(8,128)(2,1)S(1)}, u32[]{:S(2)}, u32[]{:S(2)}) collective-permute-start(bf16[128,128]{1,0:T(8,128)(2,1)S(1)} %get-tuple-element.21.refs_1_.refs_4_), channel_id=1, source_target_pairs={{2,0},{4,2},{6,4},{0,6},{3,1},{5,3},{7,5},{1,7},{10,8},{12,10},{14... | collective-permute-start | bytes 98312 | tf_op jit(solution)/shard_map/ppermute | solution.py:226
  20.0 1.9 %collective-permute-start.3 = (bf16[16,128,128]{2,1,0:T(8,128)(2,1)S(1)}, bf16[16,128,128]{2,1,0:T(8,128)(2,1)S(1)}, u32[]{:S(2)}, u32[]{:S(2)}) collective-permute-start(bf16[16,128,128]{2,1,0:T(8,128)(2,1)S(1)} %all-to-all-done), channel_id=1, source_target_pairs={{0,1},{1,0},{2,3},{3,2},{4,5},{5,4},{6,7},{7,6},{8,9},{9,8},{10,11... | collective-permute-start | bytes 1572872 | tf_op jit(solution)/shard_map/ppermute | solution.py:242
  43.5 6.5 %collective-permute-start.4 = (f32[128,128]{1,0:T(8,128)S(1)}, f32[128,128]{1,0:T(8,128)S(1)}, u32[]{:S(2)}, u32[]{:S(2)}) collective-permute-start(f32[128,128]{1,0:T(8,128)S(1)} %get-tuple-element.28), channel_id=1, source_target_pairs={{4,0},{6,2},{0,4},{2,6},{5,1},{7,3},{1,5},{3,7},{12,8},{14,10},{8,... | collective-permute-start | bytes 196616 | tf_op jit(solution)/shard_map/ppermute | solution.py:226
  44.6 5.8 %collective-permute-start.5 = (f32[128,128]{1,0:T(8,128)S(1)}, f32[128,128]{1,0:T(8,128)S(1)}, u32[]{:S(2)}, u32[]{:S(2)}) collective-permute-start(f32[128,128]{1,0:T(8,128)S(1)} %get-tuple-element.29), channel_id=1, source_target_pairs={{6,0},{0,2},{2,4},{4,6},{7,1},{1,3},{3,5},{5,7},{14,8},{8,10},{10,... | collective-permute-start | bytes 196616 | tf_op jit(solution)/shard_map/ppermute | solution.py:226
  45.1 5.3 %collective-permute-start.6 = (f32[128,128]{1,0:T(8,128)S(1)}, f32[128,128]{1,0:T(8,128)S(1)}, u32[]{:S(2)}, u32[]{:S(2)}) collective-permute-start(f32[128,128]{1,0:T(8,128)S(1)} %get-tuple-element.30), channel_id=1, source_target_pairs={{2,0},{4,2},{6,4},{0,6},{3,1},{5,3},{7,5},{1,7},{10,8},{12,10},{14... | collective-permute-start | bytes 196616 | tf_op jit(solution)/shard_map/ppermute | solution.py:226
  47.8 2.6 %copy-start.2 = (f32[128,128]{1,0:T(8,128)S(1)}, f32[128,128]{1,0:T(8,128)}, u32[]{:S(2)}) copy-start(f32[128,128]{1,0:T(8,128)} %x_ref.3) | copy-start | bytes 196612

commit v6 on v5

--- a/solution.py
+++ b/solution.py
@@ -29,7 +29,6 @@
 F32 = jnp.float32
 BF16 = jnp.bfloat16
 VMEM = pl.BlockSpec(memory_space=pltpu.VMEM)
-SMEM = pl.BlockSpec(memory_space=pltpu.SMEM)
 
 
 def call(body, outs, scratch=(), flops=0, nbytes=0, exps=0):
@@ -37,7 +36,7 @@
         return pl.pallas_call(
             body,
             out_shape=outs,
-            in_specs=[SMEM if a.dtype == jnp.int32 and a.ndim == 1 else VMEM for a in args],
+            in_specs=[VMEM] * len(args),
             out_specs=[VMEM] * len(outs),
             scratch_shapes=list(scratch),
             compiler_params=pltpu.CompilerParams(vmem_limit_bytes=16 * 2**20),
@@ -75,6 +74,11 @@
     return jnp.exp2(s * SCALE)
 
 
+def position():
+    y, xh, xl = (lax.axis_index(a) for a in XY)
+    return lax.axis_index("z"), lax.axis_index("co"), (y * 2 + xh) * 2 + xl
+
+
 def slot(xy, half):
     return (xy - FIRST[0] + (FIRST[0] - FIRST[1]) * half) & (NXY - 1)
 
@@ -85,8 +89,8 @@
 
 
 def sums_kernel(own_half, *refs):
-    place_ref, u0, u1, u2, u3, c_ref, mate_ref = refs[:7]
-    z, co, xy = place_ref[0], place_ref[1], place_ref[2]
+    u0, u1, u2, u3, c_ref, mate_ref = refs[:6]
+    z, co, xy = position()
     half = co if own_half else 1 - co
     mates = mate_ref[...]
     here = local_mates(mates, z, half)
@@ -120,12 +124,12 @@
     rows = [sums[:, r * ROWS : (r + 1) * ROWS] for r in range(NZ)]
     rows.append(pos[:, :ROWS] + pos[:, ROWS:])
     if own_half:
-        out_ref = refs[7]
+        out_ref = refs[6]
         for q, row in enumerate(rows):
             out_ref[q : q + 1] = row
         out_ref[5:8] = jnp.zeros((3, ROWS), F32)
         return
-    in_ref, send_ref = refs[7:]
+    in_ref, send_ref = refs[6:]
     rows = [row + in_ref[q : q + 1] for q, row in enumerate(rows)]
     planes = []
     for k in range(NZ):
@@ -149,13 +153,13 @@
 def grads_kernel(blocks, *refs):
     n = len(blocks)
     first = 0 not in blocks
-    place_ref, own_ref, other_ref, mate_ref = refs[:4]
-    u_refs = refs[4 : 4 + n]
-    z, co, xy = place_ref[0], place_ref[1], place_ref[2]
-    got_ref = refs[4 + n]
+    own_ref, other_ref, mate_ref = refs[:3]
+    u_refs = refs[3 : 3 + n]
+    z, co, xy = position()
+    got_ref = refs[3 + n]
     if first:
-        out_refs = refs[5 + n : 5 + 2 * n]
-        inv_ref, aux_ref = refs[5 + 2 * n :]
+        out_refs = refs[4 + n : 4 + 2 * n]
+        inv_ref, aux_ref = refs[4 + 2 * n :]
         for k in range(NXY):
             for c in range(NCO):
                 got = [got_ref[k * 8 + q * 2 + c, :, 0:ROWS].astype(F32) for q in range(NZ)]
@@ -169,7 +173,7 @@
             aux_ref[r : r + 1] = 1.0 / part
         aux_ref[NZ:] = jnp.zeros((8 - NZ, ROWS), F32)
     else:
-        inv_ref, aux_ref, *out_refs, loss_ref = refs[5 + n :]
+        inv_ref, aux_ref, *out_refs, loss_ref = refs[4 + n :]
         logs = jnp.zeros((2, 2 * ROWS), F32)
         pos = jnp.zeros((2, ROWS), F32)
         for k in range(NXY):
@@ -227,10 +231,7 @@
 
 
 def body(proj, partner):
-    y, xh, xl = (lax.axis_index(a) for a in XY)
-    z, co = lax.axis_index("z"), lax.axis_index("co")
-    xy = (y * 2 + xh) * 2 + xl
-    place = jnp.stack([z, co, xy]).astype(jnp.int32)
+    z, co, xy = position()
     unit, copies = call(norm_kernel, [sds((ROWS, ROWS), BF16), sds((NXY, ROWS, ROWS), BF16)])(proj)
     plane = lax.all_to_all(copies, ALL, 0, 0, axis_index_groups=PLANES, tiled=True)
     rows = [unit] + [shift(unit, r) for r in range(1, NZ)]
@@ -247,14 +248,14 @@
     work = dict(flops=2 * n * cols * ROWS, nbytes=2**20, exps=n * cols)
     first = call(
         functools.partial(sums_kernel, True), [sds((8, ROWS))], **work
-    )(place, *rows, plane, mates)
+    )(*rows, plane, mates)
     (send,) = call(
         functools.partial(sums_kernel, False), [sds((NDEV, 2, 3 * ROWS), BF16)], **work
-    )(place, *rows, other, mates, *first)
+    )(*rows, other, mates, *first)
     got = lax.all_to_all(send, ALL, 0, 0, tiled=True)
     work = dict(flops=6 * n * cols * ROWS, nbytes=2**20, exps=2 * n * cols)
     block = sds((ROWS, ROWS))
-    held = (place, plane, other, mates)
+    held = (plane, other, mates)
     b2, b1, b3, *inv = call(
         functools.partial(grads_kernel, (2, 1, 3)),
         [block] * 3 + [sds((NCO, 1, cols)), sds((8, ROWS))],

time: 51.5 us -> 50.4 us (0.979)
  Pallas kernels: 9.51 us -> 7.37 us
  waiting for transfers between devices: 3.65 us -> 4.79 us
    pallas_call x6, Pallas kernels: 9.51 us -> 7.37 us  [run(): pl.pallas_call(body, out_shape=outs, in_specs=[VMEM] * len(args), out_spe...]
    ppermute x1, waiting for transfers between devices: 0.35 us -> 0.97 us  [body(): other = lax.ppermute(plane, 'co', [(0, 1), (1, 0)])]
    ppermute x6, waiting for transfers between devices: 3.3 us -> 3.81 us  [shift(): return lax.ppermute(x, 'z', [((k + by) % NZ, k) for k in range(NZ)])]
  transfers between devices with their start and end apart: 8 -> 8, of which waited for: 4 -> 5; matrix products, arithmetic and copies ran while one was open for 0% -> 0% of each run, Pallas kernels for 7% -> 5%
where the time goes in v6:
time: 50.4 us; the launch traced here: 50.2 us
  starting transfers between devices  18.9 us (38%)
  blocking collectives  17.5 us (35%)
  Pallas kernels  7.37 us (15%)
  waiting for transfers between devices  4.79 us (10%)
  local copies, waits for them, and re-layouts  0.9 us (2%)
  between operations  0.7 us (1%)
    all_to_all x1, blocking collectives, body(): got = lax.all_to_all(send, ALL, 0, 0, tiled=True)  17.5 us
    ppermute x6, starting transfers between devices, shift(): return lax.ppermute(x, 'z', [((k + by) % NZ, k) for k in range(NZ)])  10.8 us
    all_to_all x1, starting transfers between devices, body(): lax.all_to_all(copies, ALL, 0, 0, axis_index_groups=PLANES, tiled=True)  8.11 us
    pallas_call x6, Pallas kernels, run(): pl.pallas_call(body, out_shape=outs, in_specs=[VMEM] * len(args), out_spe...  7.37 us
    ppermute x6, waiting for transfers between devices, shift(): return lax.ppermute(x, 'z', [((k + by) % NZ, k) for k in range(NZ)])  3.81 us
  transfers between devices with their start and end apart: 8, of which 5 were waited for; matrix products, arithmetic and copies ran while one was open for 0% of the time, Pallas kernels for 5%

profile of v6, /device:TPU:0, one launch (start us, length us, event | category | flops | bytes accessed | tf_op | source)
XLA Modules:
  0.0 50.2 jit_solution(8894972286721398307)
XLA Ops:
  0.6 0.0 copy-start
  0.6 0.0 copy-start.1
  0.7 0.9 %copy-done.1 = f32[128,128]{1,0:T(8,128)S(1)} copy-done((f32[128,128]{1,0:T(8,128)S(1)}, f32[128,128]{1,0:T(8,128)}, u32[]{:S(2)}) %copy-start.1) | copy-done | bytes 65560
  1.5 0.9 %shard_map.41 = (bf16[128,128]{1,0:T(8,128)(2,1)S(1)}, bf16[16,128,128]{2,1,0:T(8,128)(2,1)}) custom-call(f32[128,128]{1,0:T(8,128)S(1)} %copy-done.1), custom_call_target="tpu_custom_call" | custom-call | tf_op jit(solution)/shard_map/pallas_call | solution.py:36
  2.5 8.1 %all-to-all-start = ((bf16[16,128,128]{2,1,0:T(8,128)(2,1)}), bf16[16,128,128]{2,1,0:T(8,128)(2,1)S(1)}, u32[]{:S(2)}, u32[]{:S(2)}) async-start(bf16[16,128,128]{2,1,0:T(8,128)(2,1)} %get-tuple-element.17), calls=%async_computation | async-start | bytes 1048576 | tf_op jit(solution)/shard_map/all_to_all | solution.py:236
  10.6 1.9 %collective-permute-start.2 = (bf16[128,128]{1,0:T(8,128)(2,1)S(1)}, bf16[128,128]{1,0:T(8,128)(2,1)S(1)}, u32[]{:S(2)}, u32[]{:S(2)}) collective-permute-start(bf16[128,128]{1,0:T(8,128)(2,1)S(1)} %get-tuple-element.21.refs_0_.refs_3_), channel_id=1, source_target_pairs={{6,0},{0,2},{2,4},{4,6},{7,1},{1,3},{3,5},{5,7},{14,8},{8,10},{10,... | collective-permute-start | bytes 98312 | tf_op jit(solution)/shard_map/ppermute | solution.py:230
  12.5 3.6 %collective-permute-start.1 = (bf16[128,128]{1,0:T(8,128)(2,1)S(1)}, bf16[128,128]{1,0:T(8,128)(2,1)S(1)}, u32[]{:S(2)}, u32[]{:S(2)}) collective-permute-start(bf16[128,128]{1,0:T(8,128)(2,1)S(1)} %get-tuple-element.21.refs_0_.refs_3_), channel_id=1, source_target_pairs={{4,0},{6,2},{0,4},{2,6},{5,1},{7,3},{1,5},{3,7},{12,8},{14,10},{8,... | collective-permute-start | bytes 98312 | tf_op jit(solution)/shard_map/ppermute | solution.py:230
  16.1 1.0 %collective-permute-start = (bf16[128,128]{1,0:T(8,128)(2,1)S(1)}, bf16[128,128]{1,0:T(8,128)(2,1)S(1)}, u32[]{:S(2)}, u32[]{:S(2)}) collective-permute-start(bf16[128,128]{1,0:T(8,128)(2,1)S(1)} %get-tuple-element.21.refs_0_.refs_3_), channel_id=1, source_target_pairs={{2,0},{4,2},{6,4},{0,6},{3,1},{5,3},{7,5},{1,7},{10,8},{12,10},{14... | collective-permute-start | bytes 98312 | tf_op jit(solution)/shard_map/ppermute | solution.py:230
  17.1 0.0 copy-done
  17.1 0.0 collective-permute-done.2.refs_3_.refs_5_
  17.1 1.2 %collective-permute-done.1.refs_2_.refs_3_ = bf16[128,128]{1,0:T(8,128)(2,1)S(1)} collective-permute-done((bf16[128,128]{1,0:T(8,128)(2,1)S(1)}, bf16[128,128]{1,0:T(8,128)(2,1)S(1)}, u32[]{:S(2)}, u32[]{:S(2)}) %collective-permute-start.1) | collective-permute-done | bytes 32800 | tf_op jit(solution)/shard_map/ppermute | solution.py:230
  18.3 1.7 %collective-permute-done.refs_1_.refs_4_ = bf16[128,128]{1,0:T(8,128)(2,1)S(1)} collective-permute-done((bf16[128,128]{1,0:T(8,128)(2,1)S(1)}, bf16[128,128]{1,0:T(8,128)(2,1)S(1)}, u32[]{:S(2)}, u32[]{:S(2)}) %collective-permute-start) | collective-permute-done | bytes 32800 | tf_op jit(solution)/shard_map/ppermute | solution.py:230
  20.0 0.0 all-to-all-done
  20.0 0.0 collective-permute-start.3
  20.0 0.9 %shard_map.42.refs_6_ = f32[8,128]{1,0:T(8,128)S(1)} custom-call(bf16[128,128]{1,0:T(8,128)(2,1)S(1)} %get-tuple-element.21.refs_0_.refs_3_, bf16[128,128]{1,0:T(8,128)(2,1)S(1)} %collective-permute-done.refs_1_.refs_4_, bf16[128,128]{1,0:T(8,128)(2,1)S(1)} %collective-permute-done.1.refs_2_.refs_3_, ...), custom_call_target="tpu_custom_call" | custom-call | flops 268435456 | bytes 1048576 | tf_op jit(solution)/shard_map/pallas_call | solution.py:36
  20.9 1.0 %collective-permute-done.3 = bf16[16,128,128]{2,1,0:T(8,128)(2,1)S(1)} collective-permute-done((bf16[16,128,128]{2,1,0:T(8,128)(2,1)S(1)}, bf16[16,128,128]{2,1,0:T(8,128)(2,1)S(1)}, u32[]{:S(2)}, u32[]{:S(2)}) %collective-permute-start.3) | collective-permute-done | bytes 524320 | tf_op jit(solution)/shard_map/ppermute | solution.py:243
  21.9 0.9 %shard_map.43 = bf16[128,2,384]{2,1,0:T(2,128)(2,1)S(1)} custom-call(bf16[128,128]{1,0:T(8,128)(2,1)S(1)} %get-tuple-element.21.refs_0_.refs_3_, bf16[128,128]{1,0:T(8,128)(2,1)S(1)} %collective-permute-done.refs_1_.refs_4_, bf16[128,128]{1,0:T(8,128)(2,1)S(1)} %collective-permute-done.1.refs_2_.refs_3_, ...), custom_call_target="tpu_custom_call" | custom-call | flops 268435456 | bytes 1048576 | tf_op jit(solution)/shard_map/pallas_call | solution.py:36
  22.8 17.5 %all_to_all.10.refs_6_.refs_4_ = bf16[128,2,384]{2,1,0:T(2,128)(2,1)S(1)} all-to-all(bf16[128,2,384]{2,1,0:T(2,128)(2,1)S(1)} %shard_map.43), channel_id=1, replica_groups=mesh['y'=4,'xh'=2,'xl'=2,'z'=4,'co'=2] {'y','xh','xl','z','co'}, dimensions={0} | all-to-all | bytes 393216 | tf_op jit(solution)/shard_map/all_to_all | solution.py:255
  40.3 2.2 %shard_map.44 = (f32[128,128]{1,0:T(8,128)S(1)}, f32[128,128]{1,0:T(8,128)S(1)}, f32[128,128]{1,0:T(8,128)S(1)}, f32[2,1,2048]{2,1,0:T(1,128)S(1)}, f32[8,128]{1,0:T(8,128)S(1)}) custom-call(bf16[2048,128]{1,0:T(8,128)(2,1)S(1)} %bitcast.7, bf16[2048,128]{1,0:T(8,128)(2,1)S(1)} %bitcast.10, s32[4,128]{1,0:T(4,128)S(1)} %constant_dynamic-slice_fusion.refs_5_.refs_2_, ...), custom_call_target="tpu_custom_call" | custom-call | flops 805306368 | bytes 1048576 | tf_op jit(solution)/shard_map/pallas_call | solution.py:36
  42.4 1.1 %collective-permute-start.4 = (f32[128,128]{1,0:T(8,128)S(1)}, f32[128,128]{1,0:T(8,128)S(1)}, u32[]{:S(2)}, u32[]{:S(2)}) collective-permute-start(f32[128,128]{1,0:T(8,128)S(1)} %get-tuple-element.28), channel_id=1, source_target_pairs={{4,0},{6,2},{0,4},{2,6},{5,1},{7,3},{1,5},{3,7},{12,8},{14,10},{8,... | collective-permute-start | bytes 196616 | tf_op jit(solution)/shard_map/ppermute | solution.py:230
  43.5 0.5 %collective-permute-start.5 = (f32[128,128]{1,0:T(8,128)S(1)}, f32[128,128]{1,0:T(8,128)S(1)}, u32[]{:S(2)}, u32[]{:S(2)}) collective-permute-start(f32[128,128]{1,0:T(8,128)S(1)} %get-tuple-element.29), channel_id=1, source_target_pairs={{6,0},{0,2},{2,4},{4,6},{7,1},{1,3},{3,5},{5,7},{14,8},{8,10},{10,... | collective-permute-start | bytes 196616 | tf_op jit(solution)/shard_map/ppermute | solution.py:230
  44.0 2.7 %collective-permute-start.6 = (f32[128,128]{1,0:T(8,128)S(1)}, f32[128,128]{1,0:T(8,128)S(1)}, u32[]{:S(2)}, u32[]{:S(2)}) collective-permute-start(f32[128,128]{1,0:T(8,128)S(1)} %get-tuple-element.30), channel_id=1, source_target_pairs={{2,0},{4,2},{6,4},{0,6},{3,1},{5,3},{7,5},{1,7},{10,8},{12,10},{14... | collective-permute-start | bytes 196616 | tf_op jit(solution)/shard_map/ppermute | solution.py:230
  46.7 0.0 copy-start.2
  46.7 1.6 %shard_map.45 = (f32[128,128]{1,0:T(8,128)S(1)}, f32[1,1]{1,0:T(1,128)}) custom-call(bf16[2048,128]{1,0:T(8,128)(2,1)S(1)} %bitcast.8, bf16[2048,128]{1,0:T(8,128)(2,1)S(1)} %bitcast.11, s32[4,128]{1,0:T(4,128)S(1)} %constant_dynamic-slice_fusion.refs_5_.refs_2_, bf16[128,128]{1,0:T(8,128)(2,1)S(1)} %get-tuple-element.21.refs_0_.refs_3_, ...), custom_call_target="tpu_custom_call" | custom-call | flops 805306368 | bytes 1048576 | tf_op jit(solution)/shard_map/pallas_call | solution.py:36
  48.4 0.4 collective-permute-done.4.b0
  48.8 0.5 %collective-permute-done.5.b1 = f32[128,128]{1,0:T(8,128)S(1)} collective-permute-done((f32[128,128]{1,0:T(8,128)S(1)}, f32[128,128]{1,0:T(8,128)S(1)}, u32[]{:S(2)}, u32[]{:S(2)}) %collective-permute-start.5) | collective-permute-done | bytes 65568 | tf_op jit(solution)/shard_map/ppermute | solution.py:230
  49.3 0.0 collective-permute-done.6.b2
  49.3 0.0 copy-done.2
  49.3 0.8 %shard_map.46 = f32[128,128]{1,0:T(8,128)} custom-call(f32[128,128]{1,0:T(8,128)S(1)} %copy-done.2, f32[128,128]{1,0:T(8,128)S(1)} %collective-permute-done.4.b0, f32[128,128]{1,0:T(8,128)S(1)} %collective-permute-done.5.b1, f32[128,128]{1,0:T(8,128)S(1)} %collective-permute-done.6.b2, f32[128,128]{1,0:T(8,128)S(1)} %get-tuple-element.31.b3), custom_call_target="tpu_custom_call" | custom-call | tf_op jit(solution)/shard_map/pallas_call | solution.py:36
  (3 shorter events, 0.0 us)
Async XLA Ops:
  0.6 16.5 %copy-start = (s32[16384]{0:T(1024)S(1)}, s32[16384]{0:T(1024)}, u32[]{:S(2)}) copy-start(s32[16384]{0:T(1024)} %param.3) | copy-start | bytes 196612
  0.6 0.9 %copy-start.1 = (f32[128,128]{1,0:T(8,128)S(1)}, f32[128,128]{1,0:T(8,128)}, u32[]{:S(2)}) copy-start(f32[128,128]{1,0:T(8,128)} %x_ref.3) | copy-start | bytes 196612
  2.5 17.5 %all-to-all-start = ((bf16[16,128,128]{2,1,0:T(8,128)(2,1)}), bf16[16,128,128]{2,1,0:T(8,128)(2,1)S(1)}, u32[]{:S(2)}, u32[]{:S(2)}) async-start(bf16[16,128,128]{2,1,0:T(8,128)(2,1)} %get-tuple-element.17), calls=%async_computation | async-start | bytes 1048576 | tf_op jit(solution)/shard_map/all_to_all | solution.py:236
  10.6 6.6 %collective-permute-start.2 = (bf16[128,128]{1,0:T(8,128)(2,1)S(1)}, bf16[128,128]{1,0:T(8,128)(2,1)S(1)}, u32[]{:S(2)}, u32[]{:S(2)}) collective-permute-start(bf16[128,128]{1,0:T(8,128)(2,1)S(1)} %get-tuple-element.21.refs_0_.refs_3_), channel_id=1, source_target_pairs={{6,0},{0,2},{2,4},{4,6},{7,1},{1,3},{3,5},{5,7},{14,8},{8,10},{10,... | collective-permute-start | bytes 98312 | tf_op jit(solution)/shard_map/ppermute | solution.py:230
  12.5 5.8 %collective-permute-start.1 = (bf16[128,128]{1,0:T(8,128)(2,1)S(1)}, bf16[128,128]{1,0:T(8,128)(2,1)S(1)}, u32[]{:S(2)}, u32[]{:S(2)}) collective-permute-start(bf16[128,128]{1,0:T(8,128)(2,1)S(1)} %get-tuple-element.21.refs_0_.refs_3_), channel_id=1, source_target_pairs={{4,0},{6,2},{0,4},{2,6},{5,1},{7,3},{1,5},{3,7},{12,8},{14,10},{8,... | collective-permute-start | bytes 98312 | tf_op jit(solution)/shard_map/ppermute | solution.py:230
  16.1 3.9 %collective-permute-start = (bf16[128,128]{1,0:T(8,128)(2,1)S(1)}, bf16[128,128]{1,0:T(8,128)(2,1)S(1)}, u32[]{:S(2)}, u32[]{:S(2)}) collective-permute-start(bf16[128,128]{1,0:T(8,128)(2,1)S(1)} %get-tuple-element.21.refs_0_.refs_3_), channel_id=1, source_target_pairs={{2,0},{4,2},{6,4},{0,6},{3,1},{5,3},{7,5},{1,7},{10,8},{12,10},{14... | collective-permute-start | bytes 98312 | tf_op jit(solution)/shard_map/ppermute | solution.py:230
  20.0 1.9 %collective-permute-start.3 = (bf16[16,128,128]{2,1,0:T(8,128)(2,1)S(1)}, bf16[16,128,128]{2,1,0:T(8,128)(2,1)S(1)}, u32[]{:S(2)}, u32[]{:S(2)}) collective-permute-start(bf16[16,128,128]{2,1,0:T(8,128)(2,1)S(1)} %all-to-all-done), channel_id=1, source_target_pairs={{0,1},{1,0},{2,3},{3,2},{4,5},{5,4},{6,7},{7,6},{8,9},{9,8},{10,11... | collective-permute-start | bytes 1572872 | tf_op jit(solution)/shard_map/ppermute | solution.py:243
  42.4 6.4 %collective-permute-start.4 = (f32[128,128]{1,0:T(8,128)S(1)}, f32[128,128]{1,0:T(8,128)S(1)}, u32[]{:S(2)}, u32[]{:S(2)}) collective-permute-start(f32[128,128]{1,0:T(8,128)S(1)} %get-tuple-element.28), channel_id=1, source_target_pairs={{4,0},{6,2},{0,4},{2,6},{5,1},{7,3},{1,5},{3,7},{12,8},{14,10},{8,... | collective-permute-start | bytes 196616 | tf_op jit(solution)/shard_map/ppermute | solution.py:230
  43.5 5.8 %collective-permute-start.5 = (f32[128,128]{1,0:T(8,128)S(1)}, f32[128,128]{1,0:T(8,128)S(1)}, u32[]{:S(2)}, u32[]{:S(2)}) collective-permute-start(f32[128,128]{1,0:T(8,128)S(1)} %get-tuple-element.29), channel_id=1, source_target_pairs={{6,0},{0,2},{2,4},{4,6},{7,1},{1,3},{3,5},{5,7},{14,8},{8,10},{10,... | collective-permute-start | bytes 196616 | tf_op jit(solution)/shard_map/ppermute | solution.py:230
  44.0 5.3 %collective-permute-start.6 = (f32[128,128]{1,0:T(8,128)S(1)}, f32[128,128]{1,0:T(8,128)S(1)}, u32[]{:S(2)}, u32[]{:S(2)}) collective-permute-start(f32[128,128]{1,0:T(8,128)S(1)} %get-tuple-element.30), channel_id=1, source_target_pairs={{2,0},{4,2},{6,4},{0,6},{3,1},{5,3},{7,5},{1,7},{10,8},{12,10},{14... | collective-permute-start | bytes 196616 | tf_op jit(solution)/shard_map/ppermute | solution.py:230
  46.7 2.6 %copy-start.2 = (f32[128,128]{1,0:T(8,128)S(1)}, f32[128,128]{1,0:T(8,128)}, u32[]{:S(2)}) copy-start(f32[128,128]{1,0:T(8,128)} %x_ref.3) | copy-start | bytes 196612

commit v7 on v6

--- a/solution.py
+++ b/solution.py
@@ -214,15 +214,30 @@
                 w = w - jnp.where(mate == lane + (c + k), 2.0, 0.0)
                 weight.append(w.astype(BF16))
             total = total + dot_nn(jnp.concatenate(weight, axis=1), c_ref[c : c + CHUNK])
+    if not first:
+        out_refs[0][...] = total
+        return
+    u = u.astype(F32)
+    along = jnp.sum(u * total, axis=1, keepdims=True)
     for q, out_ref in enumerate(out_refs):
-        out_ref[...] = total[q * ROWS : (q + 1) * ROWS]
-
-
-def final_kernel(x_ref, b0, b1, b2, b3, grad_ref):
+        rows = slice(q * ROWS, (q + 1) * ROWS)
+        row = jnp.transpose(jnp.broadcast_to(along[rows], (ROWS, ROWS)))[0:1]
+        high = row.astype(BF16).astype(F32)
+        out_ref[0:ROWS] = (total[rows] - along[rows] * u[rows]).astype(BF16)
+        out_ref[ROWS:] = jnp.concatenate([high, row - high, jnp.zeros((14, ROWS), F32)], axis=0).astype(BF16)
+
+
+def final_kernel(x_ref, u_ref, b1, b2, b3, b0, grad_ref):
     x = x_ref[...]
     radius = jnp.sqrt(jnp.sum(x * x, axis=1, keepdims=True) + EPS)
     unit = x / radius
-    d = INV_TEMP * (b0[...] + b1[...] + b2[...] + b3[...])
+    d = b0[...]
+    along = jnp.zeros((16, ROWS), F32)
+    for b_ref in (b1, b2, b3):
+        d = d + b_ref[0:ROWS].astype(F32)
+        along = along + b_ref[ROWS:].astype(F32)
+    d = d + down_rows(along[0:1] + along[1:2]) * u_ref[...].astype(F32)
+    d = INV_TEMP * d
     grad_ref[...] = (d - unit * jnp.sum(unit * d, axis=1, keepdims=True)) / radius
 
 
@@ -258,13 +273,13 @@
     held = (plane, other, mates)
     b2, b1, b3, *inv = call(
         functools.partial(grads_kernel, (2, 1, 3)),
-        [block] * 3 + [sds((NCO, 1, cols)), sds((8, ROWS))],
+        [sds((ROWS + 16, ROWS), BF16)] * 3 + [sds((NCO, 1, cols)), sds((8, ROWS))],
         **work,
     )(*held, rows[2], rows[1], rows[3], got)
     b0, loss = call(functools.partial(grads_kernel, (0,)), [block, sds((1, 1))], **work)(*held, rows[0], got, *inv)
     b = {1: b1, 2: b2, 3: b3}
     b = [shift(b[r], -r) for r in (2, 1, 3)] + [b0]
-    (grad,) = call(final_kernel, [sds((ROWS, ROWS))])(proj, *b)
+    (grad,) = call(final_kernel, [sds((ROWS, ROWS))])(proj, unit, *b)
     return loss.reshape(()), grad
 
 

time: 50.4 us -> 49.9 us (0.990)
  waiting for transfers between devices: 4.79 us -> 4.17 us
    ppermute x6, waiting for transfers between devices: 3.81 us -> 3.19 us  [shift(): return lax.ppermute(x, 'z', [((k + by) % NZ, k) for k in range(NZ)])]
  transfers between devices with their start and end apart: 8 -> 8, of which waited for: 5 -> 4; matrix products, arithmetic and copies ran while one was open for 0% -> 0% of each run, Pallas kernels for 5% -> 5%
where the time goes in v7:
time: 49.9 us; the launch traced here: 49.6 us
  starting transfers between devices  18.9 us (38%)
  blocking collectives  17.5 us (35%)
  Pallas kernels  7.48 us (15%)
  waiting for transfers between devices  4.17 us (8%)
  local copies, waits for them, and re-layouts  0.9 us (2%)
  between operations  0.7 us (1%)
    all_to_all x1, blocking collectives, body(): got = lax.all_to_all(send, ALL, 0, 0, tiled=True)  17.5 us
    ppermute x6, starting transfers between devices, shift(): return lax.ppermute(x, 'z', [((k + by) % NZ, k) for k in range(NZ)])  10.8 us
    all_to_all x1, starting transfers between devices, body(): lax.all_to_all(copies, ALL, 0, 0, axis_index_groups=PLANES, tiled=True)  8.11 us
    pallas_call x6, Pallas kernels, run(): pl.pallas_call(body, out_shape=outs, in_specs=[VMEM] * len(args), out_spe...  7.48 us
    ppermute x6, waiting for transfers between devices, shift(): return lax.ppermute(x, 'z', [((k + by) % NZ, k) for k in range(NZ)])  3.19 us
  transfers between devices with their start and end apart: 8, of which 4 were waited for; matrix products, arithmetic and copies ran while one was open for 0% of the time, Pallas kernels for 5%

profile of v7, /device:TPU:0, one launch (start us, length us, event | category | flops | bytes accessed | tf_op | source)
XLA Modules:
  0.0 49.6 jit_solution(15938264124893841909)
XLA Ops:
  0.6 0.0 copy-start
  0.6 0.0 copy-start.1
  0.7 0.9 %copy-done.1 = f32[128,128]{1,0:T(8,128)S(1)} copy-done((f32[128,128]{1,0:T(8,128)S(1)}, f32[128,128]{1,0:T(8,128)}, u32[]{:S(2)}) %copy-start.1) | copy-done | bytes 65560
  1.5 0.9 %shard_map.41 = (bf16[128,128]{1,0:T(8,128)(2,1)S(1)}, bf16[16,128,128]{2,1,0:T(8,128)(2,1)}) custom-call(f32[128,128]{1,0:T(8,128)S(1)} %copy-done.1), custom_call_target="tpu_custom_call" | custom-call | tf_op jit(solution)/shard_map/pallas_call | solution.py:36
  2.5 8.1 %all-to-all-start = ((bf16[16,128,128]{2,1,0:T(8,128)(2,1)}), bf16[16,128,128]{2,1,0:T(8,128)(2,1)S(1)}, u32[]{:S(2)}, u32[]{:S(2)}) async-start(bf16[16,128,128]{2,1,0:T(8,128)(2,1)} %get-tuple-element.17), calls=%async_computation | async-start | bytes 1048576 | tf_op jit(solution)/shard_map/all_to_all | solution.py:251
  10.6 1.9 %collective-permute-start.2 = (bf16[128,128]{1,0:T(8,128)(2,1)S(1)}, bf16[128,128]{1,0:T(8,128)(2,1)S(1)}, u32[]{:S(2)}, u32[]{:S(2)}) collective-permute-start(bf16[128,128]{1,0:T(8,128)(2,1)S(1)} %get-tuple-element.21.refs_0_.refs_3_.u_ref), channel_id=1, source_target_pairs={{6,0},{0,2},{2,4},{4,6},{7,1},{1,3},{3,5},{5,7},{14,8},{8,10},{10,... | collective-permute-start | bytes 98312 | tf_op jit(solution)/shard_map/ppermute | solution.py:245
  12.5 3.6 %collective-permute-start.1 = (bf16[128,128]{1,0:T(8,128)(2,1)S(1)}, bf16[128,128]{1,0:T(8,128)(2,1)S(1)}, u32[]{:S(2)}, u32[]{:S(2)}) collective-permute-start(bf16[128,128]{1,0:T(8,128)(2,1)S(1)} %get-tuple-element.21.refs_0_.refs_3_.u_ref), channel_id=1, source_target_pairs={{4,0},{6,2},{0,4},{2,6},{5,1},{7,3},{1,5},{3,7},{12,8},{14,10},{8,... | collective-permute-start | bytes 98312 | tf_op jit(solution)/shard_map/ppermute | solution.py:245
  16.1 1.0 %collective-permute-start = (bf16[128,128]{1,0:T(8,128)(2,1)S(1)}, bf16[128,128]{1,0:T(8,128)(2,1)S(1)}, u32[]{:S(2)}, u32[]{:S(2)}) collective-permute-start(bf16[128,128]{1,0:T(8,128)(2,1)S(1)} %get-tuple-element.21.refs_0_.refs_3_.u_ref), channel_id=1, source_target_pairs={{2,0},{4,2},{6,4},{0,6},{3,1},{5,3},{7,5},{1,7},{10,8},{12,10},{14... | collective-permute-start | bytes 98312 | tf_op jit(solution)/shard_map/ppermute | solution.py:245
  17.1 0.0 copy-done
  17.1 0.0 collective-permute-done.2.refs_3_.refs_5_
  17.1 1.2 %collective-permute-done.1.refs_2_.refs_3_ = bf16[128,128]{1,0:T(8,128)(2,1)S(1)} collective-permute-done((bf16[128,128]{1,0:T(8,128)(2,1)S(1)}, bf16[128,128]{1,0:T(8,128)(2,1)S(1)}, u32[]{:S(2)}, u32[]{:S(2)}) %collective-permute-start.1) | collective-permute-done | bytes 32800 | tf_op jit(solution)/shard_map/ppermute | solution.py:245
  18.3 1.7 %collective-permute-done.refs_1_.refs_4_ = bf16[128,128]{1,0:T(8,128)(2,1)S(1)} collective-permute-done((bf16[128,128]{1,0:T(8,128)(2,1)S(1)}, bf16[128,128]{1,0:T(8,128)(2,1)S(1)}, u32[]{:S(2)}, u32[]{:S(2)}) %collective-permute-start) | collective-permute-done | bytes 32800 | tf_op jit(solution)/shard_map/ppermute | solution.py:245
  20.0 0.0 all-to-all-done
  20.0 0.0 collective-permute-start.3
  20.0 0.9 %shard_map.42.refs_6_ = f32[8,128]{1,0:T(8,128)S(1)} custom-call(bf16[128,128]{1,0:T(8,128)(2,1)S(1)} %get-tuple-element.21.refs_0_.refs_3_.u_ref, bf16[128,128]{1,0:T(8,128)(2,1)S(1)} %collective-permute-done.refs_1_.refs_4_, bf16[128,128]{1,0:T(8,128)(2,1)S(1)} %collective-permute-done.1.refs_2_.refs_3_, ...), custom_call_target="tpu_custom_call" | custom-call | flops 268435456 | bytes 1048576 | tf_op jit(solution)/shard_map/pallas_call | solution.py:36
  20.9 1.0 %collective-permute-done.3 = bf16[16,128,128]{2,1,0:T(8,128)(2,1)S(1)} collective-permute-done((bf16[16,128,128]{2,1,0:T(8,128)(2,1)S(1)}, bf16[16,128,128]{2,1,0:T(8,128)(2,1)S(1)}, u32[]{:S(2)}, u32[]{:S(2)}) %collective-permute-start.3) | collective-permute-done | bytes 524320 | tf_op jit(solution)/shard_map/ppermute | solution.py:258
  21.9 0.9 %shard_map.43 = bf16[128,2,384]{2,1,0:T(2,128)(2,1)S(1)} custom-call(bf16[128,128]{1,0:T(8,128)(2,1)S(1)} %get-tuple-element.21.refs_0_.refs_3_.u_ref, bf16[128,128]{1,0:T(8,128)(2,1)S(1)} %collective-permute-done.refs_1_.refs_4_, bf16[128,128]{1,0:T(8,128)(2,1)S(1)} %collective-permute-done.1.refs_2_.refs_3_, ...), custom_call_target="tpu_custom_call" | custom-call | flops 268435456 | bytes 1048576 | tf_op jit(solution)/shard_map/pallas_call | solution.py:36
  22.8 17.5 %all_to_all.10.refs_6_.refs_4_ = bf16[128,2,384]{2,1,0:T(2,128)(2,1)S(1)} all-to-all(bf16[128,2,384]{2,1,0:T(2,128)(2,1)S(1)} %shard_map.43), channel_id=1, replica_groups=mesh['y'=4,'xh'=2,'xl'=2,'z'=4,'co'=2] {'y','xh','xl','z','co'}, dimensions={0} | all-to-all | bytes 393216 | tf_op jit(solution)/shard_map/all_to_all | solution.py:270
  40.2 2.3 %shard_map.44 = (bf16[144,128]{1,0:T(8,128)(2,1)S(1)}, bf16[144,128]{1,0:T(8,128)(2,1)S(1)}, bf16[144,128]{1,0:T(8,128)(2,1)S(1)}, f32[2,1,2048]{2,1,0:T(1,128)S(1)}, f32[8,128]{1,0:T(8,128)S(1)}) custom-call(bf16[2048,128]{1,0:T(8,128)(2,1)S(1)} %bitcast.7, bf16[2048,128]{1,0:T(8,128)(2,1)S(1)} %bitcast.10, ...), custom_call_target="tpu_custom_call" | custom-call | flops 805306368 | bytes 1048576 | tf_op jit(solution)/shard_map/pallas_call | solution.py:36
  42.5 1.1 %collective-permute-start.4 = (bf16[144,128]{1,0:T(8,128)(2,1)S(1)}, bf16[144,128]{1,0:T(8,128)(2,1)S(1)}, u32[]{:S(2)}, u32[]{:S(2)}) collective-permute-start(bf16[144,128]{1,0:T(8,128)(2,1)S(1)} %get-tuple-element.28), channel_id=1, source_target_pairs={{4,0},{6,2},{0,4},{2,6},{5,1},{7,3},{1,5},{3,7},{12,8},{14,10},{8,... | collective-permute-start | bytes 110600 | tf_op jit(solution)/shard_map/ppermute | solution.py:245
  43.6 0.5 %collective-permute-start.5 = (bf16[144,128]{1,0:T(8,128)(2,1)S(1)}, bf16[144,128]{1,0:T(8,128)(2,1)S(1)}, u32[]{:S(2)}, u32[]{:S(2)}) collective-permute-start(bf16[144,128]{1,0:T(8,128)(2,1)S(1)} %get-tuple-element.29), channel_id=1, source_target_pairs={{6,0},{0,2},{2,4},{4,6},{7,1},{1,3},{3,5},{5,7},{14,8},{8,10},{10,... | collective-permute-start | bytes 110600 | tf_op jit(solution)/shard_map/ppermute | solution.py:245
  44.1 2.7 %collective-permute-start.6 = (bf16[144,128]{1,0:T(8,128)(2,1)S(1)}, bf16[144,128]{1,0:T(8,128)(2,1)S(1)}, u32[]{:S(2)}, u32[]{:S(2)}) collective-permute-start(bf16[144,128]{1,0:T(8,128)(2,1)S(1)} %get-tuple-element.30), channel_id=1, source_target_pairs={{2,0},{4,2},{6,4},{0,6},{3,1},{5,3},{7,5},{1,7},{10,8},{12,10},{14... | collective-permute-start | bytes 110600 | tf_op jit(solution)/shard_map/ppermute | solution.py:245
  46.8 0.0 copy-start.2
  46.8 1.6 %shard_map.45 = (f32[128,128]{1,0:T(8,128)S(1)}, f32[1,1]{1,0:T(1,128)}) custom-call(bf16[2048,128]{1,0:T(8,128)(2,1)S(1)} %bitcast.8, bf16[2048,128]{1,0:T(8,128)(2,1)S(1)} %bitcast.11, s32[4,128]{1,0:T(4,128)S(1)} %constant_dynamic-slice_fusion.refs_5_.refs_2_, bf16[128,128]{1,0:T(8,128)(2,1)S(1)} %get-tuple-element.21.refs_0_.refs_3_.u_ref, ...), custom_call_target="tpu_custom_call" | custom-call | flops 805306368 | bytes 1048576 | tf_op jit(solution)/shard_map/pallas_call | solution.py:36
  48.4 0.0 collective-permute-done.4.b1
  48.4 0.3 collective-permute-done.5.b2
  48.8 0.0 collective-permute-done.6.b3
  48.8 0.0 copy-done.2
  48.8 0.9 %shard_map.46 = f32[128,128]{1,0:T(8,128)} custom-call(f32[128,128]{1,0:T(8,128)S(1)} %copy-done.2, bf16[128,128]{1,0:T(8,128)(2,1)S(1)} %get-tuple-element.21.refs_0_.refs_3_.u_ref, bf16[144,128]{1,0:T(8,128)(2,1)S(1)} %collective-permute-done.4.b1, bf16[144,128]{1,0:T(8,128)(2,1)S(1)} %collective-permute-done.5.b2, ...), custom_call_target="tpu_custom_call" | custom-call | tf_op jit(solution)/shard_map/pallas_call | solution.py:36
  (3 shorter events, 0.0 us)
Async XLA Ops:
  0.6 16.5 %copy-start = (s32[16384]{0:T(1024)S(1)}, s32[16384]{0:T(1024)}, u32[]{:S(2)}) copy-start(s32[16384]{0:T(1024)} %param.3) | copy-start | bytes 196612
  0.6 0.9 %copy-start.1 = (f32[128,128]{1,0:T(8,128)S(1)}, f32[128,128]{1,0:T(8,128)}, u32[]{:S(2)}) copy-start(f32[128,128]{1,0:T(8,128)} %x_ref.3) | copy-start | bytes 196612
  2.5 17.5 %all-to-all-start = ((bf16[16,128,128]{2,1,0:T(8,128)(2,1)}), bf16[16,128,128]{2,1,0:T(8,128)(2,1)S(1)}, u32[]{:S(2)}, u32[]{:S(2)}) async-start(bf16[16,128,128]{2,1,0:T(8,128)(2,1)} %get-tuple-element.17), calls=%async_computation | async-start | bytes 1048576 | tf_op jit(solution)/shard_map/all_to_all | solution.py:251
  10.6 6.6 %collective-permute-start.2 = (bf16[128,128]{1,0:T(8,128)(2,1)S(1)}, bf16[128,128]{1,0:T(8,128)(2,1)S(1)}, u32[]{:S(2)}, u32[]{:S(2)}) collective-permute-start(bf16[128,128]{1,0:T(8,128)(2,1)S(1)} %get-tuple-element.21.refs_0_.refs_3_.u_ref), channel_id=1, source_target_pairs={{6,0},{0,2},{2,4},{4,6},{7,1},{1,3},{3,5},{5,7},{14,8},{8,10},{10,... | collective-permute-start | bytes 98312 | tf_op jit(solution)/shard_map/ppermute | solution.py:245
  12.5 5.8 %collective-permute-start.1 = (bf16[128,128]{1,0:T(8,128)(2,1)S(1)}, bf16[128,128]{1,0:T(8,128)(2,1)S(1)}, u32[]{:S(2)}, u32[]{:S(2)}) collective-permute-start(bf16[128,128]{1,0:T(8,128)(2,1)S(1)} %get-tuple-element.21.refs_0_.refs_3_.u_ref), channel_id=1, source_target_pairs={{4,0},{6,2},{0,4},{2,6},{5,1},{7,3},{1,5},{3,7},{12,8},{14,10},{8,... | collective-permute-start | bytes 98312 | tf_op jit(solution)/shard_map/ppermute | solution.py:245
  16.1 3.9 %collective-permute-start = (bf16[128,128]{1,0:T(8,128)(2,1)S(1)}, bf16[128,128]{1,0:T(8,128)(2,1)S(1)}, u32[]{:S(2)}, u32[]{:S(2)}) collective-permute-start(bf16[128,128]{1,0:T(8,128)(2,1)S(1)} %get-tuple-element.21.refs_0_.refs_3_.u_ref), channel_id=1, source_target_pairs={{2,0},{4,2},{6,4},{0,6},{3,1},{5,3},{7,5},{1,7},{10,8},{12,10},{14... | collective-permute-start | bytes 98312 | tf_op jit(solution)/shard_map/ppermute | solution.py:245
  20.0 1.9 %collective-permute-start.3 = (bf16[16,128,128]{2,1,0:T(8,128)(2,1)S(1)}, bf16[16,128,128]{2,1,0:T(8,128)(2,1)S(1)}, u32[]{:S(2)}, u32[]{:S(2)}) collective-permute-start(bf16[16,128,128]{2,1,0:T(8,128)(2,1)S(1)} %all-to-all-done), channel_id=1, source_target_pairs={{0,1},{1,0},{2,3},{3,2},{4,5},{5,4},{6,7},{7,6},{8,9},{9,8},{10,11... | collective-permute-start | bytes 1572872 | tf_op jit(solution)/shard_map/ppermute | solution.py:258
  42.5 5.9 %collective-permute-start.4 = (bf16[144,128]{1,0:T(8,128)(2,1)S(1)}, bf16[144,128]{1,0:T(8,128)(2,1)S(1)}, u32[]{:S(2)}, u32[]{:S(2)}) collective-permute-start(bf16[144,128]{1,0:T(8,128)(2,1)S(1)} %get-tuple-element.28), channel_id=1, source_target_pairs={{4,0},{6,2},{0,4},{2,6},{5,1},{7,3},{1,5},{3,7},{12,8},{14,10},{8,... | collective-permute-start | bytes 110600 | tf_op jit(solution)/shard_map/ppermute | solution.py:245
  43.6 5.2 %collective-permute-start.5 = (bf16[144,128]{1,0:T(8,128)(2,1)S(1)}, bf16[144,128]{1,0:T(8,128)(2,1)S(1)}, u32[]{:S(2)}, u32[]{:S(2)}) collective-permute-start(bf16[144,128]{1,0:T(8,128)(2,1)S(1)} %get-tuple-element.29), channel_id=1, source_target_pairs={{6,0},{0,2},{2,4},{4,6},{7,1},{1,3},{3,5},{5,7},{14,8},{8,10},{10,... | collective-permute-start | bytes 110600 | tf_op jit(solution)/shard_map/ppermute | solution.py:245
  44.1 4.6 %collective-permute-start.6 = (bf16[144,128]{1,0:T(8,128)(2,1)S(1)}, bf16[144,128]{1,0:T(8,128)(2,1)S(1)}, u32[]{:S(2)}, u32[]{:S(2)}) collective-permute-start(bf16[144,128]{1,0:T(8,128)(2,1)S(1)} %get-tuple-element.30), channel_id=1, source_target_pairs={{2,0},{4,2},{6,4},{0,6},{3,1},{5,3},{7,5},{1,7},{10,8},{12,10},{14... | collective-permute-start | bytes 110600 | tf_op jit(solution)/shard_map/ppermute | solution.py:245
  46.8 1.9 %copy-start.2 = (f32[128,128]{1,0:T(8,128)S(1)}, f32[128,128]{1,0:T(8,128)}, u32[]{:S(2)}) copy-start(f32[128,128]{1,0:T(8,128)} %x_ref.3) | copy-start | bytes 196612

commit v8 on v7

--- a/solution.py
+++ b/solution.py
@@ -160,10 +160,12 @@
     if first:
         out_refs = refs[4 + n : 4 + 2 * n]
         inv_ref, aux_ref = refs[4 + 2 * n :]
+        logs = jnp.zeros((2, ROWS), F32)
         for k in range(NXY):
             for c in range(NCO):
                 got = [got_ref[k * 8 + q * 2 + c, :, 0:ROWS].astype(F32) for q in range(NZ)]
                 total = got[0] + got[1] + (got[2] + got[3])
+                logs = logs + jnp.log(total)
                 at = slot(k, c) * ROWS
                 inv_ref[c, :, at : at + ROWS] = 1.0 / total[0:1]
         got = [got_ref[xy * 8 + q * 2 + co, :, 0 : 2 * ROWS].astype(F32) for q in range(NZ)]
@@ -171,27 +173,17 @@
         for r in range(NZ):
             part = total[r // 2 : r // 2 + 1, r % 2 * ROWS : (r % 2 + 1) * ROWS]
             aux_ref[r : r + 1] = 1.0 / part
-        aux_ref[NZ:] = jnp.zeros((8 - NZ, ROWS), F32)
+        logs_high = logs[0:1].astype(BF16).astype(F32)
+        logs_low = (logs[0:1] - logs_high).astype(BF16).astype(F32)
+        aux_ref[NZ : NZ + 1] = logs_high
+        aux_ref[NZ + 1 : NZ + 2] = logs_low
+        aux_ref[NZ + 2 :] = jnp.zeros((6 - NZ, ROWS), F32)
     else:
-        inv_ref, aux_ref, *out_refs, loss_ref = refs[4 + n :]
-        logs = jnp.zeros((2, 2 * ROWS), F32)
+        inv_ref, aux_ref, *out_refs, pos_ref = refs[4 + n :]
         pos = jnp.zeros((2, ROWS), F32)
-        for k in range(NXY):
-            for c in range(NCO):
-                got = [got_ref[k * 8 + q * 2 + c].astype(F32) for q in range(NZ)]
-                got = got[0] + got[1] + (got[2] + got[3])
-                pos = pos + got[:, 2 * ROWS :]
-                logs = logs + jnp.log(got[:, : 2 * ROWS])
-        pos = jnp.sum(pos, axis=0, keepdims=True)
-        parts = [logs[r // 2 : r // 2 + 1, r % 2 * ROWS : (r % 2 + 1) * ROWS] for r in range(NZ)]
-        loss = -pos
-        for k in range(NZ):
-            r = lax.rem(k - z + NZ, NZ)
-            row = parts[0]
-            for q in range(1, NZ):
-                row = jnp.where(r == q, parts[q], row)
-            loss = loss + row
-        loss_ref[...] = jnp.sum(loss, axis=1, keepdims=True) / VIEWS
+        for k in range(NDEV):
+            pos = pos + got_ref[k, :, 2 * ROWS :].astype(F32)
+        pos_ref[...] = jnp.sum(pos, axis=0, keepdims=True)
     own = slot(xy, co)
     inv_row = jnp.concatenate([down_rows(aux_ref[r : r + 1]) for r in blocks], axis=0)
     mates = mate_ref[...]
@@ -224,21 +216,35 @@
         row = jnp.transpose(jnp.broadcast_to(along[rows], (ROWS, ROWS)))[0:1]
         high = row.astype(BF16).astype(F32)
         out_ref[0:ROWS] = (total[rows] - along[rows] * u[rows]).astype(BF16)
-        out_ref[ROWS:] = jnp.concatenate([high, row - high, jnp.zeros((14, ROWS), F32)], axis=0).astype(BF16)
-
-
-def final_kernel(x_ref, u_ref, b1, b2, b3, b0, grad_ref):
+        out_ref[ROWS:] = jnp.concatenate(
+            [high, row - high, logs_high, logs_low, jnp.zeros((12, ROWS), F32)], axis=0
+        ).astype(BF16)
+
+
+def final_kernel(x_ref, u_ref, aux_ref, pos_ref, b2, b1, b3, b0, loss_ref, grad_ref):
+    z = position()[0]
     x = x_ref[...]
     radius = jnp.sqrt(jnp.sum(x * x, axis=1, keepdims=True) + EPS)
     unit = x / radius
     d = b0[...]
-    along = jnp.zeros((16, ROWS), F32)
+    along = jnp.zeros((1, ROWS), F32)
+    logs = [aux_ref[NZ : NZ + 1] + aux_ref[NZ + 1 : NZ + 2]]
     for b_ref in (b1, b2, b3):
         d = d + b_ref[0:ROWS].astype(F32)
-        along = along + b_ref[ROWS:].astype(F32)
-    d = d + down_rows(along[0:1] + along[1:2]) * u_ref[...].astype(F32)
+        tail = b_ref[ROWS:].astype(F32)
+        along = along + (tail[0:1] + tail[1:2])
+        logs.append(tail[2:3] + tail[3:4])
+    d = d + down_rows(along) * u_ref[...].astype(F32)
     d = INV_TEMP * d
     grad_ref[...] = (d - unit * jnp.sum(unit * d, axis=1, keepdims=True)) / radius
+    loss = -pos_ref[...]
+    for k in range(NZ):
+        r = lax.rem(z - k + NZ, NZ)
+        row = logs[0]
+        for q in range(1, NZ):
+            row = jnp.where(r == q, logs[q], row)
+        loss = loss + row
+    loss_ref[...] = jnp.sum(loss, axis=1, keepdims=True) / VIEWS
 
 
 def shift(x, by):
@@ -276,10 +282,10 @@
         [sds((ROWS + 16, ROWS), BF16)] * 3 + [sds((NCO, 1, cols)), sds((8, ROWS))],
         **work,
     )(*held, rows[2], rows[1], rows[3], got)
-    b0, loss = call(functools.partial(grads_kernel, (0,)), [block, sds((1, 1))], **work)(*held, rows[0], got, *inv)
+    b0, pos = call(functools.partial(grads_kernel, (0,)), [block, sds((1, ROWS))], **work)(*held, rows[0], got, *inv)
     b = {1: b1, 2: b2, 3: b3}
     b = [shift(b[r], -r) for r in (2, 1, 3)] + [b0]
-    (grad,) = call(final_kernel, [sds((ROWS, ROWS))])(proj, unit, *b)
+    loss, grad = call(final_kernel, [sds((1, 1)), sds((ROWS, ROWS))])(proj, unit, inv[1], pos, *b)
     return loss.reshape(()), grad
 
 

time: 49.9 us -> 49.9 us (level)
  Pallas kernels: 7.48 us -> 6.92 us
  waiting for transfers between devices: 4.17 us -> 4.7 us
    pallas_call x6, Pallas kernels: 7.48 us -> 6.92 us  [run(): pl.pallas_call(body, out_shape=outs, in_specs=[VMEM] * len(args), out_spe...]
    ppermute x6, waiting for transfers between devices: 3.19 us -> 3.72 us  [shift(): return lax.ppermute(x, 'z', [((k + by) % NZ, k) for k in range(NZ)])]
  transfers between devices with their start and end apart: 8 -> 8, of which waited for: 4 -> 5; matrix products, arithmetic and copies ran while one was open for 0% -> 0% of each run, Pallas kernels for 5% -> 4%
where the time goes in v8:
time: 49.9 us; the launch traced here: 49.6 us
  starting transfers between devices  18.9 us (38%)
  blocking collectives  17.5 us (35%)
  Pallas kernels  6.92 us (14%)
  waiting for transfers between devices  4.7 us (9%)
  local copies, waits for them, and re-layouts  0.9 us (2%)
  between operations  0.7 us (1%)
    all_to_all x1, blocking collectives, body(): got = lax.all_to_all(send, ALL, 0, 0, tiled=True)  17.5 us
    ppermute x6, starting transfers between devices, shift(): return lax.ppermute(x, 'z', [((k + by) % NZ, k) for k in range(NZ)])  10.8 us
    all_to_all x1, starting transfers between devices, body(): lax.all_to_all(copies, ALL, 0, 0, axis_index_groups=PLANES, tiled=True)  8.11 us
    pallas_call x6, Pallas kernels, run(): pl.pallas_call(body, out_shape=outs, in_specs=[VMEM] * len(args), out_spe...  6.92 us
    ppermute x6, waiting for transfers between devices, shift(): return lax.ppermute(x, 'z', [((k + by) % NZ, k) for k in range(NZ)])  3.72 us
  transfers between devices with their start and end apart: 8, of which 5 were waited for; matrix products, arithmetic and copies ran while one was open for 0% of the time, Pallas kernels for 4%

profile of v8, /device:TPU:0, one launch (start us, length us, event | category | flops | bytes accessed | tf_op | source)
XLA Modules:
  0.0 49.6 jit_solution(12969520300555548598)
XLA Ops:
  0.6 0.0 copy-start
  0.6 0.0 copy-start.1
  0.7 0.9 %copy-done.1 = f32[128,128]{1,0:T(8,128)S(1)} copy-done((f32[128,128]{1,0:T(8,128)S(1)}, f32[128,128]{1,0:T(8,128)}, u32[]{:S(2)}) %copy-start.1) | copy-done | bytes 65560
  1.5 0.9 %shard_map.41 = (bf16[128,128]{1,0:T(8,128)(2,1)S(1)}, bf16[16,128,128]{2,1,0:T(8,128)(2,1)}) custom-call(f32[128,128]{1,0:T(8,128)S(1)} %copy-done.1), custom_call_target="tpu_custom_call" | custom-call | tf_op jit(solution)/shard_map/pallas_call | solution.py:36
  2.5 8.1 %all-to-all-start = ((bf16[16,128,128]{2,1,0:T(8,128)(2,1)}), bf16[16,128,128]{2,1,0:T(8,128)(2,1)S(1)}, u32[]{:S(2)}, u32[]{:S(2)}) async-start(bf16[16,128,128]{2,1,0:T(8,128)(2,1)} %get-tuple-element.20), calls=%async_computation | async-start | bytes 1048576 | tf_op jit(solution)/shard_map/all_to_all | solution.py:257
  10.6 1.9 %collective-permute-start.2 = (bf16[128,128]{1,0:T(8,128)(2,1)S(1)}, bf16[128,128]{1,0:T(8,128)(2,1)S(1)}, u32[]{:S(2)}, u32[]{:S(2)}) collective-permute-start(bf16[128,128]{1,0:T(8,128)(2,1)S(1)} %get-tuple-element.26.refs_0_.refs_3_.u_ref), channel_id=1, source_target_pairs={{6,0},{0,2},{2,4},{4,6},{7,1},{1,3},{3,5},{5,7},{14,8},{8,10},{10,... | collective-permute-start | bytes 98312 | tf_op jit(solution)/shard_map/ppermute | solution.py:251
  12.5 3.6 %collective-permute-start.1 = (bf16[128,128]{1,0:T(8,128)(2,1)S(1)}, bf16[128,128]{1,0:T(8,128)(2,1)S(1)}, u32[]{:S(2)}, u32[]{:S(2)}) collective-permute-start(bf16[128,128]{1,0:T(8,128)(2,1)S(1)} %get-tuple-element.26.refs_0_.refs_3_.u_ref), channel_id=1, source_target_pairs={{4,0},{6,2},{0,4},{2,6},{5,1},{7,3},{1,5},{3,7},{12,8},{14,10},{8,... | collective-permute-start | bytes 98312 | tf_op jit(solution)/shard_map/ppermute | solution.py:251
  16.1 1.0 %collective-permute-start = (bf16[128,128]{1,0:T(8,128)(2,1)S(1)}, bf16[128,128]{1,0:T(8,128)(2,1)S(1)}, u32[]{:S(2)}, u32[]{:S(2)}) collective-permute-start(bf16[128,128]{1,0:T(8,128)(2,1)S(1)} %get-tuple-element.26.refs_0_.refs_3_.u_ref), channel_id=1, source_target_pairs={{2,0},{4,2},{6,4},{0,6},{3,1},{5,3},{7,5},{1,7},{10,8},{12,10},{14... | collective-permute-start | bytes 98312 | tf_op jit(solution)/shard_map/ppermute | solution.py:251
  17.1 0.0 copy-done
  17.1 0.0 collective-permute-done.2.refs_3_.refs_5_
  17.1 1.2 %collective-permute-done.1.refs_2_.refs_3_ = bf16[128,128]{1,0:T(8,128)(2,1)S(1)} collective-permute-done((bf16[128,128]{1,0:T(8,128)(2,1)S(1)}, bf16[128,128]{1,0:T(8,128)(2,1)S(1)}, u32[]{:S(2)}, u32[]{:S(2)}) %collective-permute-start.1) | collective-permute-done | bytes 32800 | tf_op jit(solution)/shard_map/ppermute | solution.py:251
  18.3 1.7 %collective-permute-done.refs_1_.refs_4_ = bf16[128,128]{1,0:T(8,128)(2,1)S(1)} collective-permute-done((bf16[128,128]{1,0:T(8,128)(2,1)S(1)}, bf16[128,128]{1,0:T(8,128)(2,1)S(1)}, u32[]{:S(2)}, u32[]{:S(2)}) %collective-permute-start) | collective-permute-done | bytes 32800 | tf_op jit(solution)/shard_map/ppermute | solution.py:251
  20.0 0.0 all-to-all-done
  20.0 0.0 collective-permute-start.3
  20.0 0.9 %shard_map.42.refs_6_ = f32[8,128]{1,0:T(8,128)S(1)} custom-call(bf16[128,128]{1,0:T(8,128)(2,1)S(1)} %get-tuple-element.26.refs_0_.refs_3_.u_ref, bf16[128,128]{1,0:T(8,128)(2,1)S(1)} %collective-permute-done.refs_1_.refs_4_, bf16[128,128]{1,0:T(8,128)(2,1)S(1)} %collective-permute-done.1.refs_2_.refs_3_, ...), custom_call_target="tpu_custom_call" | custom-call | flops 268435456 | bytes 1048576 | tf_op jit(solution)/shard_map/pallas_call | solution.py:36
  20.9 1.0 %collective-permute-done.3 = bf16[16,128,128]{2,1,0:T(8,128)(2,1)S(1)} collective-permute-done((bf16[16,128,128]{2,1,0:T(8,128)(2,1)S(1)}, bf16[16,128,128]{2,1,0:T(8,128)(2,1)S(1)}, u32[]{:S(2)}, u32[]{:S(2)}) %collective-permute-start.3) | collective-permute-done | bytes 524320 | tf_op jit(solution)/shard_map/ppermute | solution.py:264
  21.9 0.9 %shard_map.43 = bf16[128,2,384]{2,1,0:T(2,128)(2,1)S(1)} custom-call(bf16[128,128]{1,0:T(8,128)(2,1)S(1)} %get-tuple-element.26.refs_0_.refs_3_.u_ref, bf16[128,128]{1,0:T(8,128)(2,1)S(1)} %collective-permute-done.refs_1_.refs_4_, bf16[128,128]{1,0:T(8,128)(2,1)S(1)} %collective-permute-done.1.refs_2_.refs_3_, ...), custom_call_target="tpu_custom_call" | custom-call | flops 268435456 | bytes 1048576 | tf_op jit(solution)/shard_map/pallas_call | solution.py:36
  22.8 17.5 %all_to_all.10.refs_6_.refs_4_ = bf16[128,2,384]{2,1,0:T(2,128)(2,1)S(1)} all-to-all(bf16[128,2,384]{2,1,0:T(2,128)(2,1)S(1)} %shard_map.43), channel_id=1, replica_groups=mesh['y'=4,'xh'=2,'xl'=2,'z'=4,'co'=2] {'y','xh','xl','z','co'}, dimensions={0} | all-to-all | bytes 393216 | tf_op jit(solution)/shard_map/all_to_all | solution.py:276
  40.2 2.3 %shard_map.44 = (bf16[144,128]{1,0:T(8,128)(2,1)S(1)}, bf16[144,128]{1,0:T(8,128)(2,1)S(1)}, bf16[144,128]{1,0:T(8,128)(2,1)S(1)}, f32[2,1,2048]{2,1,0:T(1,128)S(1)}, f32[8,128]{1,0:T(8,128)S(1)}) custom-call(bf16[2048,128]{1,0:T(8,128)(2,1)S(1)} %bitcast.7, bf16[2048,128]{1,0:T(8,128)(2,1)S(1)} %bitcast.10, ...), custom_call_target="tpu_custom_call" | custom-call | flops 805306368 | bytes 1048576 | tf_op jit(solution)/shard_map/pallas_call | solution.py:36
  42.5 1.1 %collective-permute-start.4 = (bf16[144,128]{1,0:T(8,128)(2,1)S(1)}, bf16[144,128]{1,0:T(8,128)(2,1)S(1)}, u32[]{:S(2)}, u32[]{:S(2)}) collective-permute-start(bf16[144,128]{1,0:T(8,128)(2,1)S(1)} %get-tuple-element.30), channel_id=1, source_target_pairs={{4,0},{6,2},{0,4},{2,6},{5,1},{7,3},{1,5},{3,7},{12,8},{14,10},{8,... | collective-permute-start | bytes 110600 | tf_op jit(solution)/shard_map/ppermute | solution.py:251
  43.6 0.5 %collective-permute-start.5 = (bf16[144,128]{1,0:T(8,128)(2,1)S(1)}, bf16[144,128]{1,0:T(8,128)(2,1)S(1)}, u32[]{:S(2)}, u32[]{:S(2)}) collective-permute-start(bf16[144,128]{1,0:T(8,128)(2,1)S(1)} %get-tuple-element.31), channel_id=1, source_target_pairs={{6,0},{0,2},{2,4},{4,6},{7,1},{1,3},{3,5},{5,7},{14,8},{8,10},{10,... | collective-permute-start | bytes 110600 | tf_op jit(solution)/shard_map/ppermute | solution.py:251
  44.1 2.7 %collective-permute-start.6 = (bf16[144,128]{1,0:T(8,128)(2,1)S(1)}, bf16[144,128]{1,0:T(8,128)(2,1)S(1)}, u32[]{:S(2)}, u32[]{:S(2)}) collective-permute-start(bf16[144,128]{1,0:T(8,128)(2,1)S(1)} %get-tuple-element.32), channel_id=1, source_target_pairs={{2,0},{4,2},{6,4},{0,6},{3,1},{5,3},{7,5},{1,7},{10,8},{12,10},{14... | collective-permute-start | bytes 110600 | tf_op jit(solution)/shard_map/ppermute | solution.py:251
  46.8 0.0 copy-start.2
  46.8 1.1 %shard_map.45 = (f32[128,128]{1,0:T(8,128)S(1)}, f32[1,128]{1,0:T(1,128)S(1)}) custom-call(bf16[2048,128]{1,0:T(8,128)(2,1)S(1)} %bitcast.8, bf16[2048,128]{1,0:T(8,128)(2,1)S(1)} %bitcast.11, s32[4,128]{1,0:T(4,128)S(1)} %constant_dynamic-slice_fusion.refs_5_.refs_2_, bf16[128,128]{1,0:T(8,128)(2,1)S(1)} %get-tuple-element.26.refs_0_.refs_3_.u_ref, ...), custom_call_target="tpu_custom_call" | custom-call | flops 805306368 | bytes 1048576 | tf_op jit(solution)/shard_map/pallas_call | solution.py:36
  47.9 0.3 collective-permute-done.4.b2
  48.2 0.6 %collective-permute-done.5.b1 = bf16[144,128]{1,0:T(8,128)(2,1)S(1)} collective-permute-done((bf16[144,128]{1,0:T(8,128)(2,1)S(1)}, bf16[144,128]{1,0:T(8,128)(2,1)S(1)}, u32[]{:S(2)}, u32[]{:S(2)}) %collective-permute-start.5) | collective-permute-done | bytes 36896 | tf_op jit(solution)/shard_map/ppermute | solution.py:251
  48.7 0.0 collective-permute-done.6.b3
  48.7 0.0 copy-done.2
  48.8 0.9 %shard_map.46 = (f32[1,1]{1,0:T(1,128)}, f32[128,128]{1,0:T(8,128)}) custom-call(f32[128,128]{1,0:T(8,128)S(1)} %copy-done.2, bf16[128,128]{1,0:T(8,128)(2,1)S(1)} %get-tuple-element.26.refs_0_.refs_3_.u_ref, f32[8,128]{1,0:T(8,128)S(1)} %get-tuple-element.27.refs_6_.aux_ref, f32[1,128]{1,0:T(1,128)S(1)} %get-tuple-element.29.pos_ref, ...), custom_call_target="tpu_custom_call" | custom-call | tf_op jit(solution)/shard_map/pallas_call | solution.py:36
  (3 shorter events, 0.0 us)
Async XLA Ops:
  0.6 16.5 %copy-start = (s32[16384]{0:T(1024)S(1)}, s32[16384]{0:T(1024)}, u32[]{:S(2)}) copy-start(s32[16384]{0:T(1024)} %param.3) | copy-start | bytes 196612
  0.6 0.9 %copy-start.1 = (f32[128,128]{1,0:T(8,128)S(1)}, f32[128,128]{1,0:T(8,128)}, u32[]{:S(2)}) copy-start(f32[128,128]{1,0:T(8,128)} %x_ref.3) | copy-start | bytes 196612
  2.5 17.5 %all-to-all-start = ((bf16[16,128,128]{2,1,0:T(8,128)(2,1)}), bf16[16,128,128]{2,1,0:T(8,128)(2,1)S(1)}, u32[]{:S(2)}, u32[]{:S(2)}) async-start(bf16[16,128,128]{2,1,0:T(8,128)(2,1)} %get-tuple-element.20), calls=%async_computation | async-start | bytes 1048576 | tf_op jit(solution)/shard_map/all_to_all | solution.py:257
  10.6 6.6 %collective-permute-start.2 = (bf16[128,128]{1,0:T(8,128)(2,1)S(1)}, bf16[128,128]{1,0:T(8,128)(2,1)S(1)}, u32[]{:S(2)}, u32[]{:S(2)}) collective-permute-start(bf16[128,128]{1,0:T(8,128)(2,1)S(1)} %get-tuple-element.26.refs_0_.refs_3_.u_ref), channel_id=1, source_target_pairs={{6,0},{0,2},{2,4},{4,6},{7,1},{1,3},{3,5},{5,7},{14,8},{8,10},{10,... | collective-permute-start | bytes 98312 | tf_op jit(solution)/shard_map/ppermute | solution.py:251
  12.5 5.8 %collective-permute-start.1 = (bf16[128,128]{1,0:T(8,128)(2,1)S(1)}, bf16[128,128]{1,0:T(8,128)(2,1)S(1)}, u32[]{:S(2)}, u32[]{:S(2)}) collective-permute-start(bf16[128,128]{1,0:T(8,128)(2,1)S(1)} %get-tuple-element.26.refs_0_.refs_3_.u_ref), channel_id=1, source_target_pairs={{4,0},{6,2},{0,4},{2,6},{5,1},{7,3},{1,5},{3,7},{12,8},{14,10},{8,... | collective-permute-start | bytes 98312 | tf_op jit(solution)/shard_map/ppermute | solution.py:251
  16.1 3.9 %collective-permute-start = (bf16[128,128]{1,0:T(8,128)(2,1)S(1)}, bf16[128,128]{1,0:T(8,128)(2,1)S(1)}, u32[]{:S(2)}, u32[]{:S(2)}) collective-permute-start(bf16[128,128]{1,0:T(8,128)(2,1)S(1)} %get-tuple-element.26.refs_0_.refs_3_.u_ref), channel_id=1, source_target_pairs={{2,0},{4,2},{6,4},{0,6},{3,1},{5,3},{7,5},{1,7},{10,8},{12,10},{14... | collective-permute-start | bytes 98312 | tf_op jit(solution)/shard_map/ppermute | solution.py:251
  20.0 1.9 %collective-permute-start.3 = (bf16[16,128,128]{2,1,0:T(8,128)(2,1)S(1)}, bf16[16,128,128]{2,1,0:T(8,128)(2,1)S(1)}, u32[]{:S(2)}, u32[]{:S(2)}) collective-permute-start(bf16[16,128,128]{2,1,0:T(8,128)(2,1)S(1)} %all-to-all-done), channel_id=1, source_target_pairs={{0,1},{1,0},{2,3},{3,2},{4,5},{5,4},{6,7},{7,6},{8,9},{9,8},{10,11... | collective-permute-start | bytes 1572872 | tf_op jit(solution)/shard_map/ppermute | solution.py:264
  42.5 5.7 %collective-permute-start.4 = (bf16[144,128]{1,0:T(8,128)(2,1)S(1)}, bf16[144,128]{1,0:T(8,128)(2,1)S(1)}, u32[]{:S(2)}, u32[]{:S(2)}) collective-permute-start(bf16[144,128]{1,0:T(8,128)(2,1)S(1)} %get-tuple-element.30), channel_id=1, source_target_pairs={{4,0},{6,2},{0,4},{2,6},{5,1},{7,3},{1,5},{3,7},{12,8},{14,10},{8,... | collective-permute-start | bytes 110600 | tf_op jit(solution)/shard_map/ppermute | solution.py:251
  43.6 5.2 %collective-permute-start.5 = (bf16[144,128]{1,0:T(8,128)(2,1)S(1)}, bf16[144,128]{1,0:T(8,128)(2,1)S(1)}, u32[]{:S(2)}, u32[]{:S(2)}) collective-permute-start(bf16[144,128]{1,0:T(8,128)(2,1)S(1)} %get-tuple-element.31), channel_id=1, source_target_pairs={{6,0},{0,2},{2,4},{4,6},{7,1},{1,3},{3,5},{5,7},{14,8},{8,10},{10,... | collective-permute-start | bytes 110600 | tf_op jit(solution)/shard_map/ppermute | solution.py:251
  44.1 4.6 %collective-permute-start.6 = (bf16[144,128]{1,0:T(8,128)(2,1)S(1)}, bf16[144,128]{1,0:T(8,128)(2,1)S(1)}, u32[]{:S(2)}, u32[]{:S(2)}) collective-permute-start(bf16[144,128]{1,0:T(8,128)(2,1)S(1)} %get-tuple-element.32), channel_id=1, source_target_pairs={{2,0},{4,2},{6,4},{0,6},{3,1},{5,3},{7,5},{1,7},{10,8},{12,10},{14... | collective-permute-start | bytes 110600 | tf_op jit(solution)/shard_map/ppermute | solution.py:251
  46.8 1.9 %copy-start.2 = (f32[128,128]{1,0:T(8,128)S(1)}, f32[128,128]{1,0:T(8,128)}, u32[]{:S(2)}) copy-start(f32[128,128]{1,0:T(8,128)} %x_ref.3) | copy-start | bytes 196612
